TPU v7x, 256 devices: a whole 4x4x8 slice. The times are simulated.
256 devices in a mesh: seq: 16 (over z, core), fsdp: 16 (over y, x).
Axes of the slice: x: 4, y: 4, z: 8, core: 2. Of those that a mesh axis runs over, the one named last changes fastest.
Arguments:
- qkv_raw: bfloat16 [16, 2048, 4096], P('fsdp', 'seq'), may hold values from -6 to 6
- output_gate: bfloat16 [16, 2048, 2048], P('fsdp', 'seq'), may hold values from -6 to 6
- decay_codes: int32 [16, 16, 2048], P('fsdp', None, 'seq'), may hold values from 0 to 559
- beta_codes: int32 [16, 16, 2048], P('fsdp', None, 'seq'), may hold values from 32 to 319
- conv_weight: float32 [4, 4096], replicated, may hold values from -3 to 3
- decay_scale_log: float32 [16], replicated
- decay_bias: float32 [16], replicated, may hold values from -0.5 to 0.5
- norm_gain: float32 [128], replicated, may hold values from 0.5 to 1.5
- out_weight: bfloat16 [2048, 2048], P('fsdp'), may hold values from -0.125 to 0.125
Outputs:
- layer_out: bfloat16 [16, 2048, 2048], P('fsdp', 'seq')
All inputs are finite; a program needn't handle non-finite values.
Results may differ from a plain program's by a relative error of at most 0.0049.
Values may be sent and summed in bfloat16 or wider, within the bound.
No kernel may reach another device: no remote copies, remote signals or barrier semaphores. Data moves between devices by JAX's collectives and lax.ppermute only.
A program may use at most 128 MiB of HBM per device.

v0:
```python
import math

import jax
import jax.numpy as jnp
from jax import lax
from jax.experimental import pallas as pl
from jax.experimental.pallas import tpu as pltpu
from jax.sharding import PartitionSpec as P


CHIPS = 8
SEGMENTS = 16
C = 128
DK = 128
DV = 128
VH = 16
WIDTH = 2048
HALF = 1024
CODES = 4 * C
PIECE = CODES + 16
F32 = jnp.float32
BF16 = jnp.bfloat16


def to_chip(block, distance):
    return lax.ppermute(
        block, "seq", [(i, (i + 2 * distance) % SEGMENTS) for i in range(SEGMENTS)]
    )


def other_core(block):
    return lax.ppermute(block, "seq", [(i, i ^ 1) for i in range(SEGMENTS)])


def dot(left, right):
    return jnp.dot(left, right, preferred_element_type=F32)


def dot_t(left, right):
    return lax.dot_general(
        left, right, (((1,), (1,)), ((), ())), preferred_element_type=F32
    )


def split(value):
    high = value.astype(BF16)
    return high, (value - high.astype(F32)).astype(BF16)


def dot3(left, right):
    lh, ll = left
    rh, rl = right
    return dot(jnp.concatenate([lh, ll], 1), jnp.concatenate([rh, rh], 0)) + dot(lh, rl)


def silu(value):
    return value / (1.0 + jnp.exp(-value))


def pieces_kernel(place, raw, decay, beta, *rest):
    outs, rows = rest[:CHIPS], rest[CHIPS]
    z = place[0]
    rows[...] = jnp.zeros_like(rows)
    for distance in range(CHIPS):
        chip = lax.rem(z + distance, CHIPS)
        out = outs[distance]
        at = pl.multiple_of(chip * DK, DK)
        out[0:C] = raw[:, pl.ds(at, DK)]
        out[C : 2 * C] = raw[:, pl.ds(at + CHIPS * DK, DK)]
        at = pl.multiple_of(chip * 2 * DV, 2 * DV)
        out[2 * C : 3 * C] = raw[:, pl.ds(at + 2 * CHIPS * DK, DV)]
        out[3 * C : 4 * C] = raw[:, pl.ds(at + 2 * CHIPS * DK + DV, DV)]
        for first, codes in ((0, decay), (4, beta)):
            pair = codes[pl.ds(2 * chip, 2), :]
            rows[first : first + 2] = (pair >> 4).astype(F32)
            rows[first + 2 : first + 4] = (pair & 15).astype(F32)
        out[CODES:PIECE] = rows[...].astype(BF16)


def cut_pieces(place, raw, decay, beta):
    vmem = pl.BlockSpec(memory_space=pltpu.VMEM)
    return pl.pallas_call(
        pieces_kernel,
        out_shape=[jax.ShapeDtypeStruct((PIECE, DK), BF16)] * CHIPS,
        in_specs=[pl.BlockSpec(memory_space=pltpu.SMEM), vmem, vmem, vmem],
        out_specs=[vmem] * CHIPS,
        scratch_shapes=[pltpu.VMEM((16, C), F32)],
        compiler_params=pltpu.CompilerParams(vmem_limit_bytes=24 * 2**20),
        name="pieces",
    )(place, raw, decay, beta)


def head_kernel(
    place, scale_log, bias, mine, theirs, taps, gain, out, raw, decay, beta, local_out, reads, transit, adds
):
    z, core = place[0], place[1]
    head = 2 * z + core

    raw[:, 0:8] = jnp.zeros((3, 8, DK), F32)
    for distance in range(CHIPS):
        chip = lax.rem(z - distance + CHIPS, CHIPS)
        for source, its_core in ((mine, core), (theirs, 1 - core)):
            segment = 2 * chip + its_core
            to = pl.ds(pl.multiple_of(8 + segment * C, 8), C)
            raw[0, to] = source[distance, 0:C].astype(F32)
            raw[1, to] = source[distance, C : 2 * C].astype(F32)
            values = pl.ds(pl.multiple_of(2 * C + core * C, C), C)
            raw[2, to] = source[distance, values].astype(F32)
            rows = source[distance, CODES:PIECE].astype(F32)
            for first, codes in ((0, decay), (4, beta)):
                high = jnp.where(core == 0, rows[first : first + 1], rows[first + 1 : first + 2])
                low = jnp.where(core == 0, rows[first + 2 : first + 3], rows[first + 3 : first + 4])
                codes[pl.ds(segment, 1), :] = 16.0 * high + low

    level = decay[...] / 32.0 - 16.0 + bias[head]
    small = jnp.exp(-jnp.abs(level))
    one_more = 1.0 + small
    gap = one_more - 1.0
    log1p = jnp.where(gap == 0.0, small, jnp.log(one_more) * (small / jnp.where(gap == 0.0, 1.0, gap)))
    softplus = jnp.maximum(level, 0.0) + log1p
    log_decay = -jnp.exp(jnp.full((SEGMENTS, C), scale_log[head], F32)) * softplus
    row_ids = lax.broadcasted_iota(jnp.int32, (C, C), 0)
    col_ids = lax.broadcasted_iota(jnp.int32, (C, C), 1)
    sums = jnp.dot(
        log_decay,
        (row_ids <= col_ids).astype(F32),
        precision=lax.Precision.HIGHEST,
        preferred_element_type=F32,
    )
    strength = 1.0 / (1.0 + jnp.exp(8.0 - beta[...] / 32.0))
    start = jnp.exp(sums)
    end = jnp.exp(sums[:, C - 1 : C] - sums)
    columns = jnp.concatenate(
        [sums, strength, start, end, strength * start, jnp.zeros((C - 5 * SEGMENTS, C), F32)], 0
    ).T

    inclusive = row_ids >= col_ids
    strict = row_ids > col_ids

    def convolved(which, first, j):
        weights = taps[:, pl.ds(pl.multiple_of(first, DK), DK)]
        base = 8 + j * C - 3
        total = weights[0:1] * raw[which, base : base + C]
        for t in range(1, 4):
            total = total + weights[t : t + 1] * raw[which, base + t : base + t + C]
        return silu(total)

    for j in range(SEGMENTS):

        def column(kind):
            at = kind * SEGMENTS + j
            return columns[:, at : at + 1]

        queries = convolved(0, z * DK, j)
        keys = convolved(1, CHIPS * DK + z * DK, j)
        values = convolved(2, 2 * CHIPS * DK + head * DV, j)
        queries = queries * (
            lax.rsqrt(jnp.sum(queries * queries, -1, keepdims=True) + 1e-06) * (1.0 / math.sqrt(DK))
        )
        keys = keys * lax.rsqrt(jnp.sum(keys * keys, -1, keepdims=True) + 1e-06)
        qh, ql = split(queries)
        kh, kl = split(keys)
        pair = jnp.where(inclusive, jnp.exp(jnp.minimum(column(0) - sums[j : j + 1], 0.0)), 0.0)
        lower = jnp.where(strict, column(1) * pair * dot_t(kh, kh), 0.0)
        beyond = jnp.where((row_ids // 2 == col_ids // 2), -lower, 0.0)
        for b in (2, 4, 8, 16, 32, 64):
            part = jnp.where((row_ids // (2 * b) == col_ids // (2 * b)) & (row_ids // b != col_ids // b), lower, 0.0)
            near = beyond.astype(BF16)
            half = part + dot(part.astype(BF16), near)
            beyond = beyond - (half + dot(near, half.astype(BF16)))
        right = jnp.concatenate([column(1) * values, column(4) * keys], 1)
        solved = right + dot(beyond.astype(BF16), right.astype(BF16))
        gram = pair * (dot_t(jnp.concatenate([qh, ql], 1), jnp.concatenate([kh, kh], 1)) + dot_t(qh, kl))
        gh, gl = split(gram)
        new_values, write_keys = solved[:, :DV], solved[:, DV:]
        local_out[j] = dot3((gh, gl), split(new_values))
        read_high, read_low = split(column(2) * queries - dot(gh, write_keys.astype(BF16)))
        reads[j, :, :DK] = read_high
        reads[j, :, DK:] = read_low
        kh_t, kl_t = split(keys.T)
        transit[j] = dot(kh_t, (column(3) * write_keys).astype(BF16)).astype(BF16)
        adds[j] = dot3((kh_t, kl_t), split(column(3) * new_values))

    state = jnp.zeros((DK, DV), F32)
    for j in range(SEGMENTS):
        high, low = split(state)
        read = reads[j]
        rows = local_out[j] + dot(read, jnp.concatenate([high, high], 0)) + dot(read[:, :DK], low)
        square_mean = jnp.mean(rows * rows, -1, keepdims=True)
        out[j] = (rows * lax.rsqrt(square_mean + 1e-06) * gain[...]).astype(BF16)
        if j < SEGMENTS - 1:
            state = start[j : j + 1, C - 1 : C] * state - dot(transit[j], high) + adds[j]


def run_head(place, scale_log, bias, mine, theirs, taps, gain):
    vmem = pl.BlockSpec(memory_space=pltpu.VMEM)
    smem = pl.BlockSpec(memory_space=pltpu.SMEM)
    return pl.pallas_call(
        head_kernel,
        out_shape=jax.ShapeDtypeStruct((SEGMENTS, C, DV), BF16),
        in_specs=[smem, smem, smem, vmem, vmem, vmem, vmem],
        out_specs=vmem,
        scratch_shapes=[
            pltpu.VMEM((3, 8 + SEGMENTS * C, DK), F32),
            pltpu.VMEM((SEGMENTS, C), F32),
            pltpu.VMEM((SEGMENTS, C), F32),
            pltpu.VMEM((SEGMENTS, C, DV), F32),
            pltpu.VMEM((SEGMENTS, C, 2 * DK), BF16),
            pltpu.VMEM((SEGMENTS, DK, DK), BF16),
            pltpu.VMEM((SEGMENTS, DK, DV), F32),
        ],
        compiler_params=pltpu.CompilerParams(vmem_limit_bytes=40 * 2**20),
        name="head",
    )(place, scale_log, bias, mine, theirs, taps, gain)


def first_half_kernel(heads, gate, weight, normed, out):
    for h in range(VH):
        at = slice(h * DV, (h + 1) * DV)
        normed[:, at] = (heads[h].astype(F32) * silu(gate[:, at].astype(F32))).astype(BF16)
    out[...] = dot(normed[...], weight[...]).astype(BF16)


def second_half_kernel(place, normed, weight, first, out):
    core = place[1]
    out[:, pl.ds(pl.multiple_of(core * HALF, HALF), HALF)] = first[...]
    out[:, pl.ds(pl.multiple_of((1 - core) * HALF, HALF), HALF)] = dot(
        normed[...], weight[...]
    ).astype(BF16)


def project(place, heads, gate, weight, other_weight):
    vmem = pl.BlockSpec(memory_space=pltpu.VMEM)
    params = pltpu.CompilerParams(vmem_limit_bytes=32 * 2**20)
    normed, first = pl.pallas_call(
        first_half_kernel,
        out_shape=[jax.ShapeDtypeStruct((C, WIDTH), BF16), jax.ShapeDtypeStruct((C, HALF), BF16)],
        in_specs=[vmem] * 3,
        out_specs=[vmem] * 2,
        compiler_params=params,
        cost_estimate=pl.CostEstimate(flops=2 * C * WIDTH * HALF, bytes_accessed=2**23, transcendentals=0),
        name="project_first",
    )(heads, gate, weight)
    return pl.pallas_call(
        second_half_kernel,
        out_shape=jax.ShapeDtypeStruct((C, WIDTH), BF16),
        in_specs=[pl.BlockSpec(memory_space=pltpu.SMEM)] + [vmem] * 3,
        out_specs=vmem,
        compiler_params=params,
        cost_estimate=pl.CostEstimate(flops=2 * C * WIDTH * HALF, bytes_accessed=2**23, transcendentals=0),
        name="project_second",
    )(place, normed, other_weight, first)


def local(
    qkv_raw,
    output_gate,
    decay_codes,
    beta_codes,
    conv_weight,
    decay_scale_log,
    decay_bias,
    norm_gain,
    out_weight,
):
    index = lax.axis_index("seq")
    core = index % 2
    place = jnp.stack([index // 2, core]).astype(jnp.int32)
    columns = lax.dynamic_slice(out_weight, (0, core * HALF), (out_weight.shape[0], HALF))
    weight = lax.all_gather(columns, "fsdp", axis=0, tiled=True)

    pieces = cut_pieces(place, qkv_raw[0], decay_codes[0], beta_codes[0])
    arrived = {0: pieces[0]}
    for distance in (1, 7, 2, 6, 3, 5, 4):
        arrived[distance] = to_chip(pieces[distance], distance)
    mine = jnp.stack([arrived[distance] for distance in range(CHIPS)])
    theirs = other_core(mine)
    rows = run_head(place, decay_scale_log, decay_bias, mine, theirs, conv_weight, norm_gain[None])
    heads = lax.all_to_all(rows, "seq", 0, 0)
    heads, weight = lax.optimization_barrier((heads, weight))
    return project(place, heads, output_gate[0], weight, other_core(weight))[None]


def solution(mesh):
    return jax.shard_map(
        local,
        mesh=mesh,
        in_specs=(
            P("fsdp", "seq", None),
            P("fsdp", "seq", None),
            P("fsdp", None, "seq"),
            P("fsdp", None, "seq"),
            P(),
            P(),
            P(),
            P(),
            P("fsdp", None),
        ),
        out_specs=P("fsdp", "seq", None),
        check_vma=False,
    )
```

profile of v0, /device:TPU:1, one launch (start us, length us, event | category | flops | bytes accessed | tf_op | source)
XLA Modules:
  0.0 126.4 jit_solution(17503829699599737325)
XLA Ops:
  6.5 0.0 copy-start
  6.5 0.0 all-gather.2.cloned.1.call-start
  6.5 1.0 copy-done
  7.6 0.7 constant_dynamic-slice_fusion
  8.3 0.0 all-gather.2.cloned.1.call-update
  8.3 0.1 pad_add_fusion.place
  8.4 0.0 copy-start.2
  8.4 1.2 copy-done.2
  9.6 0.0 copy-start.5
  9.6 0.7 copy-done.5
  10.3 0.0 copy-start.6
  10.3 0.7 copy-done.6
  11.0 0.8 pieces.1
  11.9 2.5 %collective-permute-start = (bf16[528,128]{1,0:T(8,128)(2,1)S(1)}, bf16[528,128]{1,0:T(8,128)(2,1)S(1)}, u32[]{:S(2)}, u32[]{:S(2)}) collective-permute-start(bf16[528,128]{1,0:T(8,128)(2,1)S(1)} %get-tuple-element.18), channel_id=1, source_target_pairs={{0,32},{16,48},{32,64},{48,80},{64,96},{80,112},{96,128},{112,144}... | collective-permute-start | bytes 405512 | tf_op jit(solution)/shard_map/ppermute | solution.py:26
  14.4 3.0 %collective-permute-start.1 = (bf16[528,128]{1,0:T(8,128)(2,1)S(1)}, bf16[528,128]{1,0:T(8,128)(2,1)S(1)}, u32[]{:S(2)}, u32[]{:S(2)}) collective-permute-start(bf16[528,128]{1,0:T(8,128)(2,1)S(1)} %get-tuple-element.19), channel_id=1, source_target_pairs={{0,64},{16,80},{32,96},{48,112},{64,128},{80,144},{96,160},{112,17... | collective-permute-start | bytes 405512 | tf_op jit(solution)/shard_map/ppermute | solution.py:26
  17.4 3.8 %collective-permute-start.2 = (bf16[528,128]{1,0:T(8,128)(2,1)S(1)}, bf16[528,128]{1,0:T(8,128)(2,1)S(1)}, u32[]{:S(2)}, u32[]{:S(2)}) collective-permute-start(bf16[528,128]{1,0:T(8,128)(2,1)S(1)} %get-tuple-element.20), channel_id=1, source_target_pairs={{0,96},{16,112},{32,128},{48,144},{64,160},{80,176},{96,192},{112,... | collective-permute-start | bytes 405512 | tf_op jit(solution)/shard_map/ppermute | solution.py:26
  21.2 0.5 collective-permute-start.3
  21.6 4.5 %collective-permute-start.4 = (bf16[528,128]{1,0:T(8,128)(2,1)S(1)}, bf16[528,128]{1,0:T(8,128)(2,1)S(1)}, u32[]{:S(2)}, u32[]{:S(2)}) collective-permute-start(bf16[528,128]{1,0:T(8,128)(2,1)S(1)} %get-tuple-element.22), channel_id=1, source_target_pairs={{0,160},{16,176},{32,192},{48,208},{64,224},{80,240},{96,0},{112,1... | collective-permute-start | bytes 405512 | tf_op jit(solution)/shard_map/ppermute | solution.py:26
  26.1 0.0 copy-start.4
  26.1 0.0 copy-start.7
  26.1 0.0 copy-start.8
  26.1 0.0 copy-start.9
  26.1 0.0 collective-permute-done
  26.1 2.5 %collective-permute-start.5 = (bf16[528,128]{1,0:T(8,128)(2,1)S(1)}, bf16[528,128]{1,0:T(8,128)(2,1)S(1)}, u32[]{:S(2)}, u32[]{:S(2)}) collective-permute-start(bf16[528,128]{1,0:T(8,128)(2,1)S(1)} %get-tuple-element.23), channel_id=1, source_target_pairs={{0,192},{16,208},{32,224},{48,240},{64,0},{80,16},{96,32},{112,48}... | collective-permute-start | bytes 405512 | tf_op jit(solution)/shard_map/ppermute | solution.py:26
  28.6 0.0 collective-permute-done.1
  28.6 0.8 collective-permute-start.6
  29.5 7.9 %collective-permute-done.2 = bf16[528,128]{1,0:T(8,128)(2,1)S(1)} collective-permute-done((bf16[528,128]{1,0:T(8,128)(2,1)S(1)}, bf16[528,128]{1,0:T(8,128)(2,1)S(1)}, u32[]{:S(2)}, u32[]{:S(2)}) %collective-permute-start.2) | collective-permute-done | bytes 135200 | tf_op jit(solution)/shard_map/ppermute | solution.py:26
  37.4 1.3 %collective-permute-done.3 = bf16[528,128]{1,0:T(8,128)(2,1)S(1)} collective-permute-done((bf16[528,128]{1,0:T(8,128)(2,1)S(1)}, bf16[528,128]{1,0:T(8,128)(2,1)S(1)}, u32[]{:S(2)}, u32[]{:S(2)}) %collective-permute-start.3) | collective-permute-done | bytes 135200 | tf_op jit(solution)/shard_map/ppermute | solution.py:26
  38.7 0.0 collective-permute-done.4
  38.8 7.8 %collective-permute-done.5 = bf16[528,128]{1,0:T(8,128)(2,1)S(1)} collective-permute-done((bf16[528,128]{1,0:T(8,128)(2,1)S(1)}, bf16[528,128]{1,0:T(8,128)(2,1)S(1)}, u32[]{:S(2)}, u32[]{:S(2)}) %collective-permute-start.5) | collective-permute-done | bytes 135200 | tf_op jit(solution)/shard_map/ppermute | solution.py:26
  46.6 1.1 collective-permute-done.6
  47.7 1.0 collective-permute-start.7
  48.7 2.3 %collective-permute-done.7.theirs = bf16[8,528,128]{2,1,0:T(8,128)(2,1)S(1)} collective-permute-done((bf16[8,528,128]{2,1,0:T(8,128)(2,1)S(1)}, bf16[8,528,128]{2,1,0:T(8,128)(2,1)S(1)}, u32[]{:S(2)}, u32[]{:S(2)}) %collective-permute-start.7) | collective-permute-done | bytes 1081376 | tf_op jit(solution)/shard_map/ppermute | solution.py:32
  51.0 0.0 copy-done.4
  51.0 0.0 copy-done.7
  51.0 0.0 copy-done.8
  51.0 0.0 copy-done.9
  51.0 36.4 %head.1 = bf16[16,128,128]{2,1,0:T(8,128)(2,1)S(1)} custom-call(s32[2]{0:T(128)S(1)} %pad_add_fusion.place, f32[16]{0:T(128)S(1)} %copy-done.7, f32[16]{0:T(128)S(1)} %copy-done.8, bf16[8,528,128]{2,1,0:T(8,128)(2,1)S(1)} %bitcast_dynamic-update-slice_fusion.mine, bf16[8,528,128]{2,1,0:T(8,128)(2,1)S(1)} %collective-permute-done.7.theirs, ...), custom_call_target="tpu_custom_call" | custom-call | tf_op jit(solution)/shard_map/head/pallas_call | solution.py:198
  87.4 0.0 copy-start.3
  87.4 22.7 %all_to_all.5.heads = bf16[16,128,128]{2,1,0:T(8,128)(2,1)S(1)} all-to-all(bf16[16,128,128]{2,1,0:T(8,128)(2,1)S(1)} %head.1), channel_id=1, replica_groups=mesh['seq'=16,'fsdp'=16] {'seq'}, dimensions={0} | all-to-all | bytes 1048576 | tf_op jit(solution)/shard_map/all_to_all | solution.py:279
  110.1 0.0 all-gather.2.cloned.1.call-done.weight
  110.1 0.0 collective-permute-start.8
  110.1 0.0 copy-done.3
  110.1 0.0 copy-start.1
  110.1 2.2 %copy-done.1 = bf16[2048,1024]{1,0:T(8,128)(2,1)S(1)} copy-done((bf16[2048,1024]{1,0:T(8,128)(2,1)S(1)}, bf16[2048,1024]{1,0:T(8,128)(2,1)}, u32[]{:S(2)}) %copy-start.1) | copy-done | bytes 4194328
  112.3 1.0 project_first.1
  113.4 4.1 %collective-permute-done.8.weight = bf16[2048,1024]{1,0:T(8,128)(2,1)S(1)} collective-permute-done((bf16[2048,1024]{1,0:T(8,128)(2,1)}, bf16[2048,1024]{1,0:T(8,128)(2,1)S(1)}, u32[]{:S(2)}, u32[]{:S(2)}) %collective-permute-start.8) | collective-permute-done | bytes 4194336 | tf_op jit(solution)/shard_map/ppermute | solution.py:32
  117.5 2.1 %project_second.1 = bf16[128,2048]{1,0:T(8,128)(2,1)} custom-call(s32[2]{0:T(128)S(1)} %pad_add_fusion.place, bf16[128,2048]{1,0:T(8,128)(2,1)S(1)} %get-tuple-element.27.normed, bf16[2048,1024]{1,0:T(8,128)(2,1)S(1)} %collective-permute-done.8.weight, bf16[128,1024]{1,0:T(8,128)(2,1)S(1)} %get-tuple-element.28.first), custom_call_target="tpu_custom_call" | custom-call | flops 536870912 | bytes 8388608 | tf_op jit(solution)/shard_map/project_second/pallas_call | solution.py:244
  (8 shorter events, 0.1 us)
Async XLA Ops:
  6.5 1.0 copy-start
  6.5 103.6 %all-gather.2.cloned.1.call-start = ((), (), s32[]{:S(2)}) async-start(), calls=%async_computation.1 | async-start | bytes 4456448 | tf_op jit(solution)/shard_map/all_gather | solution.py:270
  8.4 1.2 copy-start.2
  9.6 0.7 copy-start.5
  10.3 0.7 copy-start.6
  11.9 14.3 %collective-permute-start = (bf16[528,128]{1,0:T(8,128)(2,1)S(1)}, bf16[528,128]{1,0:T(8,128)(2,1)S(1)}, u32[]{:S(2)}, u32[]{:S(2)}) collective-permute-start(bf16[528,128]{1,0:T(8,128)(2,1)S(1)} %get-tuple-element.18), channel_id=1, source_target_pairs={{0,32},{16,48},{32,64},{48,80},{64,96},{80,112},{96,128},{112,144}... | collective-permute-start | bytes 405512 | tf_op jit(solution)/shard_map/ppermute | solution.py:26
  14.4 14.2 %collective-permute-start.1 = (bf16[528,128]{1,0:T(8,128)(2,1)S(1)}, bf16[528,128]{1,0:T(8,128)(2,1)S(1)}, u32[]{:S(2)}, u32[]{:S(2)}) collective-permute-start(bf16[528,128]{1,0:T(8,128)(2,1)S(1)} %get-tuple-element.19), channel_id=1, source_target_pairs={{0,64},{16,80},{32,96},{48,112},{64,128},{80,144},{96,160},{112,17... | collective-permute-start | bytes 405512 | tf_op jit(solution)/shard_map/ppermute | solution.py:26
  17.4 20.0 %collective-permute-start.2 = (bf16[528,128]{1,0:T(8,128)(2,1)S(1)}, bf16[528,128]{1,0:T(8,128)(2,1)S(1)}, u32[]{:S(2)}, u32[]{:S(2)}) collective-permute-start(bf16[528,128]{1,0:T(8,128)(2,1)S(1)} %get-tuple-element.20), channel_id=1, source_target_pairs={{0,96},{16,112},{32,128},{48,144},{64,160},{80,176},{96,192},{112,... | collective-permute-start | bytes 405512 | tf_op jit(solution)/shard_map/ppermute | solution.py:26
  21.2 17.5 %collective-permute-start.3 = (bf16[528,128]{1,0:T(8,128)(2,1)S(1)}, bf16[528,128]{1,0:T(8,128)(2,1)S(1)}, u32[]{:S(2)}, u32[]{:S(2)}) collective-permute-start(bf16[528,128]{1,0:T(8,128)(2,1)S(1)} %get-tuple-element.21), channel_id=1, source_target_pairs={{0,128},{16,144},{32,160},{48,176},{64,192},{80,208},{96,224},{112... | collective-permute-start | bytes 405512 | tf_op jit(solution)/shard_map/ppermute | solution.py:26
  21.6 17.1 %collective-permute-start.4 = (bf16[528,128]{1,0:T(8,128)(2,1)S(1)}, bf16[528,128]{1,0:T(8,128)(2,1)S(1)}, u32[]{:S(2)}, u32[]{:S(2)}) collective-permute-start(bf16[528,128]{1,0:T(8,128)(2,1)S(1)} %get-tuple-element.22), channel_id=1, source_target_pairs={{0,160},{16,176},{32,192},{48,208},{64,224},{80,240},{96,0},{112,1... | collective-permute-start | bytes 405512 | tf_op jit(solution)/shard_map/ppermute | solution.py:26
  26.1 24.9 %copy-start.4 = (f32[4,4096]{1,0:T(4,128)S(1)}, f32[4,4096]{1,0:T(4,128)}, u32[]{:S(2)}) copy-start(f32[4,4096]{1,0:T(4,128)} %taps.1) | copy-start | bytes 196612
  26.1 24.9 %copy-start.7 = (f32[16]{0:T(128)S(1)}, f32[16]{0:T(128)}, u32[]{:S(2)}) copy-start(f32[16]{0:T(128)} %scale_log.1) | copy-start | bytes 196
  26.1 24.9 %copy-start.8 = (f32[16]{0:T(128)S(1)}, f32[16]{0:T(128)}, u32[]{:S(2)}) copy-start(f32[16]{0:T(128)} %bias.1) | copy-start | bytes 196
  26.1 24.9 %copy-start.9 = (f32[128]{0:T(128)S(1)}, f32[128]{0:T(128)}, u32[]{:S(2)}) copy-start(f32[128]{0:T(128)} %param.16) | copy-start | bytes 1540
  26.1 20.4 %collective-permute-start.5 = (bf16[528,128]{1,0:T(8,128)(2,1)S(1)}, bf16[528,128]{1,0:T(8,128)(2,1)S(1)}, u32[]{:S(2)}, u32[]{:S(2)}) collective-permute-start(bf16[528,128]{1,0:T(8,128)(2,1)S(1)} %get-tuple-element.23), channel_id=1, source_target_pairs={{0,192},{16,208},{32,224},{48,240},{64,0},{80,16},{96,32},{112,48}... | collective-permute-start | bytes 405512 | tf_op jit(solution)/shard_map/ppermute | solution.py:26
  28.6 19.1 %collective-permute-start.6 = (bf16[528,128]{1,0:T(8,128)(2,1)S(1)}, bf16[528,128]{1,0:T(8,128)(2,1)S(1)}, u32[]{:S(2)}, u32[]{:S(2)}) collective-permute-start(bf16[528,128]{1,0:T(8,128)(2,1)S(1)} %get-tuple-element.24), channel_id=1, source_target_pairs={{0,224},{16,240},{32,0},{48,16},{64,32},{80,48},{96,64},{112,80},{... | collective-permute-start | bytes 405512 | tf_op jit(solution)/shard_map/ppermute | solution.py:26
  47.7 3.3 %collective-permute-start.7 = (bf16[8,528,128]{2,1,0:T(8,128)(2,1)S(1)}, bf16[8,528,128]{2,1,0:T(8,128)(2,1)S(1)}, u32[]{:S(2)}, u32[]{:S(2)}) collective-permute-start(bf16[8,528,128]{2,1,0:T(8,128)(2,1)S(1)} %bitcast_dynamic-update-slice_fusion.mine), channel_id=1, source_target_pairs={{0,16},{16,0},{32,48},{48,32},{64,80},{80,64},{96,112},{112,96},{1... | collective-permute-start | bytes 3244040 | tf_op jit(solution)/shard_map/ppermute | solution.py:32
  87.4 22.7 %copy-start.3 = (bf16[1,128,2048]{2,1,0:T(8,128)(2,1)S(1)}, bf16[1,128,2048]{2,1,0:T(8,128)(2,1)}, u32[]{:S(2)}) copy-start(bf16[1,128,2048]{2,1,0:T(8,128)(2,1)} %param.10) | copy-start | bytes 1572868
  110.1 7.4 %collective-permute-start.8 = (bf16[2048,1024]{1,0:T(8,128)(2,1)}, bf16[2048,1024]{1,0:T(8,128)(2,1)S(1)}, u32[]{:S(2)}, u32[]{:S(2)}) collective-permute-start(bf16[2048,1024]{1,0:T(8,128)(2,1)} %all-gather.2.cloned.1.call-done.weight), channel_id=1, source_target_pairs={{0,16},{16,0},{32,48},{48,32},{64,80},{80,64},{96,112},{112,96},{1... | collective-permute-start | bytes 12582920 | tf_op jit(solution)/shard_map/ppermute | solution.py:32
  110.1 2.2 %copy-start.1 = (bf16[2048,1024]{1,0:T(8,128)(2,1)S(1)}, bf16[2048,1024]{1,0:T(8,128)(2,1)}, u32[]{:S(2)}) copy-start(bf16[2048,1024]{1,0:T(8,128)(2,1)} %all-gather.2.cloned.1.call-done.weight) | copy-start | bytes 12582916
Sparse Core Ops, SparseCore 0:
  9.8 60.3 all-gather.1
where the time goes:
time: 127 us; the launch traced here: 126 us
  Pallas kernels  40.3 us (32%)
  waiting for transfers between devices  24.6 us (19%)
  blocking collectives  22.7 us (18%)
  starting transfers between devices  18.5 us (15%)
  between operations  13.5 us (11%)
  local copies, waits for them, and re-layouts  6.72 us (5%)
    pallas_call x1, Pallas kernels, run_head(): pl.pallas_call(head_kernel, out_shape=jax.ShapeDtypeStruct((SEGMENTS, C,...  36.4 us
    all_to_all x1, blocking collectives, local(): heads = lax.all_to_all(rows, 'seq', 0, 0)  22.7 us
    ppermute x7, waiting for transfers between devices, to_chip(): lax.ppermute(block, 'seq', [(i, (i + 2 * distance) % SEGMENTS) for i in r...  18.2 us
    ppermute x7, starting transfers between devices, to_chip(): lax.ppermute(block, 'seq', [(i, (i + 2 * distance) % SEGMENTS) for i in r...  17.5 us
    ppermute x2, waiting for transfers between devices, other_core(): return lax.ppermute(block, 'seq', [(i, i ^ 1) for i in range(SEGMENTS)])  6.45 us
    unnamed x27, local copies, waits for them, and re-layouts  5.98 us
  transfers between devices with their start and end apart: 10, of which 6 were waited for; matrix products, arithmetic and copies ran while one was open for 0% of the time, Pallas kernels for 30%

commit v1 on v0

v1 whole, which is shorter than its diff:
```python
import functools
import math

import jax
import jax.numpy as jnp
from jax import lax
from jax.experimental import pallas as pl
from jax.experimental.pallas import tpu as pltpu
from jax.sharding import PartitionSpec as P


CHIPS = 8
SEGMENTS = 16
C = 128
DK = 128
DV = 128
VH = 16
GROUP = 8
WIDTH = 2048
HALF = 1024
SIDE = 4
CODES = 4 * C
PIECE = CODES + 16
F32 = jnp.float32
BF16 = jnp.bfloat16


def to_chip(block, distance):
    return lax.ppermute(
        block, "seq", [(i, (i + 2 * distance) % SEGMENTS) for i in range(SEGMENTS)]
    )


def other_core(block):
    return lax.ppermute(block, "seq", [(i, i ^ 1) for i in range(SEGMENTS)])


def dot(left, right):
    return jnp.dot(left, right, preferred_element_type=F32)


def dot_t(left, right):
    return lax.dot_general(
        left, right, (((1,), (1,)), ((), ())), preferred_element_type=F32
    )


def split(value):
    high = value.astype(BF16)
    return high, (value - high.astype(F32)).astype(BF16)


def dot3(left, right):
    lh, ll = left
    rh, rl = right
    return dot(jnp.concatenate([lh, ll], 1), jnp.concatenate([rh, rh], 0)) + dot(lh, rl)


def silu(value):
    return value / (1.0 + jnp.exp(-value))


def pieces_kernel(place, raw, decay, beta, weight, *rest):
    outs, half, rows, decays, betas, sems = rest[:CHIPS], *rest[CHIPS:]
    z, core = place[0], place[1]
    copies = []

    def copy(source, target):
        copies.append(pltpu.make_async_copy(source, target, sems.at[len(copies)]))
        copies[-1].start()

    copy(decay, decays)
    copy(beta, betas)
    for distance in range(CHIPS):
        chip = lax.rem(z + distance, CHIPS)
        at = pl.multiple_of(chip * DK, DK)
        to = pl.multiple_of(chip * 2 * DV + 2 * CHIPS * DK, 2 * DV)
        for i, column in enumerate((at, at + CHIPS * DK, to, to + DV)):
            copy(raw.at[:, pl.ds(pl.multiple_of(column, DK), DK)], outs[distance].at[i * C : (i + 1) * C])
    copy(weight.at[:, pl.ds(pl.multiple_of(core * HALF, HALF), HALF)], half)
    copies[0].wait()
    copies[1].wait()
    rows[...] = jnp.zeros_like(rows)
    for distance in range(CHIPS):
        chip = lax.rem(z + distance, CHIPS)
        for first, codes in ((0, decays), (4, betas)):
            pair = codes[pl.ds(2 * chip, 2), :]
            rows[distance, first : first + 2] = (pair >> 4).astype(F32)
            rows[distance, first + 2 : first + 4] = (pair & 15).astype(F32)
        outs[distance][CODES:PIECE] = rows[distance].astype(BF16)
    for one in copies[2:]:
        one.wait()


def cut_pieces(place, raw, decay, beta, weight):
    vmem = pl.BlockSpec(memory_space=pltpu.VMEM)
    hbm = pl.BlockSpec(memory_space=pl.ANY)
    *pieces, half = pl.pallas_call(
        pieces_kernel,
        out_shape=[jax.ShapeDtypeStruct((PIECE, DK), BF16)] * CHIPS
        + [jax.ShapeDtypeStruct((weight.shape[0], HALF), BF16)],
        in_specs=[pl.BlockSpec(memory_space=pltpu.SMEM)] + [hbm] * 4,
        out_specs=[vmem] * (CHIPS + 1),
        scratch_shapes=[
            pltpu.VMEM((CHIPS, 16, C), F32),
            pltpu.VMEM((VH, C), jnp.int32),
            pltpu.VMEM((VH, C), jnp.int32),
            pltpu.SemaphoreType.DMA((3 + 4 * CHIPS,)),
        ],
        compiler_params=pltpu.CompilerParams(vmem_limit_bytes=60 * 2**20),
        name="pieces",
    )(place, raw, decay, beta, weight)
    return pieces, half


def head_kernel(
    place, scale_log, bias, mine, theirs, taps, gain, out, raw, decay, beta, local_out, reads, transit, adds,
    joins, grams, started, keys_t, rights,
):
    z, core = place[0], place[1]
    head = 2 * z + core

    raw[:, 0:8] = jnp.zeros((3, 8, DK), F32)
    for distance in range(CHIPS):
        chip = lax.rem(z - distance + CHIPS, CHIPS)
        for source, its_core in ((mine, core), (theirs, 1 - core)):
            segment = 2 * chip + its_core
            to = pl.ds(pl.multiple_of(8 + segment * C, 8), C)
            raw[0, to] = source[distance, 0:C].astype(F32)
            raw[1, to] = source[distance, C : 2 * C].astype(F32)
            values = pl.ds(pl.multiple_of(2 * C + core * C, C), C)
            raw[2, to] = source[distance, values].astype(F32)
            rows = source[distance, CODES:PIECE].astype(F32)
            for first, codes in ((0, decay), (4, beta)):
                high = jnp.where(core == 0, rows[first : first + 1], rows[first + 1 : first + 2])
                low = jnp.where(core == 0, rows[first + 2 : first + 3], rows[first + 3 : first + 4])
                codes[pl.ds(segment, 1), :] = 16.0 * high + low

    level = decay[...] / 32.0 - 16.0 + bias[head]
    small = jnp.exp(-jnp.abs(level))
    one_more = 1.0 + small
    gap = one_more - 1.0
    log1p = jnp.where(gap == 0.0, small, jnp.log(one_more) * (small / jnp.where(gap == 0.0, 1.0, gap)))
    softplus = jnp.maximum(level, 0.0) + log1p
    log_decay = -jnp.exp(jnp.full((SEGMENTS, C), scale_log[head], F32)) * softplus
    row_ids = lax.broadcasted_iota(jnp.int32, (C, C), 0)
    col_ids = lax.broadcasted_iota(jnp.int32, (C, C), 1)
    sums = jnp.dot(
        log_decay,
        (row_ids <= col_ids).astype(F32),
        precision=lax.Precision.HIGHEST,
        preferred_element_type=F32,
    )
    strength = 1.0 / (1.0 + jnp.exp(8.0 - beta[...] / 32.0))
    start = jnp.exp(sums)
    end = jnp.exp(sums[:, C - 1 : C] - sums)
    columns = jnp.concatenate(
        [sums, strength, start, end, strength * start, jnp.zeros((C - 5 * SEGMENTS, C), F32)], 0
    ).T

    inclusive = row_ids >= col_ids
    strict = row_ids > col_ids
    unit = (row_ids == col_ids).astype(BF16)

    def convolved(which, first, j):
        weights = taps[:, pl.ds(pl.multiple_of(first, DK), DK)]
        base = 8 + j * C - 3
        total = weights[0:1] * raw[which, base : base + C]
        for t in range(1, 4):
            total = total + weights[t : t + 1] * raw[which, base + t : base + t + C]
        return silu(total)

    def column(kind, j):
        at = kind * SEGMENTS + j
        return columns[:, at : at + 1]

    for level in range(1, 7):
        joins[level - 1] = (
            ((row_ids >> (level + 1)) == (col_ids >> (level + 1))) & ((row_ids >> level) != (col_ids >> level))
        ).astype(F32).astype(BF16)
    near = (row_ids >> 1) == (col_ids >> 1)

    states = [jnp.zeros((DK, DV), F32)]

    def chain(j):
        state = states[-1]
        high, low = split(state)
        if j < SEGMENTS - 1:
            states.append(start[j : j + 1, C - 1 : C] * state - dot(transit[j], high) + adds[j])
        read = reads[j]
        rows = local_out[j] + dot(read, jnp.concatenate([high, high], 0)) + dot(read[:, :DK], low)
        square_mean = jnp.mean(rows * rows, -1, keepdims=True)
        out[j] = (rows * lax.rsqrt(square_mean + 1e-06) * gain[...]).astype(BF16)

    waiting = []
    for group in range(0, SEGMENTS, GROUP):
        blocks = range(group, group + GROUP)
        kinv, right, qk, pairs = [], [], [], []
        lowers = []
        for i, j in enumerate(blocks):
            keys = convolved(1, CHIPS * DK + z * DK, j)
            keys = keys * lax.rsqrt(jnp.sum(keys * keys, -1, keepdims=True) + 1e-06)
            kh, kl = split(keys)
            pair = jnp.where(inclusive, jnp.exp(jnp.minimum(column(0, j) - sums[j : j + 1], 0.0)), 0.0)
            lower = jnp.where(strict, column(1, j) * pair * dot_t(kh, kh), 0.0)
            inverse = unit - jnp.where(near, lower, 0.0).astype(BF16)
            lowers.append(lower.astype(BF16))
            kinv.append(inverse)
            queries = convolved(0, z * DK, j)
            queries = queries * (
                lax.rsqrt(jnp.sum(queries * queries, -1, keepdims=True) + 1e-06) * (1.0 / math.sqrt(DK))
            )
            qh, ql = split(queries)
            gram = pair * (dot_t(jnp.concatenate([qh, ql], 1), jnp.concatenate([kh, kh], 1)) + dot_t(qh, kl))
            gh, gl = split(gram)
            grams[i, :, :C] = gh
            grams[i, :, C:] = gl
            started[i] = column(2, j) * queries
            kh_t, kl_t = split(keys.T)
            keys_t[i, :, :C] = kh_t
            keys_t[i, :, C:] = kl_t
            rights[i, :, DV:] = column(4, j) * keys
            rights[i, :, :DV] = column(1, j) * convolved(2, 2 * CHIPS * DK + head * DV, j)
        for level in range(6):
            half = [dot(lowers[i] * joins[level], kinv[i]).astype(BF16) for i in range(GROUP)]
            kinv = [kinv[i] - dot(kinv[i], half[i]).astype(BF16) for i in range(GROUP)]
            if waiting:
                waiting.pop(0)()
        solved = [rights[i] + dot(kinv[i] - unit, rights[i].astype(BF16)) for i in range(GROUP)]
        while waiting:
            waiting.pop(0)()
        for i, j in enumerate(blocks):
            new_values, write_keys = solved[i][:, :DV], solved[i][:, DV:]
            gh, gl = grams[i, :, :C], grams[i, :, C:]
            kh_t, kl_t = keys_t[i, :, :C], keys_t[i, :, C:]
            transit[j] = dot(kh_t, (column(3, j) * write_keys).astype(BF16)).astype(BF16)
            adds[j] = dot3((kh_t, kl_t), split(column(3, j) * new_values))
            local_out[j] = dot3((gh, gl), split(new_values))
            read_high, read_low = split(started[i] - dot(gh, write_keys.astype(BF16)))
            reads[j, :, :DK] = read_high
            reads[j, :, DK:] = read_low
            waiting.append(functools.partial(chain, j))
    while waiting:
        waiting.pop(0)()


def run_head(place, scale_log, bias, mine, theirs, taps, gain):
    vmem = pl.BlockSpec(memory_space=pltpu.VMEM)
    smem = pl.BlockSpec(memory_space=pltpu.SMEM)
    return pl.pallas_call(
        head_kernel,
        out_shape=jax.ShapeDtypeStruct((SEGMENTS, C, DV), BF16),
        in_specs=[smem, smem, smem, vmem, vmem, vmem, vmem],
        out_specs=vmem,
        scratch_shapes=[
            pltpu.VMEM((3, 8 + SEGMENTS * C, DK), F32),
            pltpu.VMEM((SEGMENTS, C), F32),
            pltpu.VMEM((SEGMENTS, C), F32),
            pltpu.VMEM((SEGMENTS, C, DV), F32),
            pltpu.VMEM((SEGMENTS, C, 2 * DK), BF16),
            pltpu.VMEM((SEGMENTS, DK, DK), BF16),
            pltpu.VMEM((SEGMENTS, DK, DV), F32),
            pltpu.VMEM((6, C, C), BF16),
            pltpu.VMEM((GROUP, C, 2 * C), BF16),
            pltpu.VMEM((GROUP, C, DK), F32),
            pltpu.VMEM((GROUP, DK, 2 * C), BF16),
            pltpu.VMEM((GROUP, C, DV + DK), F32),
        ],
        compiler_params=pltpu.CompilerParams(vmem_limit_bytes=40 * 2**20),
        cost_estimate=pl.CostEstimate(flops=10**10, bytes_accessed=2**25, transcendentals=0),
        name="head",
    )(place, scale_log, bias, mine, theirs, taps, gain)


def in_order_of(place, core, heads, ordered):
    y, x = place[2], place[3]
    for second in range(SIDE):
        for first in range(SIDE):
            back_x = jnp.where(core == 0, first, second)
            back_y = jnp.where(core == 0, second, first)
            head = lax.rem(y - back_y + SIDE, SIDE) * SIDE + lax.rem(x - back_x + SIDE, SIDE)
            at = (second * SIDE + first) * DV
            ordered[:, at : at + DV] = heads[head]


def product_of(ordered, weights):
    width = SIDE * DV
    total = dot(ordered[:, :width], weights[0][...].reshape(width, HALF))
    for second in range(1, SIDE):
        at = second * width
        total = total + dot(ordered[:, at : at + width], weights[second][...].reshape(width, HALF))
    return total.astype(BF16)


def project_kernel(place, heads, gate, *rest):
    own, others, out, normed, ordered = rest[:SIDE], rest[SIDE : 2 * SIDE], *rest[2 * SIDE :]
    core = place[1]
    for h in range(VH):
        at = slice(h * DV, (h + 1) * DV)
        normed[h] = (heads[h].astype(F32) * silu(gate[:, at].astype(F32))).astype(BF16)
    for its_core, weights in ((core, own), (1 - core, others)):
        in_order_of(place, its_core, normed, ordered)
        out[:, pl.ds(pl.multiple_of(its_core * HALF, HALF), HALF)] = product_of(ordered, weights)


def project(place, heads, gate, weights, other_weights):
    vmem = pl.BlockSpec(memory_space=pltpu.VMEM)
    return pl.pallas_call(
        project_kernel,
        out_shape=jax.ShapeDtypeStruct((C, WIDTH), BF16),
        in_specs=[pl.BlockSpec(memory_space=pltpu.SMEM)] + [vmem] * (2 + 2 * SIDE),
        out_specs=vmem,
        compiler_params=pltpu.CompilerParams(vmem_limit_bytes=40 * 2**20),
        cost_estimate=pl.CostEstimate(flops=2 * C * WIDTH * WIDTH, bytes_accessed=2**23, transcendentals=0),
        scratch_shapes=[pltpu.VMEM((VH, C, DV), BF16), pltpu.VMEM((C, WIDTH), BF16)],
        name="project",
    )(place, heads, gate, *weights, *other_weights)


def along(block, distance, second):
    route = []
    for i in range(SEGMENTS):
        by_x = (i % 2 == 0) != second
        for y in range(SIDE):
            for x in range(SIDE):
                to_y, to_x = (y, (x + distance) % SIDE) if by_x else ((y + distance) % SIDE, x)
                route.append(((i * SIDE + y) * SIDE + x, (i * SIDE + to_y) * SIDE + to_x))
    return lax.ppermute(block, ("seq", "fsdp"), route)


def local(
    qkv_raw,
    output_gate,
    decay_codes,
    beta_codes,
    conv_weight,
    decay_scale_log,
    decay_bias,
    norm_gain,
    out_weight,
):
    index, row = lax.axis_index("seq"), lax.axis_index("fsdp")
    place = jnp.stack([index // 2, index % 2, row // SIDE, row % SIDE]).astype(jnp.int32)
    barrier = lax.optimization_barrier

    pieces, half = cut_pieces(place, qkv_raw[0], decay_codes[0], beta_codes[0], out_weight)
    arrived = {0: pieces[0]}
    for distance in (1, 7, 2, 6, 3, 5, 4):
        arrived[distance] = to_chip(pieces[distance], distance)
    half, arrived[2], arrived[6] = barrier((half, arrived[2], arrived[6]))
    line = jnp.stack([half] + [along(half, distance, False) for distance in (1, 2, 3)])
    mine = jnp.stack([arrived[distance] for distance in range(CHIPS)])
    mine, line = barrier((mine, line))
    theirs, other_line = other_core(mine), other_core(line)
    weights = [line] + [along(line, distance, True) for distance in (1, 2, 3)]
    rows = run_head(place, decay_scale_log, decay_bias, mine, theirs, conv_weight, norm_gain[None])
    heads = lax.all_to_all(rows, "seq", 0, 0)
    heads, *later = barrier((heads, *weights[1:]))
    weights = [line, *later]
    other_weights = [other_line] + [other_core(weight) for weight in later]
    return project(place, heads, output_gate[0], weights, other_weights)[None]


def solution(mesh):
    return jax.shard_map(
        local,
        mesh=mesh,
        in_specs=(
            P("fsdp", "seq", None),
            P("fsdp", "seq", None),
            P("fsdp", None, "seq"),
            P("fsdp", None, "seq"),
            P(),
            P(),
            P(),
            P(),
            P("fsdp", None),
        ),
        out_specs=P("fsdp", "seq", None),
        check_vma=False,
    )
```

time: 127 us -> 95.2 us (0.75)
  Pallas kernels: 40.3 us -> 17.2 us
  blocking collectives: 22.7 us -> 0 us
  starting transfers between devices: 18.5 us -> 40.6 us
  between operations: 13.5 us -> 0.2 us
  waiting for transfers between devices: 24.6 us -> 34.3 us
  local copies, waits for them, and re-layouts: 6.72 us -> 1.88 us
    pallas_call x1, Pallas kernels: 36.4 us -> 9.37 us  [run_head(): pl.pallas_call(head_kernel, out_shape=jax.ShapeDtypeStruct((SEGMENTS, C,...]
    all_to_all x1 -> x0, blocking collectives: 22.7 us -> none  [local(): heads = lax.all_to_all(rows, 'seq', 0, 0)]
    all_to_all x0 -> x1, waiting for transfers between devices: none -> 13.4 us  [local(): heads = lax.all_to_all(rows, 'seq', 0, 0)]
    ppermute x7, waiting for transfers between devices: 18.2 us -> 6.92 us  [to_chip(): lax.ppermute(block, 'seq', [(i, (i + 2 * distance) % SEGMENTS) for i in r...]
    all_to_all x0 -> x1, starting transfers between devices: none -> 9.86 us  [local(): heads = lax.all_to_all(rows, 'seq', 0, 0)]
    ppermute x0 -> x6, starting transfers between devices: none -> 9.28 us  [along(): return lax.ppermute(block, ('seq', 'fsdp'), route)]
    ppermute x0 -> x6, waiting for transfers between devices: none -> 8.66 us  [along(): return lax.ppermute(block, ('seq', 'fsdp'), route)]
    ppermute x2 -> x5, starting transfers between devices: 0.97 us -> 5.25 us  [other_core(): return lax.ppermute(block, 'seq', [(i, i ^ 1) for i in range(SEGMENTS)])]
  transfers between devices with their start and end apart: 10 -> 19, of which waited for: 6 -> 9; matrix products, arithmetic and copies ran while one was open for 0% -> 1% of each run, Pallas kernels for 30% -> 10%
where the time goes in v1:
time: 95.2 us; the launch traced here: 95 us
  starting transfers between devices  40.6 us (43%)
  waiting for transfers between devices  34.3 us (36%)
  Pallas kernels  17.2 us (18%)
  local copies, waits for them, and re-layouts  1.88 us (2%)
    ppermute x7, starting transfers between devices, to_chip(): lax.ppermute(block, 'seq', [(i, (i + 2 * distance) % SEGMENTS) for i in r...  16.2 us
    all_to_all x1, waiting for transfers between devices, local(): heads = lax.all_to_all(rows, 'seq', 0, 0)  13.4 us
    all_to_all x1, starting transfers between devices, local(): heads = lax.all_to_all(rows, 'seq', 0, 0)  9.86 us
    pallas_call x1, Pallas kernels, run_head(): pl.pallas_call(head_kernel, out_shape=jax.ShapeDtypeStruct((SEGMENTS, C,...  9.37 us
    ppermute x6, starting transfers between devices, along(): return lax.ppermute(block, ('seq', 'fsdp'), route)  9.28 us
    ppermute x6, waiting for transfers between devices, along(): return lax.ppermute(block, ('seq', 'fsdp'), route)  8.66 us
    ppermute x7, waiting for transfers between devices, to_chip(): lax.ppermute(block, 'seq', [(i, (i + 2 * distance) % SEGMENTS) for i in r...  6.92 us
    ppermute x5, waiting for transfers between devices, other_core(): return lax.ppermute(block, 'seq', [(i, i ^ 1) for i in range(SEGMENTS)])  5.36 us
  transfers between devices with their start and end apart: 19, of which 9 were waited for; matrix products, arithmetic and copies ran while one was open for 1% of the time, Pallas kernels for 10%

profile of v1, /device:TPU:1, one launch (start us, length us, event | category | flops | bytes accessed | tf_op | source)
XLA Modules:
  0.0 95.0 jit_solution(12908450213543890997)
XLA Ops:
  0.0 0.6 pad_add_fusion.place
  0.6 3.5 %pieces.1 = (bf16[528,128]{1,0:T(8,128)(2,1)}, bf16[528,128]{1,0:T(8,128)(2,1)}, bf16[528,128]{1,0:T(8,128)(2,1)}, bf16[528,128]{1,0:T(8,128)(2,1)}, bf16[528,12...) custom-call(s32[4]{0:T(128)} %pad_add_fusion.place, ...), custom_call_target="tpu_custom_call" | custom-call | tf_op jit(solution)/shard_map/pieces/pallas_call | solution.py:98
  4.1 0.0 copy-start.7
  4.1 2.5 %collective-permute-start = (bf16[528,128]{1,0:T(8,128)(2,1)}, bf16[528,128]{1,0:T(8,128)(2,1)S(1)}, u32[]{:S(2)}, u32[]{:S(2)}) collective-permute-start(bf16[528,128]{1,0:T(8,128)(2,1)} %get-tuple-element.24), channel_id=1, source_target_pairs={{0,32},{16,48},{32,64},{48,80},{64,96},{80,112},{96,128},{112,144}... | collective-permute-start | bytes 405512 | tf_op jit(solution)/shard_map/ppermute | solution.py:29
  6.7 3.0 %collective-permute-start.1 = (bf16[528,128]{1,0:T(8,128)(2,1)}, bf16[528,128]{1,0:T(8,128)(2,1)S(1)}, u32[]{:S(2)}, u32[]{:S(2)}) collective-permute-start(bf16[528,128]{1,0:T(8,128)(2,1)} %get-tuple-element.26), channel_id=1, source_target_pairs={{0,64},{16,80},{32,96},{48,112},{64,128},{80,144},{96,160},{112,17... | collective-permute-start | bytes 405512 | tf_op jit(solution)/shard_map/ppermute | solution.py:29
  9.6 2.1 %collective-permute-start.2 = (bf16[528,128]{1,0:T(8,128)(2,1)}, bf16[528,128]{1,0:T(8,128)(2,1)S(1)}, u32[]{:S(2)}, u32[]{:S(2)}) collective-permute-start(bf16[528,128]{1,0:T(8,128)(2,1)} %get-tuple-element.27), channel_id=1, source_target_pairs={{0,192},{16,208},{32,224},{48,240},{64,0},{80,16},{96,32},{112,48}... | collective-permute-start | bytes 405512 | tf_op jit(solution)/shard_map/ppermute | solution.py:29
  11.8 2.8 %collective-permute-start.3 = (bf16[528,128]{1,0:T(8,128)(2,1)}, bf16[528,128]{1,0:T(8,128)(2,1)S(1)}, u32[]{:S(2)}, u32[]{:S(2)}) collective-permute-start(bf16[528,128]{1,0:T(8,128)(2,1)} %get-tuple-element.29), channel_id=1, source_target_pairs={{0,96},{16,112},{32,128},{48,144},{64,160},{80,176},{96,192},{112,... | collective-permute-start | bytes 405512 | tf_op jit(solution)/shard_map/ppermute | solution.py:29
  14.6 1.7 %collective-permute-start.4 = (bf16[528,128]{1,0:T(8,128)(2,1)}, bf16[528,128]{1,0:T(8,128)(2,1)S(1)}, u32[]{:S(2)}, u32[]{:S(2)}) collective-permute-start(bf16[528,128]{1,0:T(8,128)(2,1)} %get-tuple-element.30), channel_id=1, source_target_pairs={{0,128},{16,144},{32,160},{48,176},{64,192},{80,208},{96,224},{112... | collective-permute-start | bytes 405512 | tf_op jit(solution)/shard_map/ppermute | solution.py:29
  16.2 0.9 bitcast_dynamic-update-slice_fusion.7
  17.2 1.5 %collective-permute-done.1 = bf16[528,128]{1,0:T(8,128)(2,1)S(1)} collective-permute-done((bf16[528,128]{1,0:T(8,128)(2,1)}, bf16[528,128]{1,0:T(8,128)(2,1)S(1)}, u32[]{:S(2)}, u32[]{:S(2)}) %collective-permute-start.1) | collective-permute-done | bytes 135200 | tf_op jit(solution)/shard_map/ppermute | solution.py:29
  18.7 4.1 %collective-permute-start.5 = (bf16[528,128]{1,0:T(8,128)(2,1)}, bf16[528,128]{1,0:T(8,128)(2,1)S(1)}, u32[]{:S(2)}, u32[]{:S(2)}) collective-permute-start(bf16[528,128]{1,0:T(8,128)(2,1)} %get-tuple-element.31), channel_id=1, source_target_pairs={{0,160},{16,176},{32,192},{48,208},{64,224},{80,240},{96,0},{112,1... | collective-permute-start | bytes 405512 | tf_op jit(solution)/shard_map/ppermute | solution.py:29
  22.8 0.0 collective-permute-done.2
  22.8 0.0 collective-permute-start.6
  22.8 0.0 collective-permute-done
  22.8 2.8 %collective-permute-start.9 = (bf16[128,1024]{1,0:T(8,128)(2,1)}, bf16[128,1024]{1,0:T(8,128)(2,1)S(1)}, u32[]{:S(2)}, u32[]{:S(2)}) collective-permute-start(bf16[128,1024]{1,0:T(8,128)(2,1)} %get-tuple-element.34), channel_id=1, source_target_pairs={{0,3},{1,0},{2,1},{3,2},{4,7},{5,4},{6,5},{7,6},{8,11},{9,8},{10,9... | collective-permute-start | bytes 786440 | tf_op jit(solution)/shard_map/ppermute | solution.py:328
  25.7 3.9 %collective-permute-done.3 = bf16[528,128]{1,0:T(8,128)(2,1)S(1)} collective-permute-done((bf16[528,128]{1,0:T(8,128)(2,1)}, bf16[528,128]{1,0:T(8,128)(2,1)S(1)}, u32[]{:S(2)}, u32[]{:S(2)}) %collective-permute-start.3) | collective-permute-done | bytes 135200 | tf_op jit(solution)/shard_map/ppermute | solution.py:29
  29.5 2.9 %collective-permute-start.8 = (bf16[128,1024]{1,0:T(8,128)(2,1)}, bf16[128,1024]{1,0:T(8,128)(2,1)S(1)}, u32[]{:S(2)}, u32[]{:S(2)}) collective-permute-start(bf16[128,1024]{1,0:T(8,128)(2,1)} %get-tuple-element.34), channel_id=1, source_target_pairs={{0,2},{1,3},{2,0},{3,1},{4,6},{5,7},{6,4},{7,5},{8,10},{9,11},{10,... | collective-permute-start | bytes 786440 | tf_op jit(solution)/shard_map/ppermute | solution.py:328
  32.5 0.0 collective-permute-done.4
  32.5 0.5 collective-permute-start.7
  33.0 0.0 collective-permute-done.5
  33.0 1.5 %collective-permute-done.6 = bf16[528,128]{1,0:T(8,128)(2,1)S(1)} collective-permute-done((bf16[528,128]{1,0:T(8,128)(2,1)}, bf16[528,128]{1,0:T(8,128)(2,1)S(1)}, u32[]{:S(2)}, u32[]{:S(2)}) %collective-permute-start.6) | collective-permute-done | bytes 135200 | tf_op jit(solution)/shard_map/ppermute | solution.py:29
  34.6 0.0 copy-start.3
  34.6 0.0 copy-start.4
  34.6 0.0 copy-start.5
  34.6 0.0 copy-start.6
  34.6 0.0 collective-permute-done.9
  34.6 1.9 %collective-permute-done.8 = bf16[128,1024]{1,0:T(8,128)(2,1)S(1)} collective-permute-done((bf16[128,1024]{1,0:T(8,128)(2,1)}, bf16[128,1024]{1,0:T(8,128)(2,1)S(1)}, u32[]{:S(2)}, u32[]{:S(2)}) %collective-permute-start.8) | collective-permute-done | bytes 262176 | tf_op jit(solution)/shard_map/ppermute | solution.py:328
  36.5 3.1 %collective-permute-done.7 = bf16[128,1024]{1,0:T(8,128)(2,1)S(1)} collective-permute-done((bf16[128,1024]{1,0:T(8,128)(2,1)S(1)}, bf16[128,1024]{1,0:T(8,128)(2,1)S(1)}, u32[]{:S(2)}, u32[]{:S(2)}) %collective-permute-start.7) | collective-permute-done | bytes 262176 | tf_op jit(solution)/shard_map/ppermute | solution.py:328
  39.6 0.1 pad_maximum_fusion.rest_0_
  39.7 4.5 %collective-permute-start.10 = (bf16[8,528,128]{2,1,0:T(8,128)(2,1)S(1)}, bf16[8,528,128]{2,1,0:T(8,128)(2,1)S(1)}, u32[]{:S(2)}, u32[]{:S(2)}) collective-permute-start(bf16[8,528,128]{2,1,0:T(8,128)(2,1)S(1)} %bitcast_dynamic-update-slice_fusion.mine), channel_id=1, source_target_pairs={{0,16},{16,0},{32,48},{48,32},{64,80},{80,64},{96,112},{112,96},{1... | collective-permute-start | bytes 3244040 | tf_op jit(solution)/shard_map/ppermute | solution.py:35
  44.3 0.3 collective-permute-start.13
  44.5 2.8 %collective-permute-start.12 = (bf16[4,128,1024]{2,1,0:T(8,128)(2,1)S(1)}, bf16[4,128,1024]{2,1,0:T(8,128)(2,1)}, u32[]{:S(2)}, u32[]{:S(2)}) collective-permute-start(bf16[4,128,1024]{2,1,0:T(8,128)(2,1)S(1)} %pad_maximum_fusion.rest_0_), channel_id=1, source_target_pairs={{0,8},{1,9},{2,10},{3,11},{4,12},{5,13},{6,14},{7,15},{8,0},{9,1},... | collective-permute-start | bytes 3145736 | tf_op jit(solution)/shard_map/ppermute | solution.py:328
  47.3 0.0 collective-permute-start.11
  47.4 9.4 %head.1 = bf16[16,128,128]{2,1,0:T(8,128)(2,1)S(1)} custom-call(s32[4]{0:T(128)S(1)} %copy-done.2, f32[16]{0:T(128)S(1)} %copy-done.4, f32[16]{0:T(128)S(1)} %copy-done.5, bf16[8,528,128]{2,1,0:T(8,128)(2,1)S(1)} %bitcast_dynamic-update-slice_fusion.mine, bf16[8,528,128]{2,1,0:T(8,128)(2,1)S(1)} %collective-permute-done.10.theirs, f32[4,4096]{1,0:T(4,128)S(1)} %copy-done.3, ...), custom_call_target="tpu_custom_call" | custom-call | flops 10000000000 | bytes 33554432 | tf_op jit(solution)/shard_map/head/pallas_call | solution.py:250
  56.8 0.0 copy-start.1
  56.8 0.8 copy-done.1
  57.6 9.9 %all-to-all-start = ((bf16[16,128,128]{2,1,0:T(8,128)(2,1)}), bf16[16,128,128]{2,1,0:T(8,128)(2,1)S(1)}, u32[]{:S(2)}, u32[]{:S(2)}) async-start(bf16[16,128,128]{2,1,0:T(8,128)(2,1)} %copy-done.1), calls=%async_computation | async-start | bytes 1048576 | tf_op jit(solution)/shard_map/all_to_all | solution.py:357
  67.4 0.2 collective-permute-start.14
  67.6 0.0 collective-permute-done.13.rest_3_
  67.6 0.0 collective-permute-done.12.rest_2_
  67.6 3.7 %collective-permute-done.11.rest_1_ = bf16[4,128,1024]{2,1,0:T(8,128)(2,1)} collective-permute-done((bf16[4,128,1024]{2,1,0:T(8,128)(2,1)S(1)}, bf16[4,128,1024]{2,1,0:T(8,128)(2,1)}, u32[]{:S(2)}, u32[]{:S(2)}) %collective-permute-start.11) | collective-permute-done | bytes 1048608 | tf_op jit(solution)/shard_map/ppermute | solution.py:328
  71.3 13.4 %all-to-all-done.heads = bf16[16,128,128]{2,1,0:T(8,128)(2,1)S(1)} async-done(((bf16[16,128,128]{2,1,0:T(8,128)(2,1)}), bf16[16,128,128]{2,1,0:T(8,128)(2,1)S(1)}, u32[]{:S(2)}, u32[]{:S(2)}) %all-to-all-start) | async-done | bytes 524320 | tf_op jit(solution)/shard_map/all_to_all | solution.py:357
  84.7 0.0 collective-permute-start.15
  84.7 0.5 collective-permute-start.16
  85.2 0.0 collective-permute-start.17
  85.3 2.4 %collective-permute-done.15.rest_5_ = bf16[4,128,1024]{2,1,0:T(8,128)(2,1)S(1)} collective-permute-done((bf16[4,128,1024]{2,1,0:T(8,128)(2,1)}, bf16[4,128,1024]{2,1,0:T(8,128)(2,1)S(1)}, u32[]{:S(2)}, u32[]{:S(2)}) %collective-permute-start.15) | collective-permute-done | bytes 1048608 | tf_op jit(solution)/shard_map/ppermute | solution.py:35
  87.6 3.0 %collective-permute-done.16.rest_6_ = bf16[4,128,1024]{2,1,0:T(8,128)(2,1)S(1)} collective-permute-done((bf16[4,128,1024]{2,1,0:T(8,128)(2,1)}, bf16[4,128,1024]{2,1,0:T(8,128)(2,1)S(1)}, u32[]{:S(2)}, u32[]{:S(2)}) %collective-permute-start.16) | collective-permute-done | bytes 1048608 | tf_op jit(solution)/shard_map/ppermute | solution.py:35
  90.6 4.4 %project.1 = bf16[128,2048]{1,0:T(8,128)(2,1)} custom-call(s32[4]{0:T(128)S(1)} %copy-done.2, bf16[16,128,128]{2,1,0:T(8,128)(2,1)S(1)} %all-to-all-done.heads, bf16[128,2048]{1,0:T(8,128)(2,1)S(1)} %bitcast.30, bf16[4,128,1024]{2,1,0:T(8,128)(2,1)S(1)} %pad_maximum_fusion.rest_0_, bf16[4,128,1024]{2,1,0:T(8,128)(2,1)} %collective-permute-done.11.rest_1_, ...), custom_call_target="tpu_custom_call" | custom-call | flops 1073741824 | bytes 8388608 | tf_op jit(solution)/shard_map/project/pallas_call | solution.py:308
  (19 shorter events, 0.2 us)
Async XLA Ops:
  4.1 28.4 %copy-start.7 = (bf16[128,1024]{1,0:T(8,128)(2,1)S(1)}, bf16[128,1024]{1,0:T(8,128)(2,1)}, u32[]{:S(2)}) copy-start(bf16[128,1024]{1,0:T(8,128)(2,1)} %get-tuple-element.34) | copy-start | bytes 786436
  4.1 18.7 %collective-permute-start = (bf16[528,128]{1,0:T(8,128)(2,1)}, bf16[528,128]{1,0:T(8,128)(2,1)S(1)}, u32[]{:S(2)}, u32[]{:S(2)}) collective-permute-start(bf16[528,128]{1,0:T(8,128)(2,1)} %get-tuple-element.24), channel_id=1, source_target_pairs={{0,32},{16,48},{32,64},{48,80},{64,96},{80,112},{96,128},{112,144}... | collective-permute-start | bytes 405512 | tf_op jit(solution)/shard_map/ppermute | solution.py:29
  6.7 12.1 %collective-permute-start.1 = (bf16[528,128]{1,0:T(8,128)(2,1)}, bf16[528,128]{1,0:T(8,128)(2,1)S(1)}, u32[]{:S(2)}, u32[]{:S(2)}) collective-permute-start(bf16[528,128]{1,0:T(8,128)(2,1)} %get-tuple-element.26), channel_id=1, source_target_pairs={{0,64},{16,80},{32,96},{48,112},{64,128},{80,144},{96,160},{112,17... | collective-permute-start | bytes 405512 | tf_op jit(solution)/shard_map/ppermute | solution.py:29
  9.6 13.1 %collective-permute-start.2 = (bf16[528,128]{1,0:T(8,128)(2,1)}, bf16[528,128]{1,0:T(8,128)(2,1)S(1)}, u32[]{:S(2)}, u32[]{:S(2)}) collective-permute-start(bf16[528,128]{1,0:T(8,128)(2,1)} %get-tuple-element.27), channel_id=1, source_target_pairs={{0,192},{16,208},{32,224},{48,240},{64,0},{80,16},{96,32},{112,48}... | collective-permute-start | bytes 405512 | tf_op jit(solution)/shard_map/ppermute | solution.py:29
  11.8 17.8 %collective-permute-start.3 = (bf16[528,128]{1,0:T(8,128)(2,1)}, bf16[528,128]{1,0:T(8,128)(2,1)S(1)}, u32[]{:S(2)}, u32[]{:S(2)}) collective-permute-start(bf16[528,128]{1,0:T(8,128)(2,1)} %get-tuple-element.29), channel_id=1, source_target_pairs={{0,96},{16,112},{32,128},{48,144},{64,160},{80,176},{96,192},{112,... | collective-permute-start | bytes 405512 | tf_op jit(solution)/shard_map/ppermute | solution.py:29
  14.6 17.9 %collective-permute-start.4 = (bf16[528,128]{1,0:T(8,128)(2,1)}, bf16[528,128]{1,0:T(8,128)(2,1)S(1)}, u32[]{:S(2)}, u32[]{:S(2)}) collective-permute-start(bf16[528,128]{1,0:T(8,128)(2,1)} %get-tuple-element.30), channel_id=1, source_target_pairs={{0,128},{16,144},{32,160},{48,176},{64,192},{80,208},{96,224},{112... | collective-permute-start | bytes 405512 | tf_op jit(solution)/shard_map/ppermute | solution.py:29
  18.7 14.3 %collective-permute-start.5 = (bf16[528,128]{1,0:T(8,128)(2,1)}, bf16[528,128]{1,0:T(8,128)(2,1)S(1)}, u32[]{:S(2)}, u32[]{:S(2)}) collective-permute-start(bf16[528,128]{1,0:T(8,128)(2,1)} %get-tuple-element.31), channel_id=1, source_target_pairs={{0,160},{16,176},{32,192},{48,208},{64,224},{80,240},{96,0},{112,1... | collective-permute-start | bytes 405512 | tf_op jit(solution)/shard_map/ppermute | solution.py:29
  22.8 11.7 %collective-permute-start.6 = (bf16[528,128]{1,0:T(8,128)(2,1)}, bf16[528,128]{1,0:T(8,128)(2,1)S(1)}, u32[]{:S(2)}, u32[]{:S(2)}) collective-permute-start(bf16[528,128]{1,0:T(8,128)(2,1)} %get-tuple-element.33), channel_id=1, source_target_pairs={{0,224},{16,240},{32,0},{48,16},{64,32},{80,48},{96,64},{112,80},{... | collective-permute-start | bytes 405512 | tf_op jit(solution)/shard_map/ppermute | solution.py:29
  22.8 11.8 %collective-permute-start.9 = (bf16[128,1024]{1,0:T(8,128)(2,1)}, bf16[128,1024]{1,0:T(8,128)(2,1)S(1)}, u32[]{:S(2)}, u32[]{:S(2)}) collective-permute-start(bf16[128,1024]{1,0:T(8,128)(2,1)} %get-tuple-element.34), channel_id=1, source_target_pairs={{0,3},{1,0},{2,1},{3,2},{4,7},{5,4},{6,5},{7,6},{8,11},{9,8},{10,9... | collective-permute-start | bytes 786440 | tf_op jit(solution)/shard_map/ppermute | solution.py:328
  29.5 7.0 %collective-permute-start.8 = (bf16[128,1024]{1,0:T(8,128)(2,1)}, bf16[128,1024]{1,0:T(8,128)(2,1)S(1)}, u32[]{:S(2)}, u32[]{:S(2)}) collective-permute-start(bf16[128,1024]{1,0:T(8,128)(2,1)} %get-tuple-element.34), channel_id=1, source_target_pairs={{0,2},{1,3},{2,0},{3,1},{4,6},{5,7},{6,4},{7,5},{8,10},{9,11},{10,... | collective-permute-start | bytes 786440 | tf_op jit(solution)/shard_map/ppermute | solution.py:328
  32.5 7.1 %collective-permute-start.7 = (bf16[128,1024]{1,0:T(8,128)(2,1)S(1)}, bf16[128,1024]{1,0:T(8,128)(2,1)S(1)}, u32[]{:S(2)}, u32[]{:S(2)}) collective-permute-start(bf16[128,1024]{1,0:T(8,128)(2,1)S(1)} %copy-done.7), channel_id=1, source_target_pairs={{0,1},{1,2},{2,3},{3,0},{4,5},{5,6},{6,7},{7,4},{8,9},{9,10},{10,1... | collective-permute-start | bytes 786440 | tf_op jit(solution)/shard_map/ppermute | solution.py:328
  34.6 12.8 %copy-start.2 = (s32[4]{0:T(128)S(1)}, s32[4]{0:T(128)}, u32[]{:S(2)}) copy-start(s32[4]{0:T(128)} %pad_add_fusion.place) | copy-start | bytes 52
  34.6 12.8 %copy-start.3 = (f32[4,4096]{1,0:T(4,128)S(1)}, f32[4,4096]{1,0:T(4,128)}, u32[]{:S(2)}) copy-start(f32[4,4096]{1,0:T(4,128)} %taps.1) | copy-start | bytes 196612
  34.6 12.8 %copy-start.4 = (f32[16]{0:T(128)S(1)}, f32[16]{0:T(128)}, u32[]{:S(2)}) copy-start(f32[16]{0:T(128)} %scale_log.1) | copy-start | bytes 196
  34.6 12.8 %copy-start.5 = (f32[16]{0:T(128)S(1)}, f32[16]{0:T(128)}, u32[]{:S(2)}) copy-start(f32[16]{0:T(128)} %bias.1) | copy-start | bytes 196
  34.6 12.8 %copy-start.6 = (f32[128]{0:T(128)S(1)}, f32[128]{0:T(128)}, u32[]{:S(2)}) copy-start(f32[128]{0:T(128)} %param.16) | copy-start | bytes 1540
  39.7 7.6 %collective-permute-start.10 = (bf16[8,528,128]{2,1,0:T(8,128)(2,1)S(1)}, bf16[8,528,128]{2,1,0:T(8,128)(2,1)S(1)}, u32[]{:S(2)}, u32[]{:S(2)}) collective-permute-start(bf16[8,528,128]{2,1,0:T(8,128)(2,1)S(1)} %bitcast_dynamic-update-slice_fusion.mine), channel_id=1, source_target_pairs={{0,16},{16,0},{32,48},{48,32},{64,80},{80,64},{96,112},{112,96},{1... | collective-permute-start | bytes 3244040 | tf_op jit(solution)/shard_map/ppermute | solution.py:35
  44.3 23.4 %collective-permute-start.13 = (bf16[4,128,1024]{2,1,0:T(8,128)(2,1)S(1)}, bf16[4,128,1024]{2,1,0:T(8,128)(2,1)S(1)}, u32[]{:S(2)}, u32[]{:S(2)}) collective-permute-start(bf16[4,128,1024]{2,1,0:T(8,128)(2,1)S(1)} %pad_maximum_fusion.rest_0_), channel_id=1, source_target_pairs={{0,12},{1,13},{2,14},{3,15},{4,0},{5,1},{6,2},{7,3},{8,4},{9,5},{1... | collective-permute-start | bytes 3145736 | tf_op jit(solution)/shard_map/ppermute | solution.py:328
  44.5 23.1 %collective-permute-start.12 = (bf16[4,128,1024]{2,1,0:T(8,128)(2,1)S(1)}, bf16[4,128,1024]{2,1,0:T(8,128)(2,1)}, u32[]{:S(2)}, u32[]{:S(2)}) collective-permute-start(bf16[4,128,1024]{2,1,0:T(8,128)(2,1)S(1)} %pad_maximum_fusion.rest_0_), channel_id=1, source_target_pairs={{0,8},{1,9},{2,10},{3,11},{4,12},{5,13},{6,14},{7,15},{8,0},{9,1},... | collective-permute-start | bytes 3145736 | tf_op jit(solution)/shard_map/ppermute | solution.py:328
  47.3 24.0 %collective-permute-start.11 = (bf16[4,128,1024]{2,1,0:T(8,128)(2,1)S(1)}, bf16[4,128,1024]{2,1,0:T(8,128)(2,1)}, u32[]{:S(2)}, u32[]{:S(2)}) collective-permute-start(bf16[4,128,1024]{2,1,0:T(8,128)(2,1)S(1)} %pad_maximum_fusion.rest_0_), channel_id=1, source_target_pairs={{0,4},{1,5},{2,6},{3,7},{4,8},{5,9},{6,10},{7,11},{8,12},{9,13},{1... | collective-permute-start | bytes 3145736 | tf_op jit(solution)/shard_map/ppermute | solution.py:328
  56.8 0.8 copy-start.1
  57.6 33.1 %copy-start = (bf16[1,128,2048]{2,1,0:T(8,128)(2,1)S(1)}, bf16[1,128,2048]{2,1,0:T(8,128)(2,1)}, u32[]{:S(2)}) copy-start(bf16[1,128,2048]{2,1,0:T(8,128)(2,1)} %param.10) | copy-start | bytes 1572868
  57.6 27.2 %all-to-all-start = ((bf16[16,128,128]{2,1,0:T(8,128)(2,1)}), bf16[16,128,128]{2,1,0:T(8,128)(2,1)S(1)}, u32[]{:S(2)}, u32[]{:S(2)}) async-start(bf16[16,128,128]{2,1,0:T(8,128)(2,1)} %copy-done.1), calls=%async_computation | async-start | bytes 1048576 | tf_op jit(solution)/shard_map/all_to_all | solution.py:357
  67.4 17.8 %collective-permute-start.14 = (bf16[4,128,1024]{2,1,0:T(8,128)(2,1)S(1)}, bf16[4,128,1024]{2,1,0:T(8,128)(2,1)}, u32[]{:S(2)}, u32[]{:S(2)}) collective-permute-start(bf16[4,128,1024]{2,1,0:T(8,128)(2,1)S(1)} %pad_maximum_fusion.rest_0_), channel_id=1, source_target_pairs={{0,16},{16,0},{32,48},{48,32},{64,80},{80,64},{96,112},{112,96},{1... | collective-permute-start | bytes 3145736 | tf_op jit(solution)/shard_map/ppermute | solution.py:35
  84.7 2.9 %collective-permute-start.15 = (bf16[4,128,1024]{2,1,0:T(8,128)(2,1)}, bf16[4,128,1024]{2,1,0:T(8,128)(2,1)S(1)}, u32[]{:S(2)}, u32[]{:S(2)}) collective-permute-start(bf16[4,128,1024]{2,1,0:T(8,128)(2,1)} %collective-permute-done.11.rest_1_), channel_id=1, source_target_pairs={{0,16},{16,0},{32,48},{48,32},{64,80},{80,64},{96,112},{112,96},{1... | collective-permute-start | bytes 3145736 | tf_op jit(solution)/shard_map/ppermute | solution.py:35
  84.7 5.9 %collective-permute-start.16 = (bf16[4,128,1024]{2,1,0:T(8,128)(2,1)}, bf16[4,128,1024]{2,1,0:T(8,128)(2,1)S(1)}, u32[]{:S(2)}, u32[]{:S(2)}) collective-permute-start(bf16[4,128,1024]{2,1,0:T(8,128)(2,1)} %collective-permute-done.12.rest_2_), channel_id=1, source_target_pairs={{0,16},{16,0},{32,48},{48,32},{64,80},{80,64},{96,112},{112,96},{1... | collective-permute-start | bytes 3145736 | tf_op jit(solution)/shard_map/ppermute | solution.py:35
  85.2 5.4 %collective-permute-start.17 = (bf16[4,128,1024]{2,1,0:T(8,128)(2,1)S(1)}, bf16[4,128,1024]{2,1,0:T(8,128)(2,1)S(1)}, u32[]{:S(2)}, u32[]{:S(2)}) collective-permute-start(bf16[4,128,1024]{2,1,0:T(8,128)(2,1)S(1)} %collective-permute-done.13.rest_3_), channel_id=1, source_target_pairs={{0,16},{16,0},{32,48},{48,32},{64,80},{80,64},{96,112},{112,96},{1... | collective-permute-start | bytes 3145736 | tf_op jit(solution)/shard_map/ppermute | solution.py:35

commit v2 on v1

v2 whole, which is shorter than its diff:
```python
import math

import jax
import jax.numpy as jnp
from jax import lax
from jax.experimental import pallas as pl
from jax.experimental.pallas import tpu as pltpu
from jax.sharding import PartitionSpec as P


CHIPS = 8
SEGMENTS = 16
C = 128
DK = 128
DV = 128
VH = 16
HEADS = 8
KEYS = 4
BLOCKS = 2
WIDTH = 2048
HALF = 1024
QK = KEYS * DK
RAW = 2 * QK + HEADS * DV
ROW = RAW + HEADS * DV
TALL = C + 16
TERMS_MIB = 60
SIDE = 4
F32 = jnp.float32
BF16 = jnp.bfloat16
VMEM = pl.BlockSpec(memory_space=pltpu.VMEM)
SMEM = pl.BlockSpec(memory_space=pltpu.SMEM)


def to_chip(block, distance):
    return lax.ppermute(
        block, "seq", [(i, (i + 2 * distance) % SEGMENTS) for i in range(SEGMENTS)]
    )


def other_core(block):
    return lax.ppermute(block, "seq", [(i, i ^ 1) for i in range(SEGMENTS)])


def between_chips(blocks):
    groups = [[2 * z + c for z in range(CHIPS)] for c in range(2)]
    return lax.all_to_all(blocks, "seq", 0, 0, axis_index_groups=groups)


def dot(left, right):
    return jnp.dot(left, right, preferred_element_type=F32)


def dot_t(left, right):
    return lax.dot_general(
        left, right, (((1,), (1,)), ((), ())), preferred_element_type=F32
    )


def split(value):
    high = value.astype(BF16)
    return high, (value - high.astype(F32)).astype(BF16)


def dot3(left, right):
    lh, ll = left
    rh, rl = right
    return dot(jnp.concatenate([lh, ll], 1), jnp.concatenate([rh, rh], 0)) + dot(lh, rl)


def silu(value):
    return value / (1.0 + jnp.exp(-value))


ANY = pl.BlockSpec(memory_space=pl.ANY)
KEPT = (
    ((C, C), F32),
    ((BLOCKS * HEADS, C), F32),
    ((BLOCKS * HEADS, C, C), F32),
    ((BLOCKS * KEYS, C, 2 * DK), BF16),
    ((BLOCKS * HEADS, C, 2 * DV + 2 * DK), BF16),
    ((HEADS, DK, DK), BF16),
    ((HEADS, DK, 2 * DV), BF16),
)


def shape(dims, kind):
    return jax.ShapeDtypeStruct(dims, kind)


def my_core():
    return lax.rem(lax.axis_index("seq"), 2)


def params(mib):
    return pltpu.CompilerParams(vmem_limit_bytes=mib * 2**20)


def cost(flops, moved):
    return pl.CostEstimate(flops=flops, bytes_accessed=moved, transcendentals=0)


def cut_kernel(raw, gate, decay, beta, weight, give, tail, half, rows, decays, betas, sems):
    core = my_core()
    copies = []

    def copy(source, target):
        copies.append(pltpu.make_async_copy(source, target, sems.at[len(copies)]))
        copies[-1].start()

    def cut(ref, first, width, part, at=0, count=C):
        column = pl.multiple_of(first + part * width, width)
        return ref.at[at : at + count, pl.ds(column, width)]

    copy(decay, decays)
    copy(beta, betas)
    parts = ((0, QK, 0), (2 * QK, QK, QK), (4 * QK, HEADS * DV, 2 * QK))
    for first, width, to in parts:
        copy(cut(raw, first, width, 1 - core), give.at[0:C, to : to + width])
    copy(cut(gate, 0, HEADS * DV, 1 - core), give.at[0:C, RAW:ROW])
    for first, width, to in parts:
        copy(cut(raw, first, width, core, C - 16, 16), tail.at[:, to : to + width])
    copy(cut(weight, 0, HALF, core), half)
    give[C:TALL, 2 * C :] = jnp.zeros((16, ROW - 2 * C), BF16)
    copies[0].wait()
    copies[1].wait()
    for at, codes in ((0, decays), (C, betas)):
        code = codes[pl.ds(pl.multiple_of((1 - core) * HEADS, HEADS), HEADS), :]
        rows[0:HEADS, at : at + C] = (code >> 4).astype(F32)
        rows[HEADS:16, at : at + C] = (code & 15).astype(F32)
    give[C:TALL, 0 : 2 * C] = rows[...].astype(BF16)
    for one in copies[2:]:
        one.wait()


def cut_rows(raw, gate, decay, beta, weight):
    return pl.pallas_call(
        cut_kernel,
        out_shape=[
            shape((TALL, ROW), BF16),
            shape((16, RAW), BF16),
            shape((weight.shape[0], HALF), BF16),
        ],
        in_specs=[ANY] * 5,
        out_specs=[VMEM] * 3,
        scratch_shapes=[
            pltpu.VMEM((16, 2 * C), F32),
            pltpu.VMEM((VH, C), jnp.int32),
            pltpu.VMEM((VH, C), jnp.int32),
            pltpu.SemaphoreType.DMA((10,)),
        ],
        compiler_params=params(60),
        name="cut",
    )(raw, gate, decay, beta, weight)


def assemble(core, staged, halo, raw, first, width):
    at = slice(first, first + width)
    raw[0:8] = halo[:, at].astype(F32)[8:16]
    for i, block in enumerate((core, 1 - core)):
        raw[pl.ds(pl.multiple_of(8 + block * C, 8), C)] = staged[i].astype(F32)


def convolved(raw, taps, at, channel, j):
    weights = taps[:, pl.ds(pl.multiple_of(channel, DK), DK)]
    base = 8 + j * C - 3
    total = weights[0:1] * raw[base : base + C, at : at + DK]
    for t in range(1, 4):
        total = total + weights[t : t + 1] * raw[base + t : base + t + C, at : at + DK]
    return silu(total)


def over_length(value):
    return lax.rsqrt(jnp.sum(value * value, -1, keepdims=True) + 1e-06)


def unit_of(j, h):
    return j * HEADS + h


def column(columns, kind, unit):
    at = kind * BLOCKS * HEADS + unit
    return columns[:, at : at + 1]


def terms_kernel(
    scale_log, bias, decay_codes, beta_codes, own, got, halo, taps,
    message, *rest,
):
    outs, kept, rest = rest[: len(KEPT)], rest[len(KEPT) : 2 * len(KEPT)], rest[2 * len(KEPT) :]
    raw, staged, their_codes, decay, beta, joins, keys_t, rights, transit, arrive, sems = rest
    columns, starts, pairs, keys_out, solved_out, early_transit, early_add = kept
    core = my_core()
    copies = []
    column_of = pl.multiple_of(2 * QK + core * QK, QK), pl.multiple_of(4 * QK + core * HEADS * DV, HEADS * DV)
    loads = [
        pltpu.make_async_copy(*one, arrive.at[i])
        for i, one in enumerate((
            (own.at[:, pl.ds(column_of[0], QK)], staged.at[0, :, 0:QK]),
            (own.at[:, pl.ds(column_of[1], HEADS * DV)], staged.at[0, :, QK:]),
            (got.at[0:C, QK:RAW], staged.at[1]),
            (got.at[C:TALL, 0 : 2 * C], their_codes),
        ))
    ]
    for one in loads:
        one.start()

    def leave(which, first=0, count=None):
        source, target = kept[which], outs[which]
        if count:
            source, target = source.at[first : first + count], target.at[first : first + count]
        copies.append(pltpu.make_async_copy(source, target, sems.at[len(copies)]))
        copies[-1].start()

    loads[3].wait()
    codes = their_codes[...].astype(F32)
    ours = pl.ds(pl.multiple_of(core * HEADS, HEADS), HEADS)
    theirs = pl.ds(pl.multiple_of((1 - core) * HEADS, HEADS), HEADS)
    decay[ours, :] = decay_codes[ours, :].astype(F32)
    beta[ours, :] = beta_codes[ours, :].astype(F32)
    decay[theirs, :] = 16.0 * codes[0:HEADS, 0:C] + codes[HEADS:16, 0:C]
    beta[theirs, :] = 16.0 * codes[0:HEADS, C:] + codes[HEADS:16, C:]

    def by_head(ref):
        rows = [jnp.full((1, C), ref[core * HEADS + h], F32) for h in range(HEADS)]
        return jnp.concatenate(rows * BLOCKS, 0)

    level = decay[...] / 32.0 - 16.0 + by_head(bias)
    small = jnp.exp(-jnp.abs(level))
    one_more = 1.0 + small
    gap = one_more - 1.0
    log1p = jnp.where(gap == 0.0, small, jnp.log(one_more) * (small / jnp.where(gap == 0.0, 1.0, gap)))
    log_decay = -jnp.exp(by_head(scale_log)) * (jnp.maximum(level, 0.0) + log1p)
    row_ids = lax.broadcasted_iota(jnp.int32, (C, C), 0)
    col_ids = lax.broadcasted_iota(jnp.int32, (C, C), 1)
    sums = jnp.dot(
        log_decay,
        (row_ids <= col_ids).astype(F32),
        precision=lax.Precision.HIGHEST,
        preferred_element_type=F32,
    )
    strength = 1.0 / (1.0 + jnp.exp(8.0 - beta[...] / 32.0))
    start = jnp.exp(sums)
    starts[...] = start
    end = jnp.exp(sums[:, C - 1 : C] - sums)
    units = BLOCKS * HEADS
    columns[...] = jnp.concatenate(
        [sums, strength, start, end, strength * start, jnp.zeros((C - 5 * units, C), F32)], 0
    ).T

    leave(0)
    leave(1)
    inclusive = row_ids >= col_ids
    strict = row_ids > col_ids
    eye = (row_ids == col_ids).astype(BF16)
    for k in range(1, 7):
        joins[k - 1] = (
            ((row_ids >> (k + 1)) == (col_ids >> (k + 1))) & ((row_ids >> k) != (col_ids >> k))
        ).astype(F32).astype(BF16)
    near = (row_ids >> 1) == (col_ids >> 1)

    for one in loads[:3]:
        one.wait()
    assemble(core, staged, halo, raw, QK, RAW - QK)
    for j in range(BLOCKS):
        lowers, inverses = [], []
        for g in range(KEYS):
            keys = convolved(raw, taps, g * DK, 2 * QK + core * QK + g * DK, j)
            keys = keys * over_length(keys)
            kh, kl = split(keys)
            keys_out[j * KEYS + g, :, :DK] = kh
            keys_out[j * KEYS + g, :, DK:] = kl
            kh_t, kl_t = split(keys.T)
            keys_t[g, :, :C] = kh_t
            keys_t[g, :, C:] = kl_t
            gram = dot_t(kh, kh)
            for h in (2 * g, 2 * g + 1):
                u = unit_of(j, h)
                pair = jnp.where(inclusive, jnp.exp(jnp.minimum(column(columns, 0, u) - sums[u : u + 1], 0.0)), 0.0)
                pairs[u] = pair
                lower = jnp.where(strict, column(columns, 1, u) * pair * gram, 0.0)
                lowers.append(lower.astype(BF16))
                inverses.append(eye - jnp.where(near, lower, 0.0).astype(BF16))
                values = convolved(raw, taps, QK + h * DV, 4 * QK + core * HEADS * DV + h * DV, j)
                rights[h, :, :DV] = column(columns, 1, u) * values
                rights[h, :, DV:] = column(columns, 4, u) * keys
        leave(2, j * HEADS, HEADS)
        leave(3, j * KEYS, KEYS)
        for k in range(6):
            halves = [dot(lowers[h] * joins[k], inverses[h]).astype(BF16) for h in range(HEADS)]
            inverses = [inverses[h] - dot(inverses[h], halves[h]).astype(BF16) for h in range(HEADS)]
        for h in range(HEADS):
            u = unit_of(j, h)
            solved = rights[h] + dot(inverses[h] - eye, rights[h].astype(BF16))
            values, writes = solved[:, :DV], solved[:, DV:]
            high, low = split(values)
            solved_out[u, :, :DV] = high
            solved_out[u, :, DV : 2 * DV] = low
            high, low = split(writes)
            solved_out[u, :, 2 * DV : 2 * DV + DK] = high
            solved_out[u, :, 2 * DV + DK :] = low
            leave(4, u, 1)
            kt = keys_t[h // 2, :, :C], keys_t[h // 2, :, C:]
            moved = dot3(kt, split(column(columns, 3, u) * writes))
            add = dot3(kt, split(column(columns, 3, u) * values))
            last = start[u : u + 1, C - 1 : C]
            if j == 0:
                transit[h] = moved
                early_transit[h] = moved.astype(BF16)
                add_high, add_low = split(add)
                early_add[h, :, :DV] = add_high
                early_add[h, :, DV:] = add_low
            else:
                first = start[unit_of(0, h) : unit_of(0, h) + 1, C - 1 : C]
                second = moved.astype(BF16)
                crossed = dot(second, jnp.concatenate([early_transit[h], early_add[h, :, :DV]], 1))
                earlier = early_add[h, :, :DV].astype(F32) + early_add[h, :, DV:].astype(F32)
                message[h, 0:C, :DK] = (last * transit[h] + first * moved - crossed[:, :DK]).astype(BF16)
                message[h, 0:C, DK:] = (last * earlier - crossed[:, DK:] + add).astype(BF16)
                both = jnp.broadcast_to(first * last, (1, DK))
                top = both.astype(BF16).astype(F32)
                middle = (both - top).astype(BF16).astype(F32)
                parts = jnp.concatenate([top, middle, both - top - middle, jnp.zeros((13, DK), F32)], 0)
                message[h, C:TALL, :DK] = parts.astype(BF16)
                message[h, C:TALL, DK:] = jnp.zeros((16, DV), BF16)
        if j == 0:
            leave(5)
            leave(6)
    for one in copies:
        one.wait()


def run_terms(*operands):
    units = BLOCKS * HEADS
    return pl.pallas_call(
        terms_kernel,
        out_shape=[shape((HEADS, TALL, DK + DV), BF16)] + [shape(*one) for one in KEPT],
        in_specs=[SMEM] * 2 + [VMEM] * 2 + [ANY] * 2 + [VMEM] * 2,
        out_specs=[VMEM] + [ANY] * len(KEPT),
        scratch_shapes=[pltpu.VMEM(*one) for one in KEPT]
        + [
            pltpu.VMEM((8 + BLOCKS * C, RAW - QK), F32),
            pltpu.VMEM((BLOCKS, C, RAW - QK), BF16),
            pltpu.VMEM((16, 2 * C), BF16),
            pltpu.VMEM((units, C), F32),
            pltpu.VMEM((units, C), F32),
            pltpu.VMEM((6, C, C), BF16),
            pltpu.VMEM((KEYS, DK, 2 * C), BF16),
            pltpu.VMEM((HEADS, C, DV + DK), F32),
            pltpu.VMEM((HEADS, DK, DK), F32),
            pltpu.SemaphoreType.DMA((4,)),
            pltpu.SemaphoreType.DMA((24,)),
        ],
        compiler_params=params(TERMS_MIB),
        cost_estimate=cost(8 * 10**9, 2**25),
        name="terms",
    )(*operands)


def reads_kernel(own, got, halo, taps, *rest):
    sources, (base, reads), kept = rest[: len(KEPT)], rest[len(KEPT) : len(KEPT) + 2], rest[len(KEPT) + 2 : -5]
    bases, readers, raw, staged, sems = rest[-5:]
    core = my_core()
    columns, starts, pairs, keys, solved, early_transit, early_add = kept
    copies = []

    def move(source, target, first=None, count=HEADS):
        if first is not None:
            source, target = source.at[first : first + count], target.at[first : first + count]
        copies.append(pltpu.make_async_copy(source, target, sems.at[len(copies)]))
        copies[-1].start()

    move(own.at[:, pl.ds(pl.multiple_of(core * QK, QK), QK)], staged.at[0])
    move(got.at[0:C, 0:QK], staged.at[1])
    for i in (0, 1, 3):
        move(sources[i], kept[i])
    for j in range(BLOCKS):
        move(sources[2], pairs, j * HEADS)
        move(sources[4], solved, j * HEADS)
        if j == 0:
            move(sources[5], early_transit)
            move(sources[6], early_add)
    for one in copies[:5]:
        one.wait()
    assemble(core, staged, halo, raw, 0, QK)
    for j in range(BLOCKS):
        for one in copies[5:7] if j == 0 else copies[7:11]:
            one.wait()
        for g in range(KEYS):
            queries = convolved(raw, taps, g * DK, core * QK + g * DK, j)
            queries = queries * (over_length(queries) * (1.0 / math.sqrt(DK)))
            qh, ql = split(queries)
            both = keys[j * KEYS + g]
            kh, kl = both[:, :DK], both[:, DK:]
            plain = dot_t(jnp.concatenate([qh, ql], 1), jnp.concatenate([kh, kh], 1)) + dot_t(qh, kl)
            for h in (2 * g, 2 * g + 1):
                u = unit_of(j, h)
                gram = split(pairs[u] * plain)
                inner = solved[u]
                out = dot3(gram, (inner[:, :DV], inner[:, DV : 2 * DV]))
                writes = inner[:, 2 * DV : 2 * DV + DK], inner[:, 2 * DV + DK :]
                read = column(columns, 2, u) * queries - dot3(gram, writes)
                if j:
                    high, low = split(read)
                    out = out + dot3((high, low), (early_add[h, :, :DV], early_add[h, :, DV:]))
                    before = unit_of(0, h)
                    read = starts[before : before + 1, C - 1 : C] * read - dot(high, early_transit[h])
                bases[u] = out
                high, low = split(read)
                readers[u, :, :DK] = high
                readers[u, :, DK:] = low
        move(bases, base, j * HEADS)
        move(readers, reads, j * HEADS)
    for one in copies[11:]:
        one.wait()


def run_reads(*operands):
    units = BLOCKS * HEADS
    return pl.pallas_call(
        reads_kernel,
        out_shape=[shape((units, C, DV), F32), shape((units, C, 2 * DK), BF16)],
        in_specs=[ANY] * 2 + [VMEM] * 2 + [ANY] * len(KEPT),
        out_specs=[ANY] * 2,
        scratch_shapes=[pltpu.VMEM(*one) for one in KEPT]
        + [
            pltpu.VMEM((units, C, DV), F32),
            pltpu.VMEM((units, C, 2 * DK), BF16),
            pltpu.VMEM((8 + BLOCKS * C, QK), F32),
            pltpu.VMEM((BLOCKS, C, QK), BF16),
            pltpu.SemaphoreType.DMA((15,)),
        ],
        compiler_params=params(TERMS_MIB),
        cost_estimate=cost(4 * 10**9, 2**24),
        name="reads",
    )(*operands)


def enter_kernel(arrived, entering, messages, sems):
    copies = [
        pltpu.make_async_copy(arrived.at[chip], messages.at[chip], sems.at[chip]) for chip in range(CHIPS - 1)
    ]
    for one in copies:
        one.start()
    state = jnp.zeros((DK, DV), F32)
    for chip in range(CHIPS):
        high = state.astype(BF16)
        entering[chip] = high
        if chip < CHIPS - 1:
            copies[chip].wait()
            parts = messages[chip, C:TALL, :DK].astype(F32)
            factor = parts[0:1] + parts[1:2] + parts[2:3]
            state = factor * state - dot(messages[chip, 0:C, :DK], high) + messages[chip, 0:C, DK:].astype(F32)


def run_enter(messages):
    return pl.pallas_call(
        enter_kernel,
        out_shape=shape((CHIPS, DK, DV), BF16),
        in_specs=[ANY],
        out_specs=VMEM,
        scratch_shapes=[pltpu.VMEM((CHIPS, TALL, DK + DV), BF16), pltpu.SemaphoreType.DMA((CHIPS - 1,))],
        compiler_params=params(TERMS_MIB),
        cost_estimate=cost(10**9, 2**20),
        name="enter",
    )(messages)


def finish_kernel(arrived, base, reads, gate, got, gain, mine, theirs, entering, bases, readers, gates, sems):
    core = my_core()
    blocks = 1 - core, core
    loads = [pltpu.make_async_copy(arrived, entering, sems.at[6])]
    loads[0].start()
    for i, block in enumerate(blocks):
        units = pl.ds(pl.multiple_of(block * HEADS, HEADS), HEADS)
        column_of = pl.multiple_of(core * HEADS * DV, HEADS * DV)
        a_gate = gate.at[:, pl.ds(column_of, HEADS * DV)] if i else got.at[0:C, RAW:ROW]
        for source, target in ((a_gate, gates), (reads.at[units], readers), (base.at[units], bases)):
            loads.append(pltpu.make_async_copy(source, target.at[i], sems.at[len(loads) - 1]))
            loads[-1].start()
    for i, out in enumerate((theirs, mine)):
        for one in loads[4:] if i else loads[:4]:
            one.wait()
        for h in range(HEADS):
            state = entering[h]
            rows = bases[i, h] + dot(readers[i, h], jnp.concatenate([state, state], 0))
            square_mean = jnp.mean(rows * rows, -1, keepdims=True)
            opening = silu(gates[i, :, h * DV : (h + 1) * DV].astype(F32))
            out[h] = (rows * lax.rsqrt(square_mean + 1e-06) * gain[...] * opening).astype(BF16)


def run_finish(entering, base, reads, gate, got, gain):
    return pl.pallas_call(
        finish_kernel,
        out_shape=[shape((HEADS, C, DV), BF16)] * 2,
        in_specs=[ANY] * 5 + [VMEM],
        out_specs=[VMEM] * 2,
        scratch_shapes=[
            pltpu.VMEM((HEADS, DK, DV), BF16),
            pltpu.VMEM((BLOCKS, HEADS, C, DV), F32),
            pltpu.VMEM((BLOCKS, HEADS, C, 2 * DK), BF16),
            pltpu.VMEM((BLOCKS, C, HEADS * DV), BF16),
            pltpu.SemaphoreType.DMA((7,)),
        ],
        compiler_params=params(TERMS_MIB),
        cost_estimate=cost(2 * 10**9, 2**22),
        name="finish",
    )(entering, base, reads, gate, got, gain)


def in_order_of(core, heads, ordered):
    row = lax.axis_index("fsdp")
    y, x = row // SIDE, lax.rem(row, SIDE)
    for second in range(SIDE):
        for first in range(SIDE):
            back_x = jnp.where(core == 0, first, second)
            back_y = jnp.where(core == 0, second, first)
            head = lax.rem(y - back_y + SIDE, SIDE) * SIDE + lax.rem(x - back_x + SIDE, SIDE)
            at = (second * SIDE + first) * DV
            ordered[:, at : at + DV] = heads[head]


def product_of(ordered, weights):
    width = SIDE * DV
    total = dot(ordered[:, :width], weights[0][...].reshape(width, HALF))
    for second in range(1, SIDE):
        at = second * width
        total = total + dot(ordered[:, at : at + width], weights[second][...].reshape(width, HALF))
    return total.astype(BF16)


def first_kernel(mine, theirs, *rest):
    weights, (normed, out, ordered) = rest[:SIDE], rest[SIDE:]
    core = my_core()
    for source, its_core in ((mine, core), (theirs, 1 - core)):
        normed[pl.ds(its_core * HEADS, HEADS)] = source[...]
    in_order_of(core, normed, ordered)
    out[...] = product_of(ordered, weights)


def second_kernel(normed, first, *rest):
    weights, (out, ordered) = rest[:SIDE], rest[SIDE:]
    core = my_core()
    in_order_of(1 - core, normed, ordered)
    out[:, pl.ds(pl.multiple_of(core * HALF, HALF), HALF)] = first[...]
    out[:, pl.ds(pl.multiple_of((1 - core) * HALF, HALF), HALF)] = product_of(ordered, weights)


def project(mine, theirs, weights, other_weights):
    settings = dict(
        in_specs=[VMEM] * (2 + SIDE),
        compiler_params=params(40),
        cost_estimate=cost(C * WIDTH * WIDTH, 2**22),
        scratch_shapes=[pltpu.VMEM((C, WIDTH), BF16)],
    )
    normed, first = pl.pallas_call(
        first_kernel,
        out_shape=[shape((VH, C, DV), BF16), shape((C, HALF), BF16)],
        out_specs=[VMEM] * 2,
        name="project_first",
        **settings,
    )(mine, theirs, *weights)
    return pl.pallas_call(
        second_kernel,
        out_shape=shape((C, WIDTH), BF16),
        out_specs=VMEM,
        name="project_second",
        **settings,
    )(normed, first, *other_weights)


def along(block, distance, second):
    route = []
    for i in range(SEGMENTS):
        by_x = (i % 2 == 0) != second
        for y in range(SIDE):
            for x in range(SIDE):
                to_y, to_x = (y, (x + distance) % SIDE) if by_x else ((y + distance) % SIDE, x)
                route.append(((i * SIDE + y) * SIDE + x, (i * SIDE + to_y) * SIDE + to_x))
    return lax.ppermute(block, ("seq", "fsdp"), route)


def local(
    qkv_raw,
    output_gate,
    decay_codes,
    beta_codes,
    conv_weight,
    decay_scale_log,
    decay_bias,
    norm_gain,
    out_weight,
):
    barrier = lax.optimization_barrier
    raw, decay, beta = qkv_raw[0], decay_codes[0], beta_codes[0]
    give, tail, half = cut_rows(raw, output_gate[0], decay, beta, out_weight)
    got = other_core(give)
    tail = jnp.where(lax.axis_index("seq") % 2 == 0, got[C - 16 : C, :RAW], tail)
    halo = lax.ppermute(tail, "seq", [(i, i + 2) for i in range(SEGMENTS - 2)])
    parts = [along(half, distance, False) for distance in (1, 2, 3)]
    message, *kept = run_terms(
        decay_scale_log, decay_bias, decay, beta, raw, got, halo, conv_weight
    )
    message, half, *parts = barrier((message, half, *parts))
    messages = between_chips(message)
    line = jnp.stack([half, *parts])
    later = [along(line, distance, True) for distance in (1, 2, 3)]
    other_line = other_core(line)
    base, reads = run_reads(raw, got, halo, conv_weight, *kept)
    messages, base, reads = barrier((messages, base, reads))
    entering = between_chips(run_enter(messages))
    entering, *later = barrier((entering, *later))
    other_weights = [other_line] + [other_core(weight) for weight in later]
    mine, theirs = run_finish(entering, base, reads, output_gate[0], got, norm_gain[None])
    return project(mine, other_core(theirs), [line, *later], other_weights)[None]


def solution(mesh):
    return jax.shard_map(
        local,
        mesh=mesh,
        in_specs=(
            P("fsdp", "seq", None),
            P("fsdp", "seq", None),
            P("fsdp", None, "seq"),
            P("fsdp", None, "seq"),
            P(),
            P(),
            P(),
            P(),
            P("fsdp", None),
        ),
        out_specs=P("fsdp", "seq", None),
        check_vma=False,
    )
```

time: 95.2 us -> 88.1 us (0.925)
  Pallas kernels: 17.2 us -> 34.9 us
  starting transfers between devices: 40.6 us -> 27.9 us
  waiting for transfers between devices: 34.3 us -> 21.8 us
    pallas_call x3 -> x7, Pallas kernels: 17.2 us -> 34.9 us  [the longest x1 12.6 us: run_terms(): pl.pallas_call(terms_kernel, out_shape=[shape((HEADS, TALL, DK + DV), BF1...]
    ppermute x7 -> x1, starting transfers between devices: 16.2 us -> 1.8 us  [local(): halo = lax.ppermute(tail, 'seq', [(i, i + 2) for i in range(SEGMENTS - 2)])]
    ppermute x6, waiting for transfers between devices: 8.66 us -> 1.45 us  [along(): return lax.ppermute(block, ('seq', 'fsdp'), route)]
    ppermute x7 -> x1, waiting for transfers between devices: 6.92 us -> 0.01 us  [local(): halo = lax.ppermute(tail, 'seq', [(i, i + 2) for i in range(SEGMENTS - 2)])]
    all_to_all x1 -> x2, waiting for transfers between devices: 13.4 us -> 16.5 us  [between_chips(): return lax.all_to_all(blocks, 'seq', 0, 0, axis_index_groups=groups)]
    ppermute x5 -> x6, waiting for transfers between devices: 5.36 us -> 3.83 us  [other_core(): return lax.ppermute(block, 'seq', [(i, i ^ 1) for i in range(SEGMENTS)])]
    all_to_all x1 -> x2, starting transfers between devices: 9.86 us -> 10.7 us  [between_chips(): return lax.all_to_all(blocks, 'seq', 0, 0, axis_index_groups=groups)]
    ppermute x5 -> x6, starting transfers between devices: 5.25 us -> 5.41 us  [other_core(): return lax.ppermute(block, 'seq', [(i, i ^ 1) for i in range(SEGMENTS)])]
  transfers between devices with their start and end apart: 19 -> 15, of which waited for: 9 -> 5; matrix products, arithmetic and copies ran while one was open for 1% -> 0% of each run, Pallas kernels for 10% -> 33%
where the time goes in v2:
time: 88.1 us; the launch traced here: 87.4 us
  Pallas kernels  34.9 us (40%)
  starting transfers between devices  27.9 us (32%)
  waiting for transfers between devices  21.8 us (25%)
  local copies, waits for them, and re-layouts  1.59 us (2%)
  other arithmetic  1.03 us (1%)
    all_to_all x2, waiting for transfers between devices, between_chips(): return lax.all_to_all(blocks, 'seq', 0, 0, axis_index_groups=groups)  16.5 us
    pallas_call x1, Pallas kernels, run_terms(): pl.pallas_call(terms_kernel, out_shape=[shape((HEADS, TALL, DK + DV), BF1...  12.6 us
    all_to_all x2, starting transfers between devices, between_chips(): return lax.all_to_all(blocks, 'seq', 0, 0, axis_index_groups=groups)  10.7 us
    ppermute x6, starting transfers between devices, along(): return lax.ppermute(block, ('seq', 'fsdp'), route)  9.96 us
    pallas_call x1, Pallas kernels, run_reads(): pl.pallas_call(reads_kernel, out_shape=[shape((units, C, DV), F32), shape...  7.87 us
    ppermute x6, starting transfers between devices, other_core(): return lax.ppermute(block, 'seq', [(i, i ^ 1) for i in range(SEGMENTS)])  5.41 us
    ppermute x6, waiting for transfers between devices, other_core(): return lax.ppermute(block, 'seq', [(i, i ^ 1) for i in range(SEGMENTS)])  3.83 us
    pallas_call x1, Pallas kernels, project(): pl.pallas_call(second_kernel, out_shape=shape((C, WIDTH), BF16), out_spec...  3.69 us
  transfers between devices with their start and end apart: 15, of which 5 were waited for; matrix products, arithmetic and copies ran while one was open for 0% of the time, Pallas kernels for 33%

profile of v2, /device:TPU:1, one launch (start us, length us, event | category | flops | bytes accessed | tf_op | source)
XLA Modules:
  0.0 87.4 jit_solution(12567292898043367142)
XLA Ops:
  0.0 2.4 %cut.1 = (bf16[144,3072]{1,0:T(8,128)(2,1)}, bf16[16,2048]{1,0:T(8,128)(2,1)}, bf16[128,1024]{1,0:T(8,128)(2,1)}) custom-call(bf16[128,4096]{1,0:T(8,128)(2,1)} %bitcast.10, bf16[128,2048]{1,0:T(8,128)(2,1)} %bitcast.13, s32[16,128]{1,0:T(8,128)} %bitcast.19, s32[16,128]{1,0:T(8,128)} %bitcast.21, bf16[128,2048]{1,0:T(8,128)(2,1)} %weight.1), custom_call_target="tpu_custom_call" | custom-call | tf_op jit(solution)/shard_map/cut/pallas_call | solution.py:136
  2.4 3.3 %collective-permute-start = (bf16[144,3072]{1,0:T(8,128)(2,1)}, bf16[144,3072]{1,0:T(8,128)(2,1)S(1)}, u32[]{:S(2)}, u32[]{:S(2)}) collective-permute-start(bf16[144,3072]{1,0:T(8,128)(2,1)} %get-tuple-element.34), channel_id=1, source_target_pairs={{0,16},{16,0},{32,48},{48,32},{64,80},{80,64},{96,112},{112,96},{1... | collective-permute-start | bytes 2654216 | tf_op jit(solution)/shard_map/ppermute | solution.py:41
  5.8 2.3 %collective-permute-done.got = bf16[144,3072]{1,0:T(8,128)(2,1)S(1)} collective-permute-done((bf16[144,3072]{1,0:T(8,128)(2,1)}, bf16[144,3072]{1,0:T(8,128)(2,1)S(1)}, u32[]{:S(2)}, u32[]{:S(2)}) %collective-permute-start) | collective-permute-done | bytes 884768 | tf_op jit(solution)/shard_map/ppermute | solution.py:41
  8.0 0.0 copy-start.3
  8.0 0.9 %slice_select_fusion = bf16[16,2048]{1,0:T(8,128)(2,1)S(1)} fusion(bf16[16,2048]{1,0:T(8,128)(2,1)} %get-tuple-element.35, bf16[144,3072]{1,0:T(8,128)(2,1)S(1)} %collective-permute-done.got, pred[]{:T(512)S(6)} %eq.5), kind=kLoop, calls=%fused_computation.1 | loop fusion | flops 32768 | bytes 196609 | tf_op jit(solution)/shard_map/jit(_where)/select_n | solution.py:597
  8.9 1.8 %collective-permute-start.1 = (bf16[16,2048]{1,0:T(8,128)(2,1)S(1)}, bf16[16,2048]{1,0:T(8,128)(2,1)S(1)}, u32[]{:S(2)}, u32[]{:S(2)}) collective-permute-start(bf16[16,2048]{1,0:T(8,128)(2,1)S(1)} %slice_select_fusion), channel_id=1, source_target_pairs={{0,32},{16,48},{32,64},{48,80},{64,96},{80,112},{96,128},{112,144}... | collective-permute-start | bytes 196616 | tf_op jit(solution)/shard_map/ppermute | solution.py:598
  10.7 0.0 copy-start.2
  10.8 1.4 %collective-permute-start.2 = (bf16[128,1024]{1,0:T(8,128)(2,1)}, bf16[128,1024]{1,0:T(8,128)(2,1)S(1)}, u32[]{:S(2)}, u32[]{:S(2)}) collective-permute-start(bf16[128,1024]{1,0:T(8,128)(2,1)} %get-tuple-element.49), channel_id=1, source_target_pairs={{0,1},{1,2},{2,3},{3,0},{4,5},{5,6},{6,7},{7,4},{8,9},{9,10},{10,1... | collective-permute-start | bytes 786440 | tf_op jit(solution)/shard_map/ppermute | solution.py:579
  12.1 2.6 %collective-permute-start.3 = (bf16[128,1024]{1,0:T(8,128)(2,1)}, bf16[128,1024]{1,0:T(8,128)(2,1)S(1)}, u32[]{:S(2)}, u32[]{:S(2)}) collective-permute-start(bf16[128,1024]{1,0:T(8,128)(2,1)} %get-tuple-element.49), channel_id=1, source_target_pairs={{0,2},{1,3},{2,0},{3,1},{4,6},{5,7},{6,4},{7,5},{8,10},{9,11},{10,... | collective-permute-start | bytes 786440 | tf_op jit(solution)/shard_map/ppermute | solution.py:579
  14.8 1.1 %collective-permute-start.4 = (bf16[128,1024]{1,0:T(8,128)(2,1)}, bf16[128,1024]{1,0:T(8,128)(2,1)S(1)}, u32[]{:S(2)}, u32[]{:S(2)}) collective-permute-start(bf16[128,1024]{1,0:T(8,128)(2,1)} %get-tuple-element.49), channel_id=1, source_target_pairs={{0,3},{1,0},{2,1},{3,2},{4,7},{5,4},{6,5},{7,6},{8,11},{9,8},{10,9... | collective-permute-start | bytes 786440 | tf_op jit(solution)/shard_map/ppermute | solution.py:579
  15.8 0.0 collective-permute-done.1.halo
  15.8 0.0 copy-done.3
  15.8 0.0 copy-start.4
  15.8 0.6 copy-done.4
  16.4 12.6 %terms.1 = (bf16[8,144,256]{2,1,0:T(8,128)(2,1)}, f32[128,128]{1,0:T(8,128)}, f32[16,128]{1,0:T(8,128)}, f32[16,128,128]{2,1,0:T(8,128)}, bf16[8,128,256]{2,1,0:...) custom-call(f32[16]{0:T(128)} %scale_log.1, f32[16]{0:T(128)} %bias.1, ...), custom_call_target="tpu_custom_call" | custom-call | flops 8000000000 | bytes 33554432 | tf_op jit(solution)/shard_map/terms/pallas_call | solution.py:334
  29.0 0.0 collective-permute-done.2
  29.1 0.0 collective-permute-done.3
  29.1 0.0 collective-permute-done.4
  29.1 7.3 %all-to-all-start = ((bf16[8,144,256]{2,1,0:T(8,128)(2,1)}), bf16[8,144,256]{2,1,0:T(8,128)(2,1)}, u32[]{:S(2)}, u32[]{:S(2)}) async-start(bf16[8,144,256]{2,1,0:T(8,128)(2,1)} %get-tuple-element.38), calls=%async_computation | async-start | bytes 1179648 | tf_op jit(solution)/shard_map/all_to_all | solution.py:46
  36.4 0.0 copy-done.2
  36.4 0.1 pad_maximum_fusion.rest_0_
  36.5 1.3 %collective-permute-start.5 = (bf16[4,128,1024]{2,1,0:T(8,128)(2,1)S(1)}, bf16[4,128,1024]{2,1,0:T(8,128)(2,1)S(1)}, u32[]{:S(2)}, u32[]{:S(2)}) collective-permute-start(bf16[4,128,1024]{2,1,0:T(8,128)(2,1)S(1)} %pad_maximum_fusion.rest_0_), channel_id=1, source_target_pairs={{0,4},{1,5},{2,6},{3,7},{4,8},{5,9},{6,10},{7,11},{8,12},{9,13},{1... | collective-permute-start | bytes 3145736 | tf_op jit(solution)/shard_map/ppermute | solution.py:579
  37.8 2.5 %collective-permute-start.6 = (bf16[4,128,1024]{2,1,0:T(8,128)(2,1)S(1)}, bf16[4,128,1024]{2,1,0:T(8,128)(2,1)S(1)}, u32[]{:S(2)}, u32[]{:S(2)}) collective-permute-start(bf16[4,128,1024]{2,1,0:T(8,128)(2,1)S(1)} %pad_maximum_fusion.rest_0_), channel_id=1, source_target_pairs={{0,8},{1,9},{2,10},{3,11},{4,12},{5,13},{6,14},{7,15},{8,0},{9,1},... | collective-permute-start | bytes 3145736 | tf_op jit(solution)/shard_map/ppermute | solution.py:579
  40.3 1.2 %collective-permute-start.7 = (bf16[4,128,1024]{2,1,0:T(8,128)(2,1)S(1)}, bf16[4,128,1024]{2,1,0:T(8,128)(2,1)}, u32[]{:S(2)}, u32[]{:S(2)}) collective-permute-start(bf16[4,128,1024]{2,1,0:T(8,128)(2,1)S(1)} %pad_maximum_fusion.rest_0_), channel_id=1, source_target_pairs={{0,12},{1,13},{2,14},{3,15},{4,0},{5,1},{6,2},{7,3},{8,4},{9,5},{1... | collective-permute-start | bytes 3145736 | tf_op jit(solution)/shard_map/ppermute | solution.py:579
  41.4 7.9 %reads.1 = (f32[16,128,128]{2,1,0:T(8,128)}, bf16[16,128,256]{2,1,0:T(8,128)(2,1)}) custom-call(bf16[128,4096]{1,0:T(8,128)(2,1)} %bitcast.12, bf16[144,3072]{1,0:T(8,128)(2,1)} %copy-done.3, bf16[16,2048]{1,0:T(8,128)(2,1)} %copy-done.4, f32[4,4096]{1,0:T(4,128)} %taps.3, f32[128,128]{1,0:T(8,128)} %get-tuple-element.39.rest_0_, ...), custom_call_target="tpu_custom_call" | custom-call | flops 4000000000 | bytes 16777216 | tf_op jit(solution)/shard_map/reads/pallas_call | solution.py:419
  49.3 6.5 %all-to-all-done.arrived = bf16[8,144,256]{2,1,0:T(8,128)(2,1)} async-done(((bf16[8,144,256]{2,1,0:T(8,128)(2,1)}), bf16[8,144,256]{2,1,0:T(8,128)(2,1)}, u32[]{:S(2)}, u32[]{:S(2)}) %all-to-all-start) | async-done | bytes 589856 | tf_op jit(solution)/shard_map/all_to_all | solution.py:46
  55.8 2.7 %enter.1 = bf16[8,128,128]{2,1,0:T(8,128)(2,1)} custom-call(bf16[8,144,256]{2,1,0:T(8,128)(2,1)} %all-to-all-done.arrived), custom_call_target="tpu_custom_call" | custom-call | flops 1000000000 | bytes 1048576 | tf_op jit(solution)/shard_map/enter/pallas_call | solution.py:456
  58.5 3.4 %all-to-all-start.1 = ((bf16[8,128,128]{2,1,0:T(8,128)(2,1)}), bf16[8,128,128]{2,1,0:T(8,128)(2,1)S(1)}, u32[]{:S(2)}, u32[]{:S(2)}) async-start(bf16[8,128,128]{2,1,0:T(8,128)(2,1)} %enter.1), calls=%async_computation.1 | async-start | bytes 524288 | tf_op jit(solution)/shard_map/all_to_all | solution.py:46
  62.0 0.6 collective-permute-start.9
  62.5 0.0 collective-permute-done.5.rest_1_
  62.5 1.4 %collective-permute-done.6.rest_2_ = bf16[4,128,1024]{2,1,0:T(8,128)(2,1)S(1)} collective-permute-done((bf16[4,128,1024]{2,1,0:T(8,128)(2,1)S(1)}, bf16[4,128,1024]{2,1,0:T(8,128)(2,1)S(1)}, u32[]{:S(2)}, u32[]{:S(2)}) %collective-permute-start.6) | collective-permute-done | bytes 1048608 | tf_op jit(solution)/shard_map/ppermute | solution.py:579
  64.0 0.0 collective-permute-done.7.rest_3_
  64.0 10.0 %all-to-all-done.1.arrived = bf16[8,128,128]{2,1,0:T(8,128)(2,1)S(1)} async-done(((bf16[8,128,128]{2,1,0:T(8,128)(2,1)}), bf16[8,128,128]{2,1,0:T(8,128)(2,1)S(1)}, u32[]{:S(2)}, u32[]{:S(2)}) %all-to-all-start.1) | async-done | bytes 262176 | tf_op jit(solution)/shard_map/all_to_all | solution.py:46
  74.0 0.0 copy-start.1
  74.0 0.7 collective-permute-start.10
  74.7 0.0 collective-permute-start.11
  74.7 0.5 collective-permute-start.12
  75.2 0.0 copy-done.1
  75.2 3.7 %finish.1 = (bf16[8,128,128]{2,1,0:T(8,128)(2,1)}, bf16[8,128,128]{2,1,0:T(8,128)(2,1)}) custom-call(bf16[8,128,128]{2,1,0:T(8,128)(2,1)} %copy-done.1, f32[16,128,128]{2,1,0:T(8,128)} %get-tuple-element.54.base, bf16[16,128,256]{2,1,0:T(8,128)(2,1)} %get-tuple-element.55.reads, bf16[128,2048]{1,0:T(8,128)(2,1)} %bitcast.14, bf16[144,3072]{1,0:T(8,128)(2,1)} %copy-done.3, ...), custom_call_target="tpu_custom_call" | custom-call | flops 2000000000 | bytes 4194304 | tf_op jit(solution)/shard_map/finish/pallas_call | solution.py:492
  78.9 0.3 collective-permute-start.8
  79.2 1.6 %collective-permute-done.8.theirs = bf16[8,128,128]{2,1,0:T(8,128)(2,1)S(1)} collective-permute-done((bf16[8,128,128]{2,1,0:T(8,128)(2,1)}, bf16[8,128,128]{2,1,0:T(8,128)(2,1)S(1)}, u32[]{:S(2)}, u32[]{:S(2)}) %collective-permute-start.8) | collective-permute-done | bytes 262176 | tf_op jit(solution)/shard_map/ppermute | solution.py:41
  80.8 0.9 %copy-done = bf16[8,128,128]{2,1,0:T(8,128)(2,1)S(1)} copy-done((bf16[8,128,128]{2,1,0:T(8,128)(2,1)S(1)}, bf16[8,128,128]{2,1,0:T(8,128)(2,1)}, u32[]{:S(2)}) %copy-start) | copy-done | bytes 262168
  81.7 2.0 %project_first.1 = (bf16[16,128,128]{2,1,0:T(8,128)(2,1)S(1)}, bf16[128,1024]{1,0:T(8,128)(2,1)S(1)}) custom-call(bf16[8,128,128]{2,1,0:T(8,128)(2,1)S(1)} %copy-done, bf16[8,128,128]{2,1,0:T(8,128)(2,1)S(1)} %collective-permute-done.8.theirs, bf16[4,128,1024]{2,1,0:T(8,128)(2,1)S(1)} %pad_maximum_fusion.rest_0_, ...), custom_call_target="tpu_custom_call" | custom-call | flops 536870912 | bytes 4194304 | tf_op jit(solution)/shard_map/project_first/pallas_call | solution.py:555
  83.7 0.0 collective-permute-done.9.rest_0_
  83.7 0.0 collective-permute-done.10.rest_1_
  83.7 0.0 collective-permute-done.11.rest_2_
  83.7 0.0 collective-permute-done.12.rest_3_
  83.7 3.7 %project_second.1 = bf16[128,2048]{1,0:T(8,128)(2,1)} custom-call(bf16[16,128,128]{2,1,0:T(8,128)(2,1)S(1)} %get-tuple-element.61.normed, bf16[128,1024]{1,0:T(8,128)(2,1)S(1)} %get-tuple-element.62.first, bf16[4,128,1024]{2,1,0:T(8,128)(2,1)} %collective-permute-done.9.rest_0_, bf16[4,128,1024]{2,1,0:T(8,128)(2,1)} %collective-permute-done.10.rest_1_, ...), custom_call_target="tpu_custom_call" | custom-call | flops 536870912 | bytes 4194304 | tf_op jit(solution)/shard_map/project_second/pallas_call | solution.py:562
  (1 shorter events, 0.0 us)
Async XLA Ops:
  2.4 5.6 %collective-permute-start = (bf16[144,3072]{1,0:T(8,128)(2,1)}, bf16[144,3072]{1,0:T(8,128)(2,1)S(1)}, u32[]{:S(2)}, u32[]{:S(2)}) collective-permute-start(bf16[144,3072]{1,0:T(8,128)(2,1)} %get-tuple-element.34), channel_id=1, source_target_pairs={{0,16},{16,0},{32,48},{48,32},{64,80},{80,64},{96,112},{112,96},{1... | collective-permute-start | bytes 2654216 | tf_op jit(solution)/shard_map/ppermute | solution.py:41
  8.0 7.8 %copy-start.3 = (bf16[144,3072]{1,0:T(8,128)(2,1)}, bf16[144,3072]{1,0:T(8,128)(2,1)S(1)}, u32[]{:S(2)}) copy-start(bf16[144,3072]{1,0:T(8,128)(2,1)S(1)} %collective-permute-done.got) | copy-start | bytes 2654212
  8.9 6.9 %collective-permute-start.1 = (bf16[16,2048]{1,0:T(8,128)(2,1)S(1)}, bf16[16,2048]{1,0:T(8,128)(2,1)S(1)}, u32[]{:S(2)}, u32[]{:S(2)}) collective-permute-start(bf16[16,2048]{1,0:T(8,128)(2,1)S(1)} %slice_select_fusion), channel_id=1, source_target_pairs={{0,32},{16,48},{32,64},{48,80},{64,96},{80,112},{96,128},{112,144}... | collective-permute-start | bytes 196616 | tf_op jit(solution)/shard_map/ppermute | solution.py:598
  10.7 25.6 %copy-start.2 = (bf16[128,1024]{1,0:T(8,128)(2,1)S(1)}, bf16[128,1024]{1,0:T(8,128)(2,1)}, u32[]{:S(2)}) copy-start(bf16[128,1024]{1,0:T(8,128)(2,1)} %get-tuple-element.49) | copy-start | bytes 786436
  10.8 18.3 %collective-permute-start.2 = (bf16[128,1024]{1,0:T(8,128)(2,1)}, bf16[128,1024]{1,0:T(8,128)(2,1)S(1)}, u32[]{:S(2)}, u32[]{:S(2)}) collective-permute-start(bf16[128,1024]{1,0:T(8,128)(2,1)} %get-tuple-element.49), channel_id=1, source_target_pairs={{0,1},{1,2},{2,3},{3,0},{4,5},{5,6},{6,7},{7,4},{8,9},{9,10},{10,1... | collective-permute-start | bytes 786440 | tf_op jit(solution)/shard_map/ppermute | solution.py:579
  12.1 16.9 %collective-permute-start.3 = (bf16[128,1024]{1,0:T(8,128)(2,1)}, bf16[128,1024]{1,0:T(8,128)(2,1)S(1)}, u32[]{:S(2)}, u32[]{:S(2)}) collective-permute-start(bf16[128,1024]{1,0:T(8,128)(2,1)} %get-tuple-element.49), channel_id=1, source_target_pairs={{0,2},{1,3},{2,0},{3,1},{4,6},{5,7},{6,4},{7,5},{8,10},{9,11},{10,... | collective-permute-start | bytes 786440 | tf_op jit(solution)/shard_map/ppermute | solution.py:579
  14.8 14.3 %collective-permute-start.4 = (bf16[128,1024]{1,0:T(8,128)(2,1)}, bf16[128,1024]{1,0:T(8,128)(2,1)S(1)}, u32[]{:S(2)}, u32[]{:S(2)}) collective-permute-start(bf16[128,1024]{1,0:T(8,128)(2,1)} %get-tuple-element.49), channel_id=1, source_target_pairs={{0,3},{1,0},{2,1},{3,2},{4,7},{5,4},{6,5},{7,6},{8,11},{9,8},{10,9... | collective-permute-start | bytes 786440 | tf_op jit(solution)/shard_map/ppermute | solution.py:579
  15.8 0.6 copy-start.4
  29.1 26.8 %all-to-all-start = ((bf16[8,144,256]{2,1,0:T(8,128)(2,1)}), bf16[8,144,256]{2,1,0:T(8,128)(2,1)}, u32[]{:S(2)}, u32[]{:S(2)}) async-start(bf16[8,144,256]{2,1,0:T(8,128)(2,1)} %get-tuple-element.38), calls=%async_computation | async-start | bytes 1179648 | tf_op jit(solution)/shard_map/all_to_all | solution.py:46
  36.5 26.0 %collective-permute-start.5 = (bf16[4,128,1024]{2,1,0:T(8,128)(2,1)S(1)}, bf16[4,128,1024]{2,1,0:T(8,128)(2,1)S(1)}, u32[]{:S(2)}, u32[]{:S(2)}) collective-permute-start(bf16[4,128,1024]{2,1,0:T(8,128)(2,1)S(1)} %pad_maximum_fusion.rest_0_), channel_id=1, source_target_pairs={{0,4},{1,5},{2,6},{3,7},{4,8},{5,9},{6,10},{7,11},{8,12},{9,13},{1... | collective-permute-start | bytes 3145736 | tf_op jit(solution)/shard_map/ppermute | solution.py:579
  37.8 26.2 %collective-permute-start.6 = (bf16[4,128,1024]{2,1,0:T(8,128)(2,1)S(1)}, bf16[4,128,1024]{2,1,0:T(8,128)(2,1)S(1)}, u32[]{:S(2)}, u32[]{:S(2)}) collective-permute-start(bf16[4,128,1024]{2,1,0:T(8,128)(2,1)S(1)} %pad_maximum_fusion.rest_0_), channel_id=1, source_target_pairs={{0,8},{1,9},{2,10},{3,11},{4,12},{5,13},{6,14},{7,15},{8,0},{9,1},... | collective-permute-start | bytes 3145736 | tf_op jit(solution)/shard_map/ppermute | solution.py:579
  40.3 23.7 %collective-permute-start.7 = (bf16[4,128,1024]{2,1,0:T(8,128)(2,1)S(1)}, bf16[4,128,1024]{2,1,0:T(8,128)(2,1)}, u32[]{:S(2)}, u32[]{:S(2)}) collective-permute-start(bf16[4,128,1024]{2,1,0:T(8,128)(2,1)S(1)} %pad_maximum_fusion.rest_0_), channel_id=1, source_target_pairs={{0,12},{1,13},{2,14},{3,15},{4,0},{5,1},{6,2},{7,3},{8,4},{9,5},{1... | collective-permute-start | bytes 3145736 | tf_op jit(solution)/shard_map/ppermute | solution.py:579
  58.5 15.5 %all-to-all-start.1 = ((bf16[8,128,128]{2,1,0:T(8,128)(2,1)}), bf16[8,128,128]{2,1,0:T(8,128)(2,1)S(1)}, u32[]{:S(2)}, u32[]{:S(2)}) async-start(bf16[8,128,128]{2,1,0:T(8,128)(2,1)} %enter.1), calls=%async_computation.1 | async-start | bytes 524288 | tf_op jit(solution)/shard_map/all_to_all | solution.py:46
  62.0 21.7 %collective-permute-start.9 = (bf16[4,128,1024]{2,1,0:T(8,128)(2,1)S(1)}, bf16[4,128,1024]{2,1,0:T(8,128)(2,1)}, u32[]{:S(2)}, u32[]{:S(2)}) collective-permute-start(bf16[4,128,1024]{2,1,0:T(8,128)(2,1)S(1)} %pad_maximum_fusion.rest_0_), channel_id=1, source_target_pairs={{0,16},{16,0},{32,48},{48,32},{64,80},{80,64},{96,112},{112,96},{1... | collective-permute-start | bytes 3145736 | tf_op jit(solution)/shard_map/ppermute | solution.py:41
  74.0 1.2 %copy-start.1 = (bf16[8,128,128]{2,1,0:T(8,128)(2,1)}, bf16[8,128,128]{2,1,0:T(8,128)(2,1)S(1)}, u32[]{:S(2)}) copy-start(bf16[8,128,128]{2,1,0:T(8,128)(2,1)S(1)} %all-to-all-done.1.arrived) | copy-start | bytes 786436
  74.0 9.7 %collective-permute-start.10 = (bf16[4,128,1024]{2,1,0:T(8,128)(2,1)S(1)}, bf16[4,128,1024]{2,1,0:T(8,128)(2,1)}, u32[]{:S(2)}, u32[]{:S(2)}) collective-permute-start(bf16[4,128,1024]{2,1,0:T(8,128)(2,1)S(1)} %collective-permute-done.5.rest_1_), channel_id=1, source_target_pairs={{0,16},{16,0},{32,48},{48,32},{64,80},{80,64},{96,112},{112,96},{1... | collective-permute-start | bytes 3145736 | tf_op jit(solution)/shard_map/ppermute | solution.py:41
  74.7 9.0 %collective-permute-start.11 = (bf16[4,128,1024]{2,1,0:T(8,128)(2,1)S(1)}, bf16[4,128,1024]{2,1,0:T(8,128)(2,1)}, u32[]{:S(2)}, u32[]{:S(2)}) collective-permute-start(bf16[4,128,1024]{2,1,0:T(8,128)(2,1)S(1)} %collective-permute-done.6.rest_2_), channel_id=1, source_target_pairs={{0,16},{16,0},{32,48},{48,32},{64,80},{80,64},{96,112},{112,96},{1... | collective-permute-start | bytes 3145736 | tf_op jit(solution)/shard_map/ppermute | solution.py:41
  74.7 9.0 %collective-permute-start.12 = (bf16[4,128,1024]{2,1,0:T(8,128)(2,1)}, bf16[4,128,1024]{2,1,0:T(8,128)(2,1)}, u32[]{:S(2)}, u32[]{:S(2)}) collective-permute-start(bf16[4,128,1024]{2,1,0:T(8,128)(2,1)} %collective-permute-done.7.rest_3_), channel_id=1, source_target_pairs={{0,16},{16,0},{32,48},{48,32},{64,80},{80,64},{96,112},{112,96},{1... | collective-permute-start | bytes 3145736 | tf_op jit(solution)/shard_map/ppermute | solution.py:41
  78.9 1.8 %collective-permute-start.8 = (bf16[8,128,128]{2,1,0:T(8,128)(2,1)}, bf16[8,128,128]{2,1,0:T(8,128)(2,1)S(1)}, u32[]{:S(2)}, u32[]{:S(2)}) collective-permute-start(bf16[8,128,128]{2,1,0:T(8,128)(2,1)} %get-tuple-element.57), channel_id=1, source_target_pairs={{0,16},{16,0},{32,48},{48,32},{64,80},{80,64},{96,112},{112,96},{1... | collective-permute-start | bytes 786440 | tf_op jit(solution)/shard_map/ppermute | solution.py:41
  80.8 1.0 %copy-start = (bf16[8,128,128]{2,1,0:T(8,128)(2,1)S(1)}, bf16[8,128,128]{2,1,0:T(8,128)(2,1)}, u32[]{:S(2)}) copy-start(bf16[8,128,128]{2,1,0:T(8,128)(2,1)} %get-tuple-element.56.mine) | copy-start | bytes 786436

commit v3 on v2

--- a/solution.py
+++ b/solution.py
@@ -24,6 +24,7 @@
 ROW = RAW + HEADS * DV
 TALL = C + 16
 TERMS_MIB = 60
+WHOLE = 2 * DK + 16
 SIDE = 4
 F32 = jnp.float32
 BF16 = jnp.bfloat16
@@ -242,9 +243,8 @@
     start = jnp.exp(sums)
     starts[...] = start
     end = jnp.exp(sums[:, C - 1 : C] - sums)
-    units = BLOCKS * HEADS
     columns[...] = jnp.concatenate(
-        [sums, strength, start, end, strength * start, jnp.zeros((C - 5 * units, C), F32)], 0
+        [sums, strength, start, end, strength * start, jnp.zeros((C - 5 * BLOCKS * HEADS, C), F32)], 0
     ).T
 
     leave(0)
@@ -261,8 +261,9 @@
     for one in loads[:3]:
         one.wait()
     assemble(core, staged, halo, raw, QK, RAW - QK)
+    units = range(BLOCKS * HEADS)
+    lowers, inverses = [], []
     for j in range(BLOCKS):
-        lowers, inverses = [], []
         for g in range(KEYS):
             keys = convolved(raw, taps, g * DK, 2 * QK + core * QK + g * DK, j)
             keys = keys * over_length(keys)
@@ -270,8 +271,8 @@
             keys_out[j * KEYS + g, :, :DK] = kh
             keys_out[j * KEYS + g, :, DK:] = kl
             kh_t, kl_t = split(keys.T)
-            keys_t[g, :, :C] = kh_t
-            keys_t[g, :, C:] = kl_t
+            keys_t[j * KEYS + g, :, :C] = kh_t
+            keys_t[j * KEYS + g, :, C:] = kl_t
             gram = dot_t(kh, kh)
             for h in (2 * g, 2 * g + 1):
                 u = unit_of(j, h)
@@ -281,48 +282,48 @@
                 lowers.append(lower.astype(BF16))
                 inverses.append(eye - jnp.where(near, lower, 0.0).astype(BF16))
                 values = convolved(raw, taps, QK + h * DV, 4 * QK + core * HEADS * DV + h * DV, j)
-                rights[h, :, :DV] = column(columns, 1, u) * values
-                rights[h, :, DV:] = column(columns, 4, u) * keys
+                rights[u, :, :DV] = column(columns, 1, u) * values
+                rights[u, :, DV:] = column(columns, 4, u) * keys
         leave(2, j * HEADS, HEADS)
         leave(3, j * KEYS, KEYS)
-        for k in range(6):
-            halves = [dot(lowers[h] * joins[k], inverses[h]).astype(BF16) for h in range(HEADS)]
-            inverses = [inverses[h] - dot(inverses[h], halves[h]).astype(BF16) for h in range(HEADS)]
-        for h in range(HEADS):
-            u = unit_of(j, h)
-            solved = rights[h] + dot(inverses[h] - eye, rights[h].astype(BF16))
-            values, writes = solved[:, :DV], solved[:, DV:]
-            high, low = split(values)
-            solved_out[u, :, :DV] = high
-            solved_out[u, :, DV : 2 * DV] = low
-            high, low = split(writes)
-            solved_out[u, :, 2 * DV : 2 * DV + DK] = high
-            solved_out[u, :, 2 * DV + DK :] = low
-            leave(4, u, 1)
-            kt = keys_t[h // 2, :, :C], keys_t[h // 2, :, C:]
-            moved = dot3(kt, split(column(columns, 3, u) * writes))
-            add = dot3(kt, split(column(columns, 3, u) * values))
-            last = start[u : u + 1, C - 1 : C]
-            if j == 0:
-                transit[h] = moved
-                early_transit[h] = moved.astype(BF16)
-                add_high, add_low = split(add)
-                early_add[h, :, :DV] = add_high
-                early_add[h, :, DV:] = add_low
-            else:
-                first = start[unit_of(0, h) : unit_of(0, h) + 1, C - 1 : C]
-                second = moved.astype(BF16)
-                crossed = dot(second, jnp.concatenate([early_transit[h], early_add[h, :, :DV]], 1))
-                earlier = early_add[h, :, :DV].astype(F32) + early_add[h, :, DV:].astype(F32)
-                message[h, 0:C, :DK] = (last * transit[h] + first * moved - crossed[:, :DK]).astype(BF16)
-                message[h, 0:C, DK:] = (last * earlier - crossed[:, DK:] + add).astype(BF16)
-                both = jnp.broadcast_to(first * last, (1, DK))
-                top = both.astype(BF16).astype(F32)
-                middle = (both - top).astype(BF16).astype(F32)
-                parts = jnp.concatenate([top, middle, both - top - middle, jnp.zeros((13, DK), F32)], 0)
-                message[h, C:TALL, :DK] = parts.astype(BF16)
-                message[h, C:TALL, DK:] = jnp.zeros((16, DV), BF16)
+    for k in range(6):
+        halves = [dot(lowers[u] * joins[k], inverses[u]).astype(BF16) for u in units]
+        inverses = [inverses[u] - dot(inverses[u], halves[u]).astype(BF16) for u in units]
+    for u in units:
+        j, h = u // HEADS, u % HEADS
+        solved = rights[u] + dot(inverses[u] - eye, rights[u].astype(BF16))
+        values, writes = solved[:, :DV], solved[:, DV:]
+        high, low = split(values)
+        solved_out[u, :, :DV] = high
+        solved_out[u, :, DV : 2 * DV] = low
+        high, low = split(writes)
+        solved_out[u, :, 2 * DV : 2 * DV + DK] = high
+        solved_out[u, :, 2 * DV + DK :] = low
+        leave(4, u, 1)
+        g = j * KEYS + h // 2
+        kt = keys_t[g, :, :C], keys_t[g, :, C:]
+        moved = dot3(kt, split(column(columns, 3, u) * writes))
+        add = dot3(kt, split(column(columns, 3, u) * values))
+        last = start[u : u + 1, C - 1 : C]
         if j == 0:
+            transit[h] = moved
+            early_transit[h] = moved.astype(BF16)
+            add_high, add_low = split(add)
+            early_add[h, :, :DV] = add_high
+            early_add[h, :, DV:] = add_low
+        else:
+            first = start[unit_of(0, h) : unit_of(0, h) + 1, C - 1 : C]
+            second = moved.astype(BF16)
+            crossed = dot(second, jnp.concatenate([early_transit[h], early_add[h, :, :DV]], 1))
+            earlier = early_add[h, :, :DV].astype(F32) + early_add[h, :, DV:].astype(F32)
+            message[h, 0:DK] = (last * transit[h] + first * moved - crossed[:, :DK]).astype(BF16)
+            message[h, DK : 2 * DK] = (last * earlier - crossed[:, DK:] + add).astype(BF16)
+            both = jnp.broadcast_to(first * last, (1, DK))
+            top = both.astype(BF16).astype(F32)
+            middle = (both - top).astype(BF16).astype(F32)
+            parts = jnp.concatenate([top, middle, both - top - middle, jnp.zeros((13, DK), F32)], 0)
+            message[h, 2 * DK : WHOLE] = parts.astype(BF16)
+        if u == HEADS - 1:
             leave(5)
             leave(6)
     for one in copies:
@@ -333,7 +334,7 @@
     units = BLOCKS * HEADS
     return pl.pallas_call(
         terms_kernel,
-        out_shape=[shape((HEADS, TALL, DK + DV), BF16)] + [shape(*one) for one in KEPT],
+        out_shape=[shape((HEADS, WHOLE, DV), BF16)] + [shape(*one) for one in KEPT],
         in_specs=[SMEM] * 2 + [VMEM] * 2 + [ANY] * 2 + [VMEM] * 2,
         out_specs=[VMEM] + [ANY] * len(KEPT),
         scratch_shapes=[pltpu.VMEM(*one) for one in KEPT]
@@ -344,8 +345,8 @@
             pltpu.VMEM((units, C), F32),
             pltpu.VMEM((units, C), F32),
             pltpu.VMEM((6, C, C), BF16),
-            pltpu.VMEM((KEYS, DK, 2 * C), BF16),
-            pltpu.VMEM((HEADS, C, DV + DK), F32),
+            pltpu.VMEM((BLOCKS * KEYS, DK, 2 * C), BF16),
+            pltpu.VMEM((units, C, DV + DK), F32),
             pltpu.VMEM((HEADS, DK, DK), F32),
             pltpu.SemaphoreType.DMA((4,)),
             pltpu.SemaphoreType.DMA((24,)),
@@ -447,9 +448,9 @@
         entering[chip] = high
         if chip < CHIPS - 1:
             copies[chip].wait()
-            parts = messages[chip, C:TALL, :DK].astype(F32)
+            parts = messages[chip, 2 * DK : WHOLE].astype(F32)
             factor = parts[0:1] + parts[1:2] + parts[2:3]
-            state = factor * state - dot(messages[chip, 0:C, :DK], high) + messages[chip, 0:C, DK:].astype(F32)
+            state = factor * state - dot(messages[chip, 0:DK], high) + messages[chip, DK : 2 * DK].astype(F32)
 
 
 def run_enter(messages):
@@ -458,7 +459,7 @@
         out_shape=shape((CHIPS, DK, DV), BF16),
         in_specs=[ANY],
         out_specs=VMEM,
-        scratch_shapes=[pltpu.VMEM((CHIPS, TALL, DK + DV), BF16), pltpu.SemaphoreType.DMA((CHIPS - 1,))],
+        scratch_shapes=[pltpu.VMEM((CHIPS, WHOLE, DV), BF16), pltpu.SemaphoreType.DMA((CHIPS - 1,))],
         compiler_params=params(TERMS_MIB),
         cost_estimate=cost(10**9, 2**20),
         name="enter",
@@ -528,44 +529,36 @@
     return total.astype(BF16)
 
 
-def first_kernel(mine, theirs, *rest):
-    weights, (normed, out, ordered) = rest[:SIDE], rest[SIDE:]
+def project_kernel(mine, theirs, *rest):
+    own, others, (out, normed, ordered, sems) = rest[:SIDE], rest[SIDE : 2 * SIDE], rest[2 * SIDE :]
     core = my_core()
-    for source, its_core in ((mine, core), (theirs, 1 - core)):
-        normed[pl.ds(its_core * HEADS, HEADS)] = source[...]
-    in_order_of(core, normed, ordered)
-    out[...] = product_of(ordered, weights)
-
-
-def second_kernel(normed, first, *rest):
-    weights, (out, ordered) = rest[:SIDE], rest[SIDE:]
-    core = my_core()
-    in_order_of(1 - core, normed, ordered)
-    out[:, pl.ds(pl.multiple_of(core * HALF, HALF), HALF)] = first[...]
-    out[:, pl.ds(pl.multiple_of((1 - core) * HALF, HALF), HALF)] = product_of(ordered, weights)
+    loads = []
+    for i, (source, its_core) in enumerate(((mine, core), (theirs, 1 - core))):
+        target = normed.at[pl.ds(pl.multiple_of(its_core * HEADS, HEADS), HEADS)]
+        loads.append(pltpu.make_async_copy(source, target, sems.at[i]))
+        loads[-1].start()
+    for one in loads:
+        one.wait()
+    for its_core, weights in ((core, own), (1 - core, others)):
+        in_order_of(its_core, normed, ordered)
+        out[:, pl.ds(pl.multiple_of(its_core * HALF, HALF), HALF)] = product_of(ordered, weights)
 
 
 def project(mine, theirs, weights, other_weights):
-    settings = dict(
-        in_specs=[VMEM] * (2 + SIDE),
+    return pl.pallas_call(
+        project_kernel,
+        out_shape=shape((C, WIDTH), BF16),
+        in_specs=[ANY] * 2 + [VMEM] * 2 * SIDE,
+        out_specs=VMEM,
         compiler_params=params(40),
-        cost_estimate=cost(C * WIDTH * WIDTH, 2**22),
-        scratch_shapes=[pltpu.VMEM((C, WIDTH), BF16)],
-    )
-    normed, first = pl.pallas_call(
-        first_kernel,
-        out_shape=[shape((VH, C, DV), BF16), shape((C, HALF), BF16)],
-        out_specs=[VMEM] * 2,
-        name="project_first",
-        **settings,
-    )(mine, theirs, *weights)
-    return pl.pallas_call(
-        second_kernel,
-        out_shape=shape((C, WIDTH), BF16),
-        out_specs=VMEM,
-        name="project_second",
-        **settings,
-    )(normed, first, *other_weights)
+        cost_estimate=cost(2 * C * WIDTH * WIDTH, 2**23),
+        scratch_shapes=[
+            pltpu.VMEM((VH, C, DV), BF16),
+            pltpu.VMEM((C, WIDTH), BF16),
+            pltpu.SemaphoreType.DMA((2,)),
+        ],
+        name="project",
+    )(mine, theirs, *weights, *other_weights)
 
 
 def along(block, distance, second):

time: 88.1 us -> 85.1 us (0.966)
  Pallas kernels: 34.9 us -> 32.6 us
    pallas_call x3 -> x2, Pallas kernels: 18.3 us -> 15.9 us  [the longest x1 11.2 us: run_terms(): pl.pallas_call(terms_kernel, out_shape=[shape((HEADS, WHOLE, DV), BF16)]...]
    all_to_all x2, waiting for transfers between devices: 16.5 us -> 15.1 us  [between_chips(): return lax.all_to_all(blocks, 'seq', 0, 0, axis_index_groups=groups)]
  transfers between devices with their start and end apart: 15 -> 15, of which waited for: 5 -> 5; matrix products, arithmetic and copies ran while one was open for 0% -> 0% of each run, Pallas kernels for 33% -> 30%
where the time goes in v3:
time: 85.1 us; the launch traced here: 84.5 us
  Pallas kernels  32.6 us (38%)
  starting transfers between devices  28 us (33%)
  waiting for transfers between devices  21.1 us (25%)
  local copies, waits for them, and re-layouts  1.57 us (2%)
  other arithmetic  1.03 us (1%)
    all_to_all x2, waiting for transfers between devices, between_chips(): return lax.all_to_all(blocks, 'seq', 0, 0, axis_index_groups=groups)  15.1 us
    pallas_call x1, Pallas kernels, run_terms(): pl.pallas_call(terms_kernel, out_shape=[shape((HEADS, WHOLE, DV), BF16)]...  11.2 us
    all_to_all x2, starting transfers between devices, between_chips(): return lax.all_to_all(blocks, 'seq', 0, 0, axis_index_groups=groups)  10.7 us
    ppermute x6, starting transfers between devices, along(): return lax.ppermute(block, ('seq', 'fsdp'), route)  9.96 us
    pallas_call x1, Pallas kernels, run_reads(): pl.pallas_call(reads_kernel, out_shape=[shape((units, C, DV), F32), shape...  7.88 us
    ppermute x6, starting transfers between devices, other_core(): return lax.ppermute(block, 'seq', [(i, i ^ 1) for i in range(SEGMENTS)])  5.46 us
    pallas_call x1, Pallas kernels, project(): pl.pallas_call(project_kernel, out_shape=shape((C, WIDTH), BF16), in_spec...  4.67 us
    ppermute x6, waiting for transfers between devices, other_core(): return lax.ppermute(block, 'seq', [(i, i ^ 1) for i in range(SEGMENTS)])  3.83 us
  transfers between devices with their start and end apart: 15, of which 5 were waited for; matrix products, arithmetic and copies ran while one was open for 0% of the time, Pallas kernels for 30%

profile of v3, /device:TPU:1, one launch (start us, length us, event | category | flops | bytes accessed | tf_op | source)
XLA Modules:
  0.0 84.5 jit_solution(18147530574663802925)
XLA Ops:
  0.0 2.4 %cut.1 = (bf16[144,3072]{1,0:T(8,128)(2,1)}, bf16[16,2048]{1,0:T(8,128)(2,1)}, bf16[128,1024]{1,0:T(8,128)(2,1)}) custom-call(bf16[128,4096]{1,0:T(8,128)(2,1)} %bitcast.10, bf16[128,2048]{1,0:T(8,128)(2,1)} %bitcast.13, s32[16,128]{1,0:T(8,128)} %bitcast.19, s32[16,128]{1,0:T(8,128)} %bitcast.21, bf16[128,2048]{1,0:T(8,128)(2,1)} %weight.1), custom_call_target="tpu_custom_call" | custom-call | tf_op jit(solution)/shard_map/cut/pallas_call | solution.py:137
  2.4 3.3 %collective-permute-start = (bf16[144,3072]{1,0:T(8,128)(2,1)}, bf16[144,3072]{1,0:T(8,128)(2,1)S(1)}, u32[]{:S(2)}, u32[]{:S(2)}) collective-permute-start(bf16[144,3072]{1,0:T(8,128)(2,1)} %get-tuple-element.32), channel_id=1, source_target_pairs={{0,16},{16,0},{32,48},{48,32},{64,80},{80,64},{96,112},{112,96},{1... | collective-permute-start | bytes 2654216 | tf_op jit(solution)/shard_map/ppermute | solution.py:42
  5.8 2.3 %collective-permute-done.got = bf16[144,3072]{1,0:T(8,128)(2,1)S(1)} collective-permute-done((bf16[144,3072]{1,0:T(8,128)(2,1)}, bf16[144,3072]{1,0:T(8,128)(2,1)S(1)}, u32[]{:S(2)}, u32[]{:S(2)}) %collective-permute-start) | collective-permute-done | bytes 884768 | tf_op jit(solution)/shard_map/ppermute | solution.py:42
  8.0 0.0 copy-start.3
  8.0 0.9 %slice_select_fusion = bf16[16,2048]{1,0:T(8,128)(2,1)S(1)} fusion(bf16[16,2048]{1,0:T(8,128)(2,1)} %get-tuple-element.33, bf16[144,3072]{1,0:T(8,128)(2,1)S(1)} %collective-permute-done.got, pred[]{:T(512)S(6)} %eq.5), kind=kLoop, calls=%fused_computation.1 | loop fusion | flops 32768 | bytes 196609 | tf_op jit(solution)/shard_map/jit(_where)/select_n | solution.py:590
  8.9 1.8 %collective-permute-start.1 = (bf16[16,2048]{1,0:T(8,128)(2,1)S(1)}, bf16[16,2048]{1,0:T(8,128)(2,1)S(1)}, u32[]{:S(2)}, u32[]{:S(2)}) collective-permute-start(bf16[16,2048]{1,0:T(8,128)(2,1)S(1)} %slice_select_fusion), channel_id=1, source_target_pairs={{0,32},{16,48},{32,64},{48,80},{64,96},{80,112},{96,128},{112,144}... | collective-permute-start | bytes 196616 | tf_op jit(solution)/shard_map/ppermute | solution.py:591
  10.7 0.0 copy-start.2
  10.8 1.4 %collective-permute-start.2 = (bf16[128,1024]{1,0:T(8,128)(2,1)}, bf16[128,1024]{1,0:T(8,128)(2,1)S(1)}, u32[]{:S(2)}, u32[]{:S(2)}) collective-permute-start(bf16[128,1024]{1,0:T(8,128)(2,1)} %get-tuple-element.47), channel_id=1, source_target_pairs={{0,1},{1,2},{2,3},{3,0},{4,5},{5,6},{6,7},{7,4},{8,9},{9,10},{10,1... | collective-permute-start | bytes 786440 | tf_op jit(solution)/shard_map/ppermute | solution.py:572
  12.1 2.6 %collective-permute-start.3 = (bf16[128,1024]{1,0:T(8,128)(2,1)}, bf16[128,1024]{1,0:T(8,128)(2,1)S(1)}, u32[]{:S(2)}, u32[]{:S(2)}) collective-permute-start(bf16[128,1024]{1,0:T(8,128)(2,1)} %get-tuple-element.47), channel_id=1, source_target_pairs={{0,2},{1,3},{2,0},{3,1},{4,6},{5,7},{6,4},{7,5},{8,10},{9,11},{10,... | collective-permute-start | bytes 786440 | tf_op jit(solution)/shard_map/ppermute | solution.py:572
  14.8 1.1 %collective-permute-start.4 = (bf16[128,1024]{1,0:T(8,128)(2,1)}, bf16[128,1024]{1,0:T(8,128)(2,1)S(1)}, u32[]{:S(2)}, u32[]{:S(2)}) collective-permute-start(bf16[128,1024]{1,0:T(8,128)(2,1)} %get-tuple-element.47), channel_id=1, source_target_pairs={{0,3},{1,0},{2,1},{3,2},{4,7},{5,4},{6,5},{7,6},{8,11},{9,8},{10,9... | collective-permute-start | bytes 786440 | tf_op jit(solution)/shard_map/ppermute | solution.py:572
  15.8 0.0 collective-permute-done.1.halo
  15.8 0.0 copy-done.3
  15.8 0.0 copy-start.4
  15.8 0.6 copy-done.4
  16.4 11.2 %terms.1 = (bf16[8,272,128]{2,1,0:T(8,128)(2,1)}, f32[128,128]{1,0:T(8,128)}, f32[16,128]{1,0:T(8,128)}, f32[16,128,128]{2,1,0:T(8,128)}, bf16[8,128,256]{2,1,0:...) custom-call(f32[16]{0:T(128)} %scale_log.1, f32[16]{0:T(128)} %bias.1, ...), custom_call_target="tpu_custom_call" | custom-call | flops 8000000000 | bytes 33554432 | tf_op jit(solution)/shard_map/terms/pallas_call | solution.py:335
  27.7 0.0 collective-permute-done.2
  27.7 0.0 collective-permute-done.3
  27.7 0.0 collective-permute-done.4
  27.7 7.3 %all-to-all-start = ((bf16[8,272,128]{2,1,0:T(8,128)(2,1)}), bf16[8,272,128]{2,1,0:T(8,128)(2,1)}, u32[]{:S(2)}, u32[]{:S(2)}) async-start(bf16[8,272,128]{2,1,0:T(8,128)(2,1)} %get-tuple-element.36), calls=%async_computation | async-start | bytes 1114112 | tf_op jit(solution)/shard_map/all_to_all | solution.py:47
  35.0 0.0 copy-done.2
  35.0 0.1 pad_maximum_fusion.rest_0_
  35.2 1.3 %collective-permute-start.5 = (bf16[4,128,1024]{2,1,0:T(8,128)(2,1)S(1)}, bf16[4,128,1024]{2,1,0:T(8,128)(2,1)S(1)}, u32[]{:S(2)}, u32[]{:S(2)}) collective-permute-start(bf16[4,128,1024]{2,1,0:T(8,128)(2,1)S(1)} %pad_maximum_fusion.rest_0_), channel_id=1, source_target_pairs={{0,4},{1,5},{2,6},{3,7},{4,8},{5,9},{6,10},{7,11},{8,12},{9,13},{1... | collective-permute-start | bytes 3145736 | tf_op jit(solution)/shard_map/ppermute | solution.py:572
  36.5 2.5 %collective-permute-start.6 = (bf16[4,128,1024]{2,1,0:T(8,128)(2,1)S(1)}, bf16[4,128,1024]{2,1,0:T(8,128)(2,1)S(1)}, u32[]{:S(2)}, u32[]{:S(2)}) collective-permute-start(bf16[4,128,1024]{2,1,0:T(8,128)(2,1)S(1)} %pad_maximum_fusion.rest_0_), channel_id=1, source_target_pairs={{0,8},{1,9},{2,10},{3,11},{4,12},{5,13},{6,14},{7,15},{8,0},{9,1},... | collective-permute-start | bytes 3145736 | tf_op jit(solution)/shard_map/ppermute | solution.py:572
  38.9 1.2 %collective-permute-start.7 = (bf16[4,128,1024]{2,1,0:T(8,128)(2,1)S(1)}, bf16[4,128,1024]{2,1,0:T(8,128)(2,1)}, u32[]{:S(2)}, u32[]{:S(2)}) collective-permute-start(bf16[4,128,1024]{2,1,0:T(8,128)(2,1)S(1)} %pad_maximum_fusion.rest_0_), channel_id=1, source_target_pairs={{0,12},{1,13},{2,14},{3,15},{4,0},{5,1},{6,2},{7,3},{8,4},{9,5},{1... | collective-permute-start | bytes 3145736 | tf_op jit(solution)/shard_map/ppermute | solution.py:572
  40.1 7.9 %reads.1 = (f32[16,128,128]{2,1,0:T(8,128)}, bf16[16,128,256]{2,1,0:T(8,128)(2,1)}) custom-call(bf16[128,4096]{1,0:T(8,128)(2,1)} %bitcast.12, bf16[144,3072]{1,0:T(8,128)(2,1)} %copy-done.3, bf16[16,2048]{1,0:T(8,128)(2,1)} %copy-done.4, f32[4,4096]{1,0:T(4,128)} %taps.3, f32[128,128]{1,0:T(8,128)} %get-tuple-element.37.rest_0_, ...), custom_call_target="tpu_custom_call" | custom-call | flops 4000000000 | bytes 16777216 | tf_op jit(solution)/shard_map/reads/pallas_call | solution.py:420
  48.0 5.8 %all-to-all-done.arrived = bf16[8,272,128]{2,1,0:T(8,128)(2,1)} async-done(((bf16[8,272,128]{2,1,0:T(8,128)(2,1)}), bf16[8,272,128]{2,1,0:T(8,128)(2,1)}, u32[]{:S(2)}, u32[]{:S(2)}) %all-to-all-start) | async-done | bytes 557088 | tf_op jit(solution)/shard_map/all_to_all | solution.py:47
  53.8 2.7 %enter.1 = bf16[8,128,128]{2,1,0:T(8,128)(2,1)} custom-call(bf16[8,272,128]{2,1,0:T(8,128)(2,1)} %all-to-all-done.arrived), custom_call_target="tpu_custom_call" | custom-call | flops 1000000000 | bytes 1048576 | tf_op jit(solution)/shard_map/enter/pallas_call | solution.py:457
  56.5 3.4 %all-to-all-start.1 = ((bf16[8,128,128]{2,1,0:T(8,128)(2,1)}), bf16[8,128,128]{2,1,0:T(8,128)(2,1)S(1)}, u32[]{:S(2)}, u32[]{:S(2)}) async-start(bf16[8,128,128]{2,1,0:T(8,128)(2,1)} %enter.1), calls=%async_computation.1 | async-start | bytes 524288 | tf_op jit(solution)/shard_map/all_to_all | solution.py:47
  59.9 0.6 collective-permute-start.9
  60.5 0.0 collective-permute-done.5.rest_1_
  60.5 2.1 %collective-permute-done.6.rest_2_ = bf16[4,128,1024]{2,1,0:T(8,128)(2,1)S(1)} collective-permute-done((bf16[4,128,1024]{2,1,0:T(8,128)(2,1)S(1)}, bf16[4,128,1024]{2,1,0:T(8,128)(2,1)S(1)}, u32[]{:S(2)}, u32[]{:S(2)}) %collective-permute-start.6) | collective-permute-done | bytes 1048608 | tf_op jit(solution)/shard_map/ppermute | solution.py:572
  62.6 0.0 collective-permute-done.7.rest_3_
  62.6 9.2 %all-to-all-done.1.arrived = bf16[8,128,128]{2,1,0:T(8,128)(2,1)S(1)} async-done(((bf16[8,128,128]{2,1,0:T(8,128)(2,1)}), bf16[8,128,128]{2,1,0:T(8,128)(2,1)S(1)}, u32[]{:S(2)}, u32[]{:S(2)}) %all-to-all-start.1) | async-done | bytes 262176 | tf_op jit(solution)/shard_map/all_to_all | solution.py:47
  71.9 0.0 copy-start.1
  71.9 0.8 collective-permute-start.10
  72.6 0.0 collective-permute-start.11
  72.6 0.5 collective-permute-start.12
  73.2 0.0 copy-done.1
  73.2 3.7 %finish.1 = (bf16[8,128,128]{2,1,0:T(8,128)(2,1)}, bf16[8,128,128]{2,1,0:T(8,128)(2,1)}) custom-call(bf16[8,128,128]{2,1,0:T(8,128)(2,1)} %copy-done.1, f32[16,128,128]{2,1,0:T(8,128)} %get-tuple-element.52.base, bf16[16,128,256]{2,1,0:T(8,128)(2,1)} %get-tuple-element.53.reads, bf16[128,2048]{1,0:T(8,128)(2,1)} %bitcast.14, bf16[144,3072]{1,0:T(8,128)(2,1)} %copy-done.3, ...), custom_call_target="tpu_custom_call" | custom-call | flops 2000000000 | bytes 4194304 | tf_op jit(solution)/shard_map/finish/pallas_call | solution.py:493
  76.8 0.3 collective-permute-start.8
  77.1 0.0 collective-permute-done.9.rest_4_
  77.1 1.6 %collective-permute-done.8.theirs = bf16[8,128,128]{2,1,0:T(8,128)(2,1)S(1)} collective-permute-done((bf16[8,128,128]{2,1,0:T(8,128)(2,1)}, bf16[8,128,128]{2,1,0:T(8,128)(2,1)S(1)}, u32[]{:S(2)}, u32[]{:S(2)}) %collective-permute-start.8) | collective-permute-done | bytes 262176 | tf_op jit(solution)/shard_map/ppermute | solution.py:42
  78.7 0.0 collective-permute-done.10.rest_5_
  78.7 0.0 collective-permute-done.11.rest_6_
  78.7 0.0 collective-permute-done.12.rest_7_
  78.7 0.0 copy-start
  78.7 0.9 %copy-done = bf16[8,128,128]{2,1,0:T(8,128)(2,1)S(1)} copy-done((bf16[8,128,128]{2,1,0:T(8,128)(2,1)S(1)}, bf16[8,128,128]{2,1,0:T(8,128)(2,1)}, u32[]{:S(2)}) %copy-start) | copy-done | bytes 262168
  79.6 4.7 %project.1 = bf16[128,2048]{1,0:T(8,128)(2,1)} custom-call(bf16[8,128,128]{2,1,0:T(8,128)(2,1)S(1)} %copy-done, bf16[8,128,128]{2,1,0:T(8,128)(2,1)S(1)} %collective-permute-done.8.theirs, bf16[4,128,1024]{2,1,0:T(8,128)(2,1)S(1)} %pad_maximum_fusion.rest_0_, bf16[4,128,1024]{2,1,0:T(8,128)(2,1)S(1)} %collective-permute-done.5.rest_1_, ...), custom_call_target="tpu_custom_call" | custom-call | flops 1073741824 | bytes 8388608 | tf_op jit(solution)/shard_map/project/pallas_call | solution.py:548
Async XLA Ops:
  2.4 5.6 %collective-permute-start = (bf16[144,3072]{1,0:T(8,128)(2,1)}, bf16[144,3072]{1,0:T(8,128)(2,1)S(1)}, u32[]{:S(2)}, u32[]{:S(2)}) collective-permute-start(bf16[144,3072]{1,0:T(8,128)(2,1)} %get-tuple-element.32), channel_id=1, source_target_pairs={{0,16},{16,0},{32,48},{48,32},{64,80},{80,64},{96,112},{112,96},{1... | collective-permute-start | bytes 2654216 | tf_op jit(solution)/shard_map/ppermute | solution.py:42
  8.0 7.8 %copy-start.3 = (bf16[144,3072]{1,0:T(8,128)(2,1)}, bf16[144,3072]{1,0:T(8,128)(2,1)S(1)}, u32[]{:S(2)}) copy-start(bf16[144,3072]{1,0:T(8,128)(2,1)S(1)} %collective-permute-done.got) | copy-start | bytes 2654212
  8.9 6.9 %collective-permute-start.1 = (bf16[16,2048]{1,0:T(8,128)(2,1)S(1)}, bf16[16,2048]{1,0:T(8,128)(2,1)S(1)}, u32[]{:S(2)}, u32[]{:S(2)}) collective-permute-start(bf16[16,2048]{1,0:T(8,128)(2,1)S(1)} %slice_select_fusion), channel_id=1, source_target_pairs={{0,32},{16,48},{32,64},{48,80},{64,96},{80,112},{96,128},{112,144}... | collective-permute-start | bytes 196616 | tf_op jit(solution)/shard_map/ppermute | solution.py:591
  10.7 24.3 %copy-start.2 = (bf16[128,1024]{1,0:T(8,128)(2,1)S(1)}, bf16[128,1024]{1,0:T(8,128)(2,1)}, u32[]{:S(2)}) copy-start(bf16[128,1024]{1,0:T(8,128)(2,1)} %get-tuple-element.47) | copy-start | bytes 786436
  10.8 16.9 %collective-permute-start.2 = (bf16[128,1024]{1,0:T(8,128)(2,1)}, bf16[128,1024]{1,0:T(8,128)(2,1)S(1)}, u32[]{:S(2)}, u32[]{:S(2)}) collective-permute-start(bf16[128,1024]{1,0:T(8,128)(2,1)} %get-tuple-element.47), channel_id=1, source_target_pairs={{0,1},{1,2},{2,3},{3,0},{4,5},{5,6},{6,7},{7,4},{8,9},{9,10},{10,1... | collective-permute-start | bytes 786440 | tf_op jit(solution)/shard_map/ppermute | solution.py:572
  12.1 15.6 %collective-permute-start.3 = (bf16[128,1024]{1,0:T(8,128)(2,1)}, bf16[128,1024]{1,0:T(8,128)(2,1)S(1)}, u32[]{:S(2)}, u32[]{:S(2)}) collective-permute-start(bf16[128,1024]{1,0:T(8,128)(2,1)} %get-tuple-element.47), channel_id=1, source_target_pairs={{0,2},{1,3},{2,0},{3,1},{4,6},{5,7},{6,4},{7,5},{8,10},{9,11},{10,... | collective-permute-start | bytes 786440 | tf_op jit(solution)/shard_map/ppermute | solution.py:572
  14.8 13.0 %collective-permute-start.4 = (bf16[128,1024]{1,0:T(8,128)(2,1)}, bf16[128,1024]{1,0:T(8,128)(2,1)S(1)}, u32[]{:S(2)}, u32[]{:S(2)}) collective-permute-start(bf16[128,1024]{1,0:T(8,128)(2,1)} %get-tuple-element.47), channel_id=1, source_target_pairs={{0,3},{1,0},{2,1},{3,2},{4,7},{5,4},{6,5},{7,6},{8,11},{9,8},{10,9... | collective-permute-start | bytes 786440 | tf_op jit(solution)/shard_map/ppermute | solution.py:572
  15.8 0.6 copy-start.4
  27.7 26.1 %all-to-all-start = ((bf16[8,272,128]{2,1,0:T(8,128)(2,1)}), bf16[8,272,128]{2,1,0:T(8,128)(2,1)}, u32[]{:S(2)}, u32[]{:S(2)}) async-start(bf16[8,272,128]{2,1,0:T(8,128)(2,1)} %get-tuple-element.36), calls=%async_computation | async-start | bytes 1114112 | tf_op jit(solution)/shard_map/all_to_all | solution.py:47
  35.2 25.3 %collective-permute-start.5 = (bf16[4,128,1024]{2,1,0:T(8,128)(2,1)S(1)}, bf16[4,128,1024]{2,1,0:T(8,128)(2,1)S(1)}, u32[]{:S(2)}, u32[]{:S(2)}) collective-permute-start(bf16[4,128,1024]{2,1,0:T(8,128)(2,1)S(1)} %pad_maximum_fusion.rest_0_), channel_id=1, source_target_pairs={{0,4},{1,5},{2,6},{3,7},{4,8},{5,9},{6,10},{7,11},{8,12},{9,13},{1... | collective-permute-start | bytes 3145736 | tf_op jit(solution)/shard_map/ppermute | solution.py:572
  36.5 26.2 %collective-permute-start.6 = (bf16[4,128,1024]{2,1,0:T(8,128)(2,1)S(1)}, bf16[4,128,1024]{2,1,0:T(8,128)(2,1)S(1)}, u32[]{:S(2)}, u32[]{:S(2)}) collective-permute-start(bf16[4,128,1024]{2,1,0:T(8,128)(2,1)S(1)} %pad_maximum_fusion.rest_0_), channel_id=1, source_target_pairs={{0,8},{1,9},{2,10},{3,11},{4,12},{5,13},{6,14},{7,15},{8,0},{9,1},... | collective-permute-start | bytes 3145736 | tf_op jit(solution)/shard_map/ppermute | solution.py:572
  38.9 23.7 %collective-permute-start.7 = (bf16[4,128,1024]{2,1,0:T(8,128)(2,1)S(1)}, bf16[4,128,1024]{2,1,0:T(8,128)(2,1)}, u32[]{:S(2)}, u32[]{:S(2)}) collective-permute-start(bf16[4,128,1024]{2,1,0:T(8,128)(2,1)S(1)} %pad_maximum_fusion.rest_0_), channel_id=1, source_target_pairs={{0,12},{1,13},{2,14},{3,15},{4,0},{5,1},{6,2},{7,3},{8,4},{9,5},{1... | collective-permute-start | bytes 3145736 | tf_op jit(solution)/shard_map/ppermute | solution.py:572
  56.5 15.4 %all-to-all-start.1 = ((bf16[8,128,128]{2,1,0:T(8,128)(2,1)}), bf16[8,128,128]{2,1,0:T(8,128)(2,1)S(1)}, u32[]{:S(2)}, u32[]{:S(2)}) async-start(bf16[8,128,128]{2,1,0:T(8,128)(2,1)} %enter.1), calls=%async_computation.1 | async-start | bytes 524288 | tf_op jit(solution)/shard_map/all_to_all | solution.py:47
  59.9 17.2 %collective-permute-start.9 = (bf16[4,128,1024]{2,1,0:T(8,128)(2,1)S(1)}, bf16[4,128,1024]{2,1,0:T(8,128)(2,1)}, u32[]{:S(2)}, u32[]{:S(2)}) collective-permute-start(bf16[4,128,1024]{2,1,0:T(8,128)(2,1)S(1)} %pad_maximum_fusion.rest_0_), channel_id=1, source_target_pairs={{0,16},{16,0},{32,48},{48,32},{64,80},{80,64},{96,112},{112,96},{1... | collective-permute-start | bytes 3145736 | tf_op jit(solution)/shard_map/ppermute | solution.py:42
  71.9 1.3 %copy-start.1 = (bf16[8,128,128]{2,1,0:T(8,128)(2,1)}, bf16[8,128,128]{2,1,0:T(8,128)(2,1)S(1)}, u32[]{:S(2)}) copy-start(bf16[8,128,128]{2,1,0:T(8,128)(2,1)S(1)} %all-to-all-done.1.arrived) | copy-start | bytes 786436
  71.9 6.8 %collective-permute-start.10 = (bf16[4,128,1024]{2,1,0:T(8,128)(2,1)S(1)}, bf16[4,128,1024]{2,1,0:T(8,128)(2,1)}, u32[]{:S(2)}, u32[]{:S(2)}) collective-permute-start(bf16[4,128,1024]{2,1,0:T(8,128)(2,1)S(1)} %collective-permute-done.5.rest_1_), channel_id=1, source_target_pairs={{0,16},{16,0},{32,48},{48,32},{64,80},{80,64},{96,112},{112,96},{1... | collective-permute-start | bytes 3145736 | tf_op jit(solution)/shard_map/ppermute | solution.py:42
  72.6 6.0 %collective-permute-start.11 = (bf16[4,128,1024]{2,1,0:T(8,128)(2,1)S(1)}, bf16[4,128,1024]{2,1,0:T(8,128)(2,1)}, u32[]{:S(2)}, u32[]{:S(2)}) collective-permute-start(bf16[4,128,1024]{2,1,0:T(8,128)(2,1)S(1)} %collective-permute-done.6.rest_2_), channel_id=1, source_target_pairs={{0,16},{16,0},{32,48},{48,32},{64,80},{80,64},{96,112},{112,96},{1... | collective-permute-start | bytes 3145736 | tf_op jit(solution)/shard_map/ppermute | solution.py:42
  72.6 6.0 %collective-permute-start.12 = (bf16[4,128,1024]{2,1,0:T(8,128)(2,1)}, bf16[4,128,1024]{2,1,0:T(8,128)(2,1)}, u32[]{:S(2)}, u32[]{:S(2)}) collective-permute-start(bf16[4,128,1024]{2,1,0:T(8,128)(2,1)} %collective-permute-done.7.rest_3_), channel_id=1, source_target_pairs={{0,16},{16,0},{32,48},{48,32},{64,80},{80,64},{96,112},{112,96},{1... | collective-permute-start | bytes 3145736 | tf_op jit(solution)/shard_map/ppermute | solution.py:42
  76.8 1.8 %collective-permute-start.8 = (bf16[8,128,128]{2,1,0:T(8,128)(2,1)}, bf16[8,128,128]{2,1,0:T(8,128)(2,1)S(1)}, u32[]{:S(2)}, u32[]{:S(2)}) collective-permute-start(bf16[8,128,128]{2,1,0:T(8,128)(2,1)} %get-tuple-element.55), channel_id=1, source_target_pairs={{0,16},{16,0},{32,48},{48,32},{64,80},{80,64},{96,112},{112,96},{1... | collective-permute-start | bytes 786440 | tf_op jit(solution)/shard_map/ppermute | solution.py:42
  78.7 1.0 %copy-start = (bf16[8,128,128]{2,1,0:T(8,128)(2,1)S(1)}, bf16[8,128,128]{2,1,0:T(8,128)(2,1)}, u32[]{:S(2)}) copy-start(bf16[8,128,128]{2,1,0:T(8,128)(2,1)} %get-tuple-element.54.mine) | copy-start | bytes 786436

commit v4 on v3

--- a/solution.py
+++ b/solution.py
@@ -76,7 +76,6 @@
 KEPT = (
     ((C, C), F32),
     ((BLOCKS * HEADS, C), F32),
-    ((BLOCKS * HEADS, C, C), F32),
     ((BLOCKS * KEYS, C, 2 * DK), BF16),
     ((BLOCKS * HEADS, C, 2 * DV + 2 * DK), BF16),
     ((HEADS, DK, DK), BF16),
@@ -154,11 +153,11 @@
     )(raw, gate, decay, beta, weight)
 
 
-def assemble(core, staged, halo, raw, first, width):
-    at = slice(first, first + width)
-    raw[0:8] = halo[:, at].astype(F32)[8:16]
+def assemble(core, staged, halo, raw, first, at, width):
+    to = slice(at, at + width)
+    raw[0:8, to] = halo[:, first + at : first + at + width].astype(F32)[8:16]
     for i, block in enumerate((core, 1 - core)):
-        raw[pl.ds(pl.multiple_of(8 + block * C, 8), C)] = staged[i].astype(F32)
+        raw[pl.ds(pl.multiple_of(8 + block * C, 8), C), to] = staged[i, :, to].astype(F32)
 
 
 def convolved(raw, taps, at, channel, j):
@@ -189,17 +188,18 @@
 ):
     outs, kept, rest = rest[: len(KEPT)], rest[len(KEPT) : 2 * len(KEPT)], rest[2 * len(KEPT) :]
     raw, staged, their_codes, decay, beta, joins, keys_t, rights, transit, arrive, sems = rest
-    columns, starts, pairs, keys_out, solved_out, early_transit, early_add = kept
+    columns, totals, keys_out, solved_out, early_transit, early_add = kept
     core = my_core()
     copies = []
     column_of = pl.multiple_of(2 * QK + core * QK, QK), pl.multiple_of(4 * QK + core * HEADS * DV, HEADS * DV)
     loads = [
         pltpu.make_async_copy(*one, arrive.at[i])
         for i, one in enumerate((
+            (got.at[C:TALL, 0 : 2 * C], their_codes),
             (own.at[:, pl.ds(column_of[0], QK)], staged.at[0, :, 0:QK]),
+            (got.at[0:C, QK : 2 * QK], staged.at[1, :, 0:QK]),
             (own.at[:, pl.ds(column_of[1], HEADS * DV)], staged.at[0, :, QK:]),
-            (got.at[0:C, QK:RAW], staged.at[1]),
-            (got.at[C:TALL, 0 : 2 * C], their_codes),
+            (got.at[0:C, 2 * QK : RAW], staged.at[1, :, QK:]),
         ))
     ]
     for one in loads:
@@ -212,7 +212,7 @@
         copies.append(pltpu.make_async_copy(source, target, sems.at[len(copies)]))
         copies[-1].start()
 
-    loads[3].wait()
+    loads[0].wait()
     codes = their_codes[...].astype(F32)
     ours = pl.ds(pl.multiple_of(core * HEADS, HEADS), HEADS)
     theirs = pl.ds(pl.multiple_of((1 - core) * HEADS, HEADS), HEADS)
@@ -241,7 +241,7 @@
     )
     strength = 1.0 / (1.0 + jnp.exp(8.0 - beta[...] / 32.0))
     start = jnp.exp(sums)
-    starts[...] = start
+    totals[...] = sums
     end = jnp.exp(sums[:, C - 1 : C] - sums)
     columns[...] = jnp.concatenate(
         [sums, strength, start, end, strength * start, jnp.zeros((C - 5 * BLOCKS * HEADS, C), F32)], 0
@@ -258,9 +258,9 @@
         ).astype(F32).astype(BF16)
     near = (row_ids >> 1) == (col_ids >> 1)
 
-    for one in loads[:3]:
+    for one in loads[1:3]:
         one.wait()
-    assemble(core, staged, halo, raw, QK, RAW - QK)
+    assemble(core, staged, halo, raw, QK, 0, QK)
     units = range(BLOCKS * HEADS)
     lowers, inverses = [], []
     for j in range(BLOCKS):
@@ -277,16 +277,19 @@
             for h in (2 * g, 2 * g + 1):
                 u = unit_of(j, h)
                 pair = jnp.where(inclusive, jnp.exp(jnp.minimum(column(columns, 0, u) - sums[u : u + 1], 0.0)), 0.0)
-                pairs[u] = pair
                 lower = jnp.where(strict, column(columns, 1, u) * pair * gram, 0.0)
                 lowers.append(lower.astype(BF16))
                 inverses.append(eye - jnp.where(near, lower, 0.0).astype(BF16))
-                values = convolved(raw, taps, QK + h * DV, 4 * QK + core * HEADS * DV + h * DV, j)
-                rights[u, :, :DV] = column(columns, 1, u) * values
                 rights[u, :, DV:] = column(columns, 4, u) * keys
-        leave(2, j * HEADS, HEADS)
-        leave(3, j * KEYS, KEYS)
+        leave(2, j * KEYS, KEYS)
+    for one in loads[3:]:
+        one.wait()
+    assemble(core, staged, halo, raw, QK, QK, HEADS * DV)
     for k in range(6):
+        for u in units[3 * k : 3 * k + 3]:
+            j, h = u // HEADS, u % HEADS
+            values = convolved(raw, taps, QK + h * DV, 4 * QK + core * HEADS * DV + h * DV, j)
+            rights[u, :, :DV] = column(columns, 1, u) * values
         halves = [dot(lowers[u] * joins[k], inverses[u]).astype(BF16) for u in units]
         inverses = [inverses[u] - dot(inverses[u], halves[u]).astype(BF16) for u in units]
     for u in units:
@@ -299,7 +302,7 @@
         high, low = split(writes)
         solved_out[u, :, 2 * DV : 2 * DV + DK] = high
         solved_out[u, :, 2 * DV + DK :] = low
-        leave(4, u, 1)
+        leave(3, u, 1)
         g = j * KEYS + h // 2
         kt = keys_t[g, :, :C], keys_t[g, :, C:]
         moved = dot3(kt, split(column(columns, 3, u) * writes))
@@ -324,8 +327,8 @@
             parts = jnp.concatenate([top, middle, both - top - middle, jnp.zeros((13, DK), F32)], 0)
             message[h, 2 * DK : WHOLE] = parts.astype(BF16)
         if u == HEADS - 1:
+            leave(4)
             leave(5)
-            leave(6)
     for one in copies:
         one.wait()
 
@@ -348,7 +351,7 @@
             pltpu.VMEM((BLOCKS * KEYS, DK, 2 * C), BF16),
             pltpu.VMEM((units, C, DV + DK), F32),
             pltpu.VMEM((HEADS, DK, DK), F32),
-            pltpu.SemaphoreType.DMA((4,)),
+            pltpu.SemaphoreType.DMA((5,)),
             pltpu.SemaphoreType.DMA((24,)),
         ],
         compiler_params=params(TERMS_MIB),
@@ -361,7 +364,7 @@
     sources, (base, reads), kept = rest[: len(KEPT)], rest[len(KEPT) : len(KEPT) + 2], rest[len(KEPT) + 2 : -5]
     bases, readers, raw, staged, sems = rest[-5:]
     core = my_core()
-    columns, starts, pairs, keys, solved, early_transit, early_add = kept
+    columns, totals, keys, solved, early_transit, early_add = kept
     copies = []
 
     def move(source, target, first=None, count=HEADS):
@@ -372,19 +375,19 @@
 
     move(own.at[:, pl.ds(pl.multiple_of(core * QK, QK), QK)], staged.at[0])
     move(got.at[0:C, 0:QK], staged.at[1])
-    for i in (0, 1, 3):
+    for i in (0, 1, 2):
         move(sources[i], kept[i])
     for j in range(BLOCKS):
-        move(sources[2], pairs, j * HEADS)
-        move(sources[4], solved, j * HEADS)
+        move(sources[3], solved, j * HEADS)
         if j == 0:
-            move(sources[5], early_transit)
-            move(sources[6], early_add)
+            move(sources[4], early_transit)
+            move(sources[5], early_add)
+    inclusive = lax.broadcasted_iota(jnp.int32, (C, C), 0) >= lax.broadcasted_iota(jnp.int32, (C, C), 1)
     for one in copies[:5]:
         one.wait()
-    assemble(core, staged, halo, raw, 0, QK)
+    assemble(core, staged, halo, raw, 0, 0, QK)
     for j in range(BLOCKS):
-        for one in copies[5:7] if j == 0 else copies[7:11]:
+        for one in copies[5:6] if j == 0 else copies[6:9]:
             one.wait()
         for g in range(KEYS):
             queries = convolved(raw, taps, g * DK, core * QK + g * DK, j)
@@ -395,7 +398,8 @@
             plain = dot_t(jnp.concatenate([qh, ql], 1), jnp.concatenate([kh, kh], 1)) + dot_t(qh, kl)
             for h in (2 * g, 2 * g + 1):
                 u = unit_of(j, h)
-                gram = split(pairs[u] * plain)
+                pair = jnp.where(inclusive, jnp.exp(jnp.minimum(column(columns, 0, u) - totals[u : u + 1], 0.0)), 0.0)
+                gram = split(pair * plain)
                 inner = solved[u]
                 out = dot3(gram, (inner[:, :DV], inner[:, DV : 2 * DV]))
                 writes = inner[:, 2 * DV : 2 * DV + DK], inner[:, 2 * DV + DK :]
@@ -404,14 +408,14 @@
                     high, low = split(read)
                     out = out + dot3((high, low), (early_add[h, :, :DV], early_add[h, :, DV:]))
                     before = unit_of(0, h)
-                    read = starts[before : before + 1, C - 1 : C] * read - dot(high, early_transit[h])
+                    read = jnp.exp(totals[before : before + 1, C - 1 : C]) * read - dot(high, early_transit[h])
                 bases[u] = out
                 high, low = split(read)
                 readers[u, :, :DK] = high
                 readers[u, :, DK:] = low
         move(bases, base, j * HEADS)
         move(readers, reads, j * HEADS)
-    for one in copies[11:]:
+    for one in copies[9:]:
         one.wait()
 
 
@@ -530,15 +534,10 @@
 
 
 def project_kernel(mine, theirs, *rest):
-    own, others, (out, normed, ordered, sems) = rest[:SIDE], rest[SIDE : 2 * SIDE], rest[2 * SIDE :]
+    own, others, (out, normed, ordered) = rest[:SIDE], rest[SIDE : 2 * SIDE], rest[2 * SIDE :]
     core = my_core()
-    loads = []
-    for i, (source, its_core) in enumerate(((mine, core), (theirs, 1 - core))):
-        target = normed.at[pl.ds(pl.multiple_of(its_core * HEADS, HEADS), HEADS)]
-        loads.append(pltpu.make_async_copy(source, target, sems.at[i]))
-        loads[-1].start()
-    for one in loads:
-        one.wait()
+    for source, its_core in ((mine, core), (theirs, 1 - core)):
+        normed[pl.ds(its_core * HEADS, HEADS)] = source[...]
     for its_core, weights in ((core, own), (1 - core, others)):
         in_order_of(its_core, normed, ordered)
         out[:, pl.ds(pl.multiple_of(its_core * HALF, HALF), HALF)] = product_of(ordered, weights)
@@ -548,14 +547,13 @@
     return pl.pallas_call(
         project_kernel,
         out_shape=shape((C, WIDTH), BF16),
-        in_specs=[ANY] * 2 + [VMEM] * 2 * SIDE,
+        in_specs=[VMEM] * (2 + 2 * SIDE),
         out_specs=VMEM,
         compiler_params=params(40),
         cost_estimate=cost(2 * C * WIDTH * WIDTH, 2**23),
         scratch_shapes=[
             pltpu.VMEM((VH, C, DV), BF16),
             pltpu.VMEM((C, WIDTH), BF16),
-            pltpu.SemaphoreType.DMA((2,)),
         ],
         name="project",
     )(mine, theirs, *weights, *other_weights)

time: 85.1 us -> 85 us (level)
  no operation moved by 1% of the time
where the time goes in v4:
time: 85 us; the launch traced here: 84.4 us
  Pallas kernels  32.4 us (38%)
  starting transfers between devices  27.9 us (33%)
  waiting for transfers between devices  21.4 us (25%)
  local copies, waits for them, and re-layouts  1.57 us (2%)
  other arithmetic  1.03 us (1%)
    all_to_all x2, waiting for transfers between devices, between_chips(): return lax.all_to_all(blocks, 'seq', 0, 0, axis_index_groups=groups)  15.4 us
    pallas_call x1, Pallas kernels, run_terms(): pl.pallas_call(terms_kernel, out_shape=[shape((HEADS, WHOLE, DV), BF16)]...  11.4 us
    all_to_all x2, starting transfers between devices, between_chips(): return lax.all_to_all(blocks, 'seq', 0, 0, axis_index_groups=groups)  10.7 us
    ppermute x6, starting transfers between devices, along(): return lax.ppermute(block, ('seq', 'fsdp'), route)  9.95 us
    pallas_call x1, Pallas kernels, run_reads(): pl.pallas_call(reads_kernel, out_shape=[shape((units, C, DV), F32), shape...  7.58 us
    ppermute x6, starting transfers between devices, other_core(): return lax.ppermute(block, 'seq', [(i, i ^ 1) for i in range(SEGMENTS)])  5.46 us
    pallas_call x1, Pallas kernels, project(): pl.pallas_call(project_kernel, out_shape=shape((C, WIDTH), BF16), in_spec...  4.64 us
    ppermute x6, waiting for transfers between devices, other_core(): return lax.ppermute(block, 'seq', [(i, i ^ 1) for i in range(SEGMENTS)])  3.83 us
  transfers between devices with their start and end apart: 15, of which 5 were waited for; matrix products, arithmetic and copies ran while one was open for 0% of the time, Pallas kernels for 30%

profile of v4, /device:TPU:1, one launch (start us, length us, event | category | flops | bytes accessed | tf_op | source)
XLA Modules:
  0.0 84.4 jit_solution(1634529876385035259)
XLA Ops:
  0.0 2.4 %cut.1 = (bf16[144,3072]{1,0:T(8,128)(2,1)}, bf16[16,2048]{1,0:T(8,128)(2,1)}, bf16[128,1024]{1,0:T(8,128)(2,1)}) custom-call(bf16[128,4096]{1,0:T(8,128)(2,1)} %bitcast.10, bf16[128,2048]{1,0:T(8,128)(2,1)} %bitcast.13, s32[16,128]{1,0:T(8,128)} %bitcast.19, s32[16,128]{1,0:T(8,128)} %bitcast.21, bf16[128,2048]{1,0:T(8,128)(2,1)} %weight.1), custom_call_target="tpu_custom_call" | custom-call | tf_op jit(solution)/shard_map/cut/pallas_call | solution.py:136
  2.4 3.3 %collective-permute-start = (bf16[144,3072]{1,0:T(8,128)(2,1)}, bf16[144,3072]{1,0:T(8,128)(2,1)S(1)}, u32[]{:S(2)}, u32[]{:S(2)}) collective-permute-start(bf16[144,3072]{1,0:T(8,128)(2,1)} %get-tuple-element.31), channel_id=1, source_target_pairs={{0,16},{16,0},{32,48},{48,32},{64,80},{80,64},{96,112},{112,96},{1... | collective-permute-start | bytes 2654216 | tf_op jit(solution)/shard_map/ppermute | solution.py:42
  5.8 2.3 %collective-permute-done.got = bf16[144,3072]{1,0:T(8,128)(2,1)S(1)} collective-permute-done((bf16[144,3072]{1,0:T(8,128)(2,1)}, bf16[144,3072]{1,0:T(8,128)(2,1)S(1)}, u32[]{:S(2)}, u32[]{:S(2)}) %collective-permute-start) | collective-permute-done | bytes 884768 | tf_op jit(solution)/shard_map/ppermute | solution.py:42
  8.0 0.0 copy-start.3
  8.0 0.9 %slice_select_fusion = bf16[16,2048]{1,0:T(8,128)(2,1)S(1)} fusion(bf16[16,2048]{1,0:T(8,128)(2,1)} %get-tuple-element.32, bf16[144,3072]{1,0:T(8,128)(2,1)S(1)} %collective-permute-done.got, pred[]{:T(512)S(6)} %eq.5), kind=kLoop, calls=%fused_computation.1 | loop fusion | flops 32768 | bytes 196609 | tf_op jit(solution)/shard_map/jit(_where)/select_n | solution.py:588
  8.9 1.8 %collective-permute-start.1 = (bf16[16,2048]{1,0:T(8,128)(2,1)S(1)}, bf16[16,2048]{1,0:T(8,128)(2,1)S(1)}, u32[]{:S(2)}, u32[]{:S(2)}) collective-permute-start(bf16[16,2048]{1,0:T(8,128)(2,1)S(1)} %slice_select_fusion), channel_id=1, source_target_pairs={{0,32},{16,48},{32,64},{48,80},{64,96},{80,112},{96,128},{112,144}... | collective-permute-start | bytes 196616 | tf_op jit(solution)/shard_map/ppermute | solution.py:589
  10.7 0.0 copy-start.2
  10.8 1.4 %collective-permute-start.2 = (bf16[128,1024]{1,0:T(8,128)(2,1)}, bf16[128,1024]{1,0:T(8,128)(2,1)S(1)}, u32[]{:S(2)}, u32[]{:S(2)}) collective-permute-start(bf16[128,1024]{1,0:T(8,128)(2,1)} %get-tuple-element.45), channel_id=1, source_target_pairs={{0,1},{1,2},{2,3},{3,0},{4,5},{5,6},{6,7},{7,4},{8,9},{9,10},{10,1... | collective-permute-start | bytes 786440 | tf_op jit(solution)/shard_map/ppermute | solution.py:570
  12.1 2.6 %collective-permute-start.3 = (bf16[128,1024]{1,0:T(8,128)(2,1)}, bf16[128,1024]{1,0:T(8,128)(2,1)S(1)}, u32[]{:S(2)}, u32[]{:S(2)}) collective-permute-start(bf16[128,1024]{1,0:T(8,128)(2,1)} %get-tuple-element.45), channel_id=1, source_target_pairs={{0,2},{1,3},{2,0},{3,1},{4,6},{5,7},{6,4},{7,5},{8,10},{9,11},{10,... | collective-permute-start | bytes 786440 | tf_op jit(solution)/shard_map/ppermute | solution.py:570
  14.8 1.1 %collective-permute-start.4 = (bf16[128,1024]{1,0:T(8,128)(2,1)}, bf16[128,1024]{1,0:T(8,128)(2,1)S(1)}, u32[]{:S(2)}, u32[]{:S(2)}) collective-permute-start(bf16[128,1024]{1,0:T(8,128)(2,1)} %get-tuple-element.45), channel_id=1, source_target_pairs={{0,3},{1,0},{2,1},{3,2},{4,7},{5,4},{6,5},{7,6},{8,11},{9,8},{10,9... | collective-permute-start | bytes 786440 | tf_op jit(solution)/shard_map/ppermute | solution.py:570
  15.8 0.0 collective-permute-done.1.halo
  15.8 0.0 copy-done.3
  15.8 0.0 copy-start.4
  15.8 0.6 copy-done.4
  16.4 11.4 %terms.1 = (bf16[8,272,128]{2,1,0:T(8,128)(2,1)}, f32[128,128]{1,0:T(8,128)}, f32[16,128]{1,0:T(8,128)}, bf16[8,128,256]{2,1,0:T(8,128)(2,1)}, bf16[16,128,512]{...) custom-call(f32[16]{0:T(128)} %scale_log.1, f32[16]{0:T(128)} %bias.1, ...), custom_call_target="tpu_custom_call" | custom-call | flops 8000000000 | bytes 33554432 | tf_op jit(solution)/shard_map/terms/pallas_call | solution.py:338
  27.9 0.0 collective-permute-done.2
  27.9 0.0 collective-permute-done.3
  27.9 0.0 collective-permute-done.4
  27.9 7.3 %all-to-all-start = ((bf16[8,272,128]{2,1,0:T(8,128)(2,1)}), bf16[8,272,128]{2,1,0:T(8,128)(2,1)}, u32[]{:S(2)}, u32[]{:S(2)}) async-start(bf16[8,272,128]{2,1,0:T(8,128)(2,1)} %get-tuple-element.35), calls=%async_computation | async-start | bytes 1114112 | tf_op jit(solution)/shard_map/all_to_all | solution.py:47
  35.2 0.0 copy-done.2
  35.2 0.1 pad_maximum_fusion.rest_0_
  35.3 1.3 %collective-permute-start.5 = (bf16[4,128,1024]{2,1,0:T(8,128)(2,1)S(1)}, bf16[4,128,1024]{2,1,0:T(8,128)(2,1)S(1)}, u32[]{:S(2)}, u32[]{:S(2)}) collective-permute-start(bf16[4,128,1024]{2,1,0:T(8,128)(2,1)S(1)} %pad_maximum_fusion.rest_0_), channel_id=1, source_target_pairs={{0,4},{1,5},{2,6},{3,7},{4,8},{5,9},{6,10},{7,11},{8,12},{9,13},{1... | collective-permute-start | bytes 3145736 | tf_op jit(solution)/shard_map/ppermute | solution.py:570
  36.6 2.4 %collective-permute-start.6 = (bf16[4,128,1024]{2,1,0:T(8,128)(2,1)S(1)}, bf16[4,128,1024]{2,1,0:T(8,128)(2,1)S(1)}, u32[]{:S(2)}, u32[]{:S(2)}) collective-permute-start(bf16[4,128,1024]{2,1,0:T(8,128)(2,1)S(1)} %pad_maximum_fusion.rest_0_), channel_id=1, source_target_pairs={{0,8},{1,9},{2,10},{3,11},{4,12},{5,13},{6,14},{7,15},{8,0},{9,1},... | collective-permute-start | bytes 3145736 | tf_op jit(solution)/shard_map/ppermute | solution.py:570
  39.1 1.2 %collective-permute-start.7 = (bf16[4,128,1024]{2,1,0:T(8,128)(2,1)S(1)}, bf16[4,128,1024]{2,1,0:T(8,128)(2,1)}, u32[]{:S(2)}, u32[]{:S(2)}) collective-permute-start(bf16[4,128,1024]{2,1,0:T(8,128)(2,1)S(1)} %pad_maximum_fusion.rest_0_), channel_id=1, source_target_pairs={{0,12},{1,13},{2,14},{3,15},{4,0},{5,1},{6,2},{7,3},{8,4},{9,5},{1... | collective-permute-start | bytes 3145736 | tf_op jit(solution)/shard_map/ppermute | solution.py:570
  40.2 7.6 %reads.1 = (f32[16,128,128]{2,1,0:T(8,128)}, bf16[16,128,256]{2,1,0:T(8,128)(2,1)}) custom-call(bf16[128,4096]{1,0:T(8,128)(2,1)} %bitcast.12, bf16[144,3072]{1,0:T(8,128)(2,1)} %copy-done.3, bf16[16,2048]{1,0:T(8,128)(2,1)} %copy-done.4, f32[4,4096]{1,0:T(4,128)} %taps.3, f32[128,128]{1,0:T(8,128)} %get-tuple-element.36.rest_0_, ...), custom_call_target="tpu_custom_call" | custom-call | flops 4000000000 | bytes 16777216 | tf_op jit(solution)/shard_map/reads/pallas_call | solution.py:424
  47.8 6.1 %all-to-all-done.arrived = bf16[8,272,128]{2,1,0:T(8,128)(2,1)} async-done(((bf16[8,272,128]{2,1,0:T(8,128)(2,1)}), bf16[8,272,128]{2,1,0:T(8,128)(2,1)}, u32[]{:S(2)}, u32[]{:S(2)}) %all-to-all-start) | async-done | bytes 557088 | tf_op jit(solution)/shard_map/all_to_all | solution.py:47
  54.0 2.7 %enter.1 = bf16[8,128,128]{2,1,0:T(8,128)(2,1)} custom-call(bf16[8,272,128]{2,1,0:T(8,128)(2,1)} %all-to-all-done.arrived), custom_call_target="tpu_custom_call" | custom-call | flops 1000000000 | bytes 1048576 | tf_op jit(solution)/shard_map/enter/pallas_call | solution.py:461
  56.6 3.4 %all-to-all-start.1 = ((bf16[8,128,128]{2,1,0:T(8,128)(2,1)}), bf16[8,128,128]{2,1,0:T(8,128)(2,1)S(1)}, u32[]{:S(2)}, u32[]{:S(2)}) async-start(bf16[8,128,128]{2,1,0:T(8,128)(2,1)} %enter.1), calls=%async_computation.1 | async-start | bytes 524288 | tf_op jit(solution)/shard_map/all_to_all | solution.py:47
  60.1 0.6 collective-permute-start.9
  60.6 0.0 collective-permute-done.5.rest_1_
  60.6 2.1 %collective-permute-done.6.rest_2_ = bf16[4,128,1024]{2,1,0:T(8,128)(2,1)S(1)} collective-permute-done((bf16[4,128,1024]{2,1,0:T(8,128)(2,1)S(1)}, bf16[4,128,1024]{2,1,0:T(8,128)(2,1)S(1)}, u32[]{:S(2)}, u32[]{:S(2)}) %collective-permute-start.6) | collective-permute-done | bytes 1048608 | tf_op jit(solution)/shard_map/ppermute | solution.py:570
  62.8 0.0 collective-permute-done.7.rest_3_
  62.8 9.2 %all-to-all-done.1.arrived = bf16[8,128,128]{2,1,0:T(8,128)(2,1)S(1)} async-done(((bf16[8,128,128]{2,1,0:T(8,128)(2,1)}), bf16[8,128,128]{2,1,0:T(8,128)(2,1)S(1)}, u32[]{:S(2)}, u32[]{:S(2)}) %all-to-all-start.1) | async-done | bytes 262176 | tf_op jit(solution)/shard_map/all_to_all | solution.py:47
  72.0 0.0 copy-start.1
  72.0 0.8 collective-permute-start.10
  72.8 0.0 collective-permute-start.11
  72.8 0.5 collective-permute-start.12
  73.3 0.0 copy-done.1
  73.3 3.7 %finish.1 = (bf16[8,128,128]{2,1,0:T(8,128)(2,1)}, bf16[8,128,128]{2,1,0:T(8,128)(2,1)}) custom-call(bf16[8,128,128]{2,1,0:T(8,128)(2,1)} %copy-done.1, f32[16,128,128]{2,1,0:T(8,128)} %get-tuple-element.50.base, bf16[16,128,256]{2,1,0:T(8,128)(2,1)} %get-tuple-element.51.reads, bf16[128,2048]{1,0:T(8,128)(2,1)} %bitcast.14, bf16[144,3072]{1,0:T(8,128)(2,1)} %copy-done.3, ...), custom_call_target="tpu_custom_call" | custom-call | flops 2000000000 | bytes 4194304 | tf_op jit(solution)/shard_map/finish/pallas_call | solution.py:497
  77.0 0.3 collective-permute-start.8
  77.3 0.0 collective-permute-done.9.rest_4_
  77.3 1.6 %collective-permute-done.8.theirs = bf16[8,128,128]{2,1,0:T(8,128)(2,1)S(1)} collective-permute-done((bf16[8,128,128]{2,1,0:T(8,128)(2,1)}, bf16[8,128,128]{2,1,0:T(8,128)(2,1)S(1)}, u32[]{:S(2)}, u32[]{:S(2)}) %collective-permute-start.8) | collective-permute-done | bytes 262176 | tf_op jit(solution)/shard_map/ppermute | solution.py:42
  78.8 0.0 collective-permute-done.10.rest_5_
  78.8 0.0 collective-permute-done.11.rest_6_
  78.9 0.0 collective-permute-done.12.rest_7_
  78.9 0.0 copy-start
  78.9 0.9 %copy-done = bf16[8,128,128]{2,1,0:T(8,128)(2,1)S(1)} copy-done((bf16[8,128,128]{2,1,0:T(8,128)(2,1)S(1)}, bf16[8,128,128]{2,1,0:T(8,128)(2,1)}, u32[]{:S(2)}) %copy-start) | copy-done | bytes 262168
  79.8 4.6 %project.1 = bf16[128,2048]{1,0:T(8,128)(2,1)} custom-call(bf16[8,128,128]{2,1,0:T(8,128)(2,1)S(1)} %copy-done, bf16[8,128,128]{2,1,0:T(8,128)(2,1)S(1)} %collective-permute-done.8.theirs, bf16[4,128,1024]{2,1,0:T(8,128)(2,1)S(1)} %pad_maximum_fusion.rest_0_, bf16[4,128,1024]{2,1,0:T(8,128)(2,1)S(1)} %collective-permute-done.5.rest_1_, ...), custom_call_target="tpu_custom_call" | custom-call | flops 1073741824 | bytes 8388608 | tf_op jit(solution)/shard_map/project/pallas_call | solution.py:547
Async XLA Ops:
  2.4 5.6 %collective-permute-start = (bf16[144,3072]{1,0:T(8,128)(2,1)}, bf16[144,3072]{1,0:T(8,128)(2,1)S(1)}, u32[]{:S(2)}, u32[]{:S(2)}) collective-permute-start(bf16[144,3072]{1,0:T(8,128)(2,1)} %get-tuple-element.31), channel_id=1, source_target_pairs={{0,16},{16,0},{32,48},{48,32},{64,80},{80,64},{96,112},{112,96},{1... | collective-permute-start | bytes 2654216 | tf_op jit(solution)/shard_map/ppermute | solution.py:42
  8.0 7.8 %copy-start.3 = (bf16[144,3072]{1,0:T(8,128)(2,1)}, bf16[144,3072]{1,0:T(8,128)(2,1)S(1)}, u32[]{:S(2)}) copy-start(bf16[144,3072]{1,0:T(8,128)(2,1)S(1)} %collective-permute-done.got) | copy-start | bytes 2654212
  8.9 6.9 %collective-permute-start.1 = (bf16[16,2048]{1,0:T(8,128)(2,1)S(1)}, bf16[16,2048]{1,0:T(8,128)(2,1)S(1)}, u32[]{:S(2)}, u32[]{:S(2)}) collective-permute-start(bf16[16,2048]{1,0:T(8,128)(2,1)S(1)} %slice_select_fusion), channel_id=1, source_target_pairs={{0,32},{16,48},{32,64},{48,80},{64,96},{80,112},{96,128},{112,144}... | collective-permute-start | bytes 196616 | tf_op jit(solution)/shard_map/ppermute | solution.py:589
  10.7 24.4 %copy-start.2 = (bf16[128,1024]{1,0:T(8,128)(2,1)S(1)}, bf16[128,1024]{1,0:T(8,128)(2,1)}, u32[]{:S(2)}) copy-start(bf16[128,1024]{1,0:T(8,128)(2,1)} %get-tuple-element.45) | copy-start | bytes 786436
  10.8 17.1 %collective-permute-start.2 = (bf16[128,1024]{1,0:T(8,128)(2,1)}, bf16[128,1024]{1,0:T(8,128)(2,1)S(1)}, u32[]{:S(2)}, u32[]{:S(2)}) collective-permute-start(bf16[128,1024]{1,0:T(8,128)(2,1)} %get-tuple-element.45), channel_id=1, source_target_pairs={{0,1},{1,2},{2,3},{3,0},{4,5},{5,6},{6,7},{7,4},{8,9},{9,10},{10,1... | collective-permute-start | bytes 786440 | tf_op jit(solution)/shard_map/ppermute | solution.py:570
  12.1 15.7 %collective-permute-start.3 = (bf16[128,1024]{1,0:T(8,128)(2,1)}, bf16[128,1024]{1,0:T(8,128)(2,1)S(1)}, u32[]{:S(2)}, u32[]{:S(2)}) collective-permute-start(bf16[128,1024]{1,0:T(8,128)(2,1)} %get-tuple-element.45), channel_id=1, source_target_pairs={{0,2},{1,3},{2,0},{3,1},{4,6},{5,7},{6,4},{7,5},{8,10},{9,11},{10,... | collective-permute-start | bytes 786440 | tf_op jit(solution)/shard_map/ppermute | solution.py:570
  14.8 13.1 %collective-permute-start.4 = (bf16[128,1024]{1,0:T(8,128)(2,1)}, bf16[128,1024]{1,0:T(8,128)(2,1)S(1)}, u32[]{:S(2)}, u32[]{:S(2)}) collective-permute-start(bf16[128,1024]{1,0:T(8,128)(2,1)} %get-tuple-element.45), channel_id=1, source_target_pairs={{0,3},{1,0},{2,1},{3,2},{4,7},{5,4},{6,5},{7,6},{8,11},{9,8},{10,9... | collective-permute-start | bytes 786440 | tf_op jit(solution)/shard_map/ppermute | solution.py:570
  15.8 0.6 copy-start.4
  27.9 26.1 %all-to-all-start = ((bf16[8,272,128]{2,1,0:T(8,128)(2,1)}), bf16[8,272,128]{2,1,0:T(8,128)(2,1)}, u32[]{:S(2)}, u32[]{:S(2)}) async-start(bf16[8,272,128]{2,1,0:T(8,128)(2,1)} %get-tuple-element.35), calls=%async_computation | async-start | bytes 1114112 | tf_op jit(solution)/shard_map/all_to_all | solution.py:47
  35.3 25.3 %collective-permute-start.5 = (bf16[4,128,1024]{2,1,0:T(8,128)(2,1)S(1)}, bf16[4,128,1024]{2,1,0:T(8,128)(2,1)S(1)}, u32[]{:S(2)}, u32[]{:S(2)}) collective-permute-start(bf16[4,128,1024]{2,1,0:T(8,128)(2,1)S(1)} %pad_maximum_fusion.rest_0_), channel_id=1, source_target_pairs={{0,4},{1,5},{2,6},{3,7},{4,8},{5,9},{6,10},{7,11},{8,12},{9,13},{1... | collective-permute-start | bytes 3145736 | tf_op jit(solution)/shard_map/ppermute | solution.py:570
  36.6 26.2 %collective-permute-start.6 = (bf16[4,128,1024]{2,1,0:T(8,128)(2,1)S(1)}, bf16[4,128,1024]{2,1,0:T(8,128)(2,1)S(1)}, u32[]{:S(2)}, u32[]{:S(2)}) collective-permute-start(bf16[4,128,1024]{2,1,0:T(8,128)(2,1)S(1)} %pad_maximum_fusion.rest_0_), channel_id=1, source_target_pairs={{0,8},{1,9},{2,10},{3,11},{4,12},{5,13},{6,14},{7,15},{8,0},{9,1},... | collective-permute-start | bytes 3145736 | tf_op jit(solution)/shard_map/ppermute | solution.py:570
  39.1 23.7 %collective-permute-start.7 = (bf16[4,128,1024]{2,1,0:T(8,128)(2,1)S(1)}, bf16[4,128,1024]{2,1,0:T(8,128)(2,1)}, u32[]{:S(2)}, u32[]{:S(2)}) collective-permute-start(bf16[4,128,1024]{2,1,0:T(8,128)(2,1)S(1)} %pad_maximum_fusion.rest_0_), channel_id=1, source_target_pairs={{0,12},{1,13},{2,14},{3,15},{4,0},{5,1},{6,2},{7,3},{8,4},{9,5},{1... | collective-permute-start | bytes 3145736 | tf_op jit(solution)/shard_map/ppermute | solution.py:570
  56.6 15.4 %all-to-all-start.1 = ((bf16[8,128,128]{2,1,0:T(8,128)(2,1)}), bf16[8,128,128]{2,1,0:T(8,128)(2,1)S(1)}, u32[]{:S(2)}, u32[]{:S(2)}) async-start(bf16[8,128,128]{2,1,0:T(8,128)(2,1)} %enter.1), calls=%async_computation.1 | async-start | bytes 524288 | tf_op jit(solution)/shard_map/all_to_all | solution.py:47
  60.1 17.2 %collective-permute-start.9 = (bf16[4,128,1024]{2,1,0:T(8,128)(2,1)S(1)}, bf16[4,128,1024]{2,1,0:T(8,128)(2,1)}, u32[]{:S(2)}, u32[]{:S(2)}) collective-permute-start(bf16[4,128,1024]{2,1,0:T(8,128)(2,1)S(1)} %pad_maximum_fusion.rest_0_), channel_id=1, source_target_pairs={{0,16},{16,0},{32,48},{48,32},{64,80},{80,64},{96,112},{112,96},{1... | collective-permute-start | bytes 3145736 | tf_op jit(solution)/shard_map/ppermute | solution.py:42
  72.0 1.3 %copy-start.1 = (bf16[8,128,128]{2,1,0:T(8,128)(2,1)}, bf16[8,128,128]{2,1,0:T(8,128)(2,1)S(1)}, u32[]{:S(2)}) copy-start(bf16[8,128,128]{2,1,0:T(8,128)(2,1)S(1)} %all-to-all-done.1.arrived) | copy-start | bytes 786436
  72.0 6.8 %collective-permute-start.10 = (bf16[4,128,1024]{2,1,0:T(8,128)(2,1)S(1)}, bf16[4,128,1024]{2,1,0:T(8,128)(2,1)}, u32[]{:S(2)}, u32[]{:S(2)}) collective-permute-start(bf16[4,128,1024]{2,1,0:T(8,128)(2,1)S(1)} %collective-permute-done.5.rest_1_), channel_id=1, source_target_pairs={{0,16},{16,0},{32,48},{48,32},{64,80},{80,64},{96,112},{112,96},{1... | collective-permute-start | bytes 3145736 | tf_op jit(solution)/shard_map/ppermute | solution.py:42
  72.8 6.0 %collective-permute-start.11 = (bf16[4,128,1024]{2,1,0:T(8,128)(2,1)S(1)}, bf16[4,128,1024]{2,1,0:T(8,128)(2,1)}, u32[]{:S(2)}, u32[]{:S(2)}) collective-permute-start(bf16[4,128,1024]{2,1,0:T(8,128)(2,1)S(1)} %collective-permute-done.6.rest_2_), channel_id=1, source_target_pairs={{0,16},{16,0},{32,48},{48,32},{64,80},{80,64},{96,112},{112,96},{1... | collective-permute-start | bytes 3145736 | tf_op jit(solution)/shard_map/ppermute | solution.py:42
  72.8 6.0 %collective-permute-start.12 = (bf16[4,128,1024]{2,1,0:T(8,128)(2,1)}, bf16[4,128,1024]{2,1,0:T(8,128)(2,1)}, u32[]{:S(2)}, u32[]{:S(2)}) collective-permute-start(bf16[4,128,1024]{2,1,0:T(8,128)(2,1)} %collective-permute-done.7.rest_3_), channel_id=1, source_target_pairs={{0,16},{16,0},{32,48},{48,32},{64,80},{80,64},{96,112},{112,96},{1... | collective-permute-start | bytes 3145736 | tf_op jit(solution)/shard_map/ppermute | solution.py:42
  77.0 1.8 %collective-permute-start.8 = (bf16[8,128,128]{2,1,0:T(8,128)(2,1)}, bf16[8,128,128]{2,1,0:T(8,128)(2,1)S(1)}, u32[]{:S(2)}, u32[]{:S(2)}) collective-permute-start(bf16[8,128,128]{2,1,0:T(8,128)(2,1)} %get-tuple-element.53), channel_id=1, source_target_pairs={{0,16},{16,0},{32,48},{48,32},{64,80},{80,64},{96,112},{112,96},{1... | collective-permute-start | bytes 786440 | tf_op jit(solution)/shard_map/ppermute | solution.py:42
  78.9 1.0 %copy-start = (bf16[8,128,128]{2,1,0:T(8,128)(2,1)S(1)}, bf16[8,128,128]{2,1,0:T(8,128)(2,1)}, u32[]{:S(2)}) copy-start(bf16[8,128,128]{2,1,0:T(8,128)(2,1)} %get-tuple-element.52.mine) | copy-start | bytes 786436

commit v5 on v4

--- a/solution.py
+++ b/solution.py
@@ -506,7 +506,7 @@
             pltpu.VMEM((BLOCKS, C, HEADS * DV), BF16),
             pltpu.SemaphoreType.DMA((7,)),
         ],
-        compiler_params=params(TERMS_MIB),
+        compiler_params=params(55),
         cost_estimate=cost(2 * 10**9, 2**22),
         name="finish",
     )(entering, base, reads, gate, got, gain)
@@ -549,7 +549,7 @@
         out_shape=shape((C, WIDTH), BF16),
         in_specs=[VMEM] * (2 + 2 * SIDE),
         out_specs=VMEM,
-        compiler_params=params(40),
+        compiler_params=params(24),
         cost_estimate=cost(2 * C * WIDTH * WIDTH, 2**23),
         scratch_shapes=[
             pltpu.VMEM((VH, C, DV), BF16),

time: 85 us -> 84.1 us (0.989)
  Pallas kernels: 32.4 us -> 31.4 us
    pallas_call x1, Pallas kernels: 4.64 us -> 3.69 us  [project(): pl.pallas_call(project_kernel, out_shape=shape((C, WIDTH), BF16), in_spec...]
where the time goes in v5:
time: 84.1 us; the launch traced here: 83.5 us
  Pallas kernels  31.4 us (37%)
  starting transfers between devices  28 us (33%)
  waiting for transfers between devices  21.4 us (25%)
  local copies, waits for them, and re-layouts  1.57 us (2%)
  other arithmetic  1.03 us (1%)
    all_to_all x2, waiting for transfers between devices, between_chips(): return lax.all_to_all(blocks, 'seq', 0, 0, axis_index_groups=groups)  15.4 us
    pallas_call x1, Pallas kernels, run_terms(): pl.pallas_call(terms_kernel, out_shape=[shape((HEADS, WHOLE, DV), BF16)]...  11.4 us
    all_to_all x2, starting transfers between devices, between_chips(): return lax.all_to_all(blocks, 'seq', 0, 0, axis_index_groups=groups)  10.7 us
    ppermute x6, starting transfers between devices, along(): return lax.ppermute(block, ('seq', 'fsdp'), route)  9.96 us
    pallas_call x1, Pallas kernels, run_reads(): pl.pallas_call(reads_kernel, out_shape=[shape((units, C, DV), F32), shape...  7.58 us
    ppermute x6, starting transfers between devices, other_core(): return lax.ppermute(block, 'seq', [(i, i ^ 1) for i in range(SEGMENTS)])  5.47 us
    ppermute x6, waiting for transfers between devices, other_core(): return lax.ppermute(block, 'seq', [(i, i ^ 1) for i in range(SEGMENTS)])  3.83 us
    pallas_call x1, Pallas kernels, project(): pl.pallas_call(project_kernel, out_shape=shape((C, WIDTH), BF16), in_spec...  3.69 us
  transfers between devices with their start and end apart: 15, of which 5 were waited for; matrix products, arithmetic and copies ran while one was open for 0% of the time, Pallas kernels for 30%

profile of v5, /device:TPU:1, one launch (start us, length us, event | category | flops | bytes accessed | tf_op | source)
XLA Modules:
  0.0 83.5 jit_solution(17386471123923846779)
XLA Ops:
  0.0 2.4 %cut.1 = (bf16[144,3072]{1,0:T(8,128)(2,1)}, bf16[16,2048]{1,0:T(8,128)(2,1)}, bf16[128,1024]{1,0:T(8,128)(2,1)}) custom-call(bf16[128,4096]{1,0:T(8,128)(2,1)} %bitcast.10, bf16[128,2048]{1,0:T(8,128)(2,1)} %bitcast.13, s32[16,128]{1,0:T(8,128)} %bitcast.19, s32[16,128]{1,0:T(8,128)} %bitcast.21, bf16[128,2048]{1,0:T(8,128)(2,1)} %weight.1), custom_call_target="tpu_custom_call" | custom-call | tf_op jit(solution)/shard_map/cut/pallas_call | solution.py:136
  2.4 3.3 %collective-permute-start = (bf16[144,3072]{1,0:T(8,128)(2,1)}, bf16[144,3072]{1,0:T(8,128)(2,1)S(1)}, u32[]{:S(2)}, u32[]{:S(2)}) collective-permute-start(bf16[144,3072]{1,0:T(8,128)(2,1)} %get-tuple-element.31), channel_id=1, source_target_pairs={{0,16},{16,0},{32,48},{48,32},{64,80},{80,64},{96,112},{112,96},{1... | collective-permute-start | bytes 2654216 | tf_op jit(solution)/shard_map/ppermute | solution.py:42
  5.8 2.3 %collective-permute-done.got = bf16[144,3072]{1,0:T(8,128)(2,1)S(1)} collective-permute-done((bf16[144,3072]{1,0:T(8,128)(2,1)}, bf16[144,3072]{1,0:T(8,128)(2,1)S(1)}, u32[]{:S(2)}, u32[]{:S(2)}) %collective-permute-start) | collective-permute-done | bytes 884768 | tf_op jit(solution)/shard_map/ppermute | solution.py:42
  8.0 0.0 copy-start.3
  8.0 0.9 %slice_select_fusion = bf16[16,2048]{1,0:T(8,128)(2,1)S(1)} fusion(bf16[16,2048]{1,0:T(8,128)(2,1)} %get-tuple-element.32, bf16[144,3072]{1,0:T(8,128)(2,1)S(1)} %collective-permute-done.got, pred[]{:T(512)S(6)} %eq.5), kind=kLoop, calls=%fused_computation.1 | loop fusion | flops 32768 | bytes 196609 | tf_op jit(solution)/shard_map/jit(_where)/select_n | solution.py:588
  8.9 1.8 %collective-permute-start.1 = (bf16[16,2048]{1,0:T(8,128)(2,1)S(1)}, bf16[16,2048]{1,0:T(8,128)(2,1)S(1)}, u32[]{:S(2)}, u32[]{:S(2)}) collective-permute-start(bf16[16,2048]{1,0:T(8,128)(2,1)S(1)} %slice_select_fusion), channel_id=1, source_target_pairs={{0,32},{16,48},{32,64},{48,80},{64,96},{80,112},{96,128},{112,144}... | collective-permute-start | bytes 196616 | tf_op jit(solution)/shard_map/ppermute | solution.py:589
  10.7 0.0 copy-start.2
  10.8 1.4 %collective-permute-start.2 = (bf16[128,1024]{1,0:T(8,128)(2,1)}, bf16[128,1024]{1,0:T(8,128)(2,1)S(1)}, u32[]{:S(2)}, u32[]{:S(2)}) collective-permute-start(bf16[128,1024]{1,0:T(8,128)(2,1)} %get-tuple-element.45), channel_id=1, source_target_pairs={{0,1},{1,2},{2,3},{3,0},{4,5},{5,6},{6,7},{7,4},{8,9},{9,10},{10,1... | collective-permute-start | bytes 786440 | tf_op jit(solution)/shard_map/ppermute | solution.py:570
  12.1 2.6 %collective-permute-start.3 = (bf16[128,1024]{1,0:T(8,128)(2,1)}, bf16[128,1024]{1,0:T(8,128)(2,1)S(1)}, u32[]{:S(2)}, u32[]{:S(2)}) collective-permute-start(bf16[128,1024]{1,0:T(8,128)(2,1)} %get-tuple-element.45), channel_id=1, source_target_pairs={{0,2},{1,3},{2,0},{3,1},{4,6},{5,7},{6,4},{7,5},{8,10},{9,11},{10,... | collective-permute-start | bytes 786440 | tf_op jit(solution)/shard_map/ppermute | solution.py:570
  14.8 1.1 %collective-permute-start.4 = (bf16[128,1024]{1,0:T(8,128)(2,1)}, bf16[128,1024]{1,0:T(8,128)(2,1)S(1)}, u32[]{:S(2)}, u32[]{:S(2)}) collective-permute-start(bf16[128,1024]{1,0:T(8,128)(2,1)} %get-tuple-element.45), channel_id=1, source_target_pairs={{0,3},{1,0},{2,1},{3,2},{4,7},{5,4},{6,5},{7,6},{8,11},{9,8},{10,9... | collective-permute-start | bytes 786440 | tf_op jit(solution)/shard_map/ppermute | solution.py:570
  15.8 0.0 collective-permute-done.1.halo
  15.8 0.0 copy-done.3
  15.8 0.0 copy-start.4
  15.8 0.6 copy-done.4
  16.4 11.4 %terms.1 = (bf16[8,272,128]{2,1,0:T(8,128)(2,1)}, f32[128,128]{1,0:T(8,128)}, f32[16,128]{1,0:T(8,128)}, bf16[8,128,256]{2,1,0:T(8,128)(2,1)}, bf16[16,128,512]{...) custom-call(f32[16]{0:T(128)} %scale_log.1, f32[16]{0:T(128)} %bias.1, ...), custom_call_target="tpu_custom_call" | custom-call | flops 8000000000 | bytes 33554432 | tf_op jit(solution)/shard_map/terms/pallas_call | solution.py:338
  27.8 0.0 collective-permute-done.2
  27.8 0.0 collective-permute-done.3
  27.9 0.0 collective-permute-done.4
  27.9 7.3 %all-to-all-start = ((bf16[8,272,128]{2,1,0:T(8,128)(2,1)}), bf16[8,272,128]{2,1,0:T(8,128)(2,1)}, u32[]{:S(2)}, u32[]{:S(2)}) async-start(bf16[8,272,128]{2,1,0:T(8,128)(2,1)} %get-tuple-element.35), calls=%async_computation | async-start | bytes 1114112 | tf_op jit(solution)/shard_map/all_to_all | solution.py:47
  35.2 0.0 copy-done.2
  35.2 0.1 pad_maximum_fusion.rest_0_
  35.3 1.3 %collective-permute-start.5 = (bf16[4,128,1024]{2,1,0:T(8,128)(2,1)S(1)}, bf16[4,128,1024]{2,1,0:T(8,128)(2,1)S(1)}, u32[]{:S(2)}, u32[]{:S(2)}) collective-permute-start(bf16[4,128,1024]{2,1,0:T(8,128)(2,1)S(1)} %pad_maximum_fusion.rest_0_), channel_id=1, source_target_pairs={{0,4},{1,5},{2,6},{3,7},{4,8},{5,9},{6,10},{7,11},{8,12},{9,13},{1... | collective-permute-start | bytes 3145736 | tf_op jit(solution)/shard_map/ppermute | solution.py:570
  36.6 2.5 %collective-permute-start.6 = (bf16[4,128,1024]{2,1,0:T(8,128)(2,1)S(1)}, bf16[4,128,1024]{2,1,0:T(8,128)(2,1)S(1)}, u32[]{:S(2)}, u32[]{:S(2)}) collective-permute-start(bf16[4,128,1024]{2,1,0:T(8,128)(2,1)S(1)} %pad_maximum_fusion.rest_0_), channel_id=1, source_target_pairs={{0,8},{1,9},{2,10},{3,11},{4,12},{5,13},{6,14},{7,15},{8,0},{9,1},... | collective-permute-start | bytes 3145736 | tf_op jit(solution)/shard_map/ppermute | solution.py:570
  39.1 1.2 %collective-permute-start.7 = (bf16[4,128,1024]{2,1,0:T(8,128)(2,1)S(1)}, bf16[4,128,1024]{2,1,0:T(8,128)(2,1)}, u32[]{:S(2)}, u32[]{:S(2)}) collective-permute-start(bf16[4,128,1024]{2,1,0:T(8,128)(2,1)S(1)} %pad_maximum_fusion.rest_0_), channel_id=1, source_target_pairs={{0,12},{1,13},{2,14},{3,15},{4,0},{5,1},{6,2},{7,3},{8,4},{9,5},{1... | collective-permute-start | bytes 3145736 | tf_op jit(solution)/shard_map/ppermute | solution.py:570
  40.2 7.6 %reads.1 = (f32[16,128,128]{2,1,0:T(8,128)}, bf16[16,128,256]{2,1,0:T(8,128)(2,1)}) custom-call(bf16[128,4096]{1,0:T(8,128)(2,1)} %bitcast.12, bf16[144,3072]{1,0:T(8,128)(2,1)} %copy-done.3, bf16[16,2048]{1,0:T(8,128)(2,1)} %copy-done.4, f32[4,4096]{1,0:T(4,128)} %taps.3, f32[128,128]{1,0:T(8,128)} %get-tuple-element.36.rest_0_, ...), custom_call_target="tpu_custom_call" | custom-call | flops 4000000000 | bytes 16777216 | tf_op jit(solution)/shard_map/reads/pallas_call | solution.py:424
  47.8 6.1 %all-to-all-done.arrived = bf16[8,272,128]{2,1,0:T(8,128)(2,1)} async-done(((bf16[8,272,128]{2,1,0:T(8,128)(2,1)}), bf16[8,272,128]{2,1,0:T(8,128)(2,1)}, u32[]{:S(2)}, u32[]{:S(2)}) %all-to-all-start) | async-done | bytes 557088 | tf_op jit(solution)/shard_map/all_to_all | solution.py:47
  53.9 2.7 %enter.1 = bf16[8,128,128]{2,1,0:T(8,128)(2,1)} custom-call(bf16[8,272,128]{2,1,0:T(8,128)(2,1)} %all-to-all-done.arrived), custom_call_target="tpu_custom_call" | custom-call | flops 1000000000 | bytes 1048576 | tf_op jit(solution)/shard_map/enter/pallas_call | solution.py:461
  56.6 3.4 %all-to-all-start.1 = ((bf16[8,128,128]{2,1,0:T(8,128)(2,1)}), bf16[8,128,128]{2,1,0:T(8,128)(2,1)S(1)}, u32[]{:S(2)}, u32[]{:S(2)}) async-start(bf16[8,128,128]{2,1,0:T(8,128)(2,1)} %enter.1), calls=%async_computation.1 | async-start | bytes 524288 | tf_op jit(solution)/shard_map/all_to_all | solution.py:47
  60.0 0.6 collective-permute-start.9
  60.6 0.0 collective-permute-done.5.rest_1_
  60.6 2.1 %collective-permute-done.6.rest_2_ = bf16[4,128,1024]{2,1,0:T(8,128)(2,1)S(1)} collective-permute-done((bf16[4,128,1024]{2,1,0:T(8,128)(2,1)S(1)}, bf16[4,128,1024]{2,1,0:T(8,128)(2,1)S(1)}, u32[]{:S(2)}, u32[]{:S(2)}) %collective-permute-start.6) | collective-permute-done | bytes 1048608 | tf_op jit(solution)/shard_map/ppermute | solution.py:570
  62.8 0.0 collective-permute-done.7.rest_3_
  62.8 9.2 %all-to-all-done.1.arrived = bf16[8,128,128]{2,1,0:T(8,128)(2,1)S(1)} async-done(((bf16[8,128,128]{2,1,0:T(8,128)(2,1)}), bf16[8,128,128]{2,1,0:T(8,128)(2,1)S(1)}, u32[]{:S(2)}, u32[]{:S(2)}) %all-to-all-start.1) | async-done | bytes 262176 | tf_op jit(solution)/shard_map/all_to_all | solution.py:47
  72.0 0.0 copy-start.1
  72.0 0.8 collective-permute-start.10
  72.8 0.0 collective-permute-start.11
  72.8 0.5 collective-permute-start.12
  73.3 0.0 copy-done.1
  73.3 3.7 %finish.1 = (bf16[8,128,128]{2,1,0:T(8,128)(2,1)}, bf16[8,128,128]{2,1,0:T(8,128)(2,1)}) custom-call(bf16[8,128,128]{2,1,0:T(8,128)(2,1)} %copy-done.1, f32[16,128,128]{2,1,0:T(8,128)} %get-tuple-element.50.base, bf16[16,128,256]{2,1,0:T(8,128)(2,1)} %get-tuple-element.51.reads, bf16[128,2048]{1,0:T(8,128)(2,1)} %bitcast.14, bf16[144,3072]{1,0:T(8,128)(2,1)} %copy-done.3, ...), custom_call_target="tpu_custom_call" | custom-call | flops 2000000000 | bytes 4194304 | tf_op jit(solution)/shard_map/finish/pallas_call | solution.py:497
  77.0 0.3 collective-permute-start.8
  77.3 0.0 collective-permute-done.9.rest_4_
  77.3 1.6 %collective-permute-done.8.theirs = bf16[8,128,128]{2,1,0:T(8,128)(2,1)S(1)} collective-permute-done((bf16[8,128,128]{2,1,0:T(8,128)(2,1)}, bf16[8,128,128]{2,1,0:T(8,128)(2,1)S(1)}, u32[]{:S(2)}, u32[]{:S(2)}) %collective-permute-start.8) | collective-permute-done | bytes 262176 | tf_op jit(solution)/shard_map/ppermute | solution.py:42
  78.8 0.0 collective-permute-done.10.rest_5_
  78.8 0.0 collective-permute-done.11.rest_6_
  78.8 0.0 collective-permute-done.12.rest_7_
  78.8 0.0 copy-start
  78.8 0.9 %copy-done = bf16[8,128,128]{2,1,0:T(8,128)(2,1)S(1)} copy-done((bf16[8,128,128]{2,1,0:T(8,128)(2,1)S(1)}, bf16[8,128,128]{2,1,0:T(8,128)(2,1)}, u32[]{:S(2)}) %copy-start) | copy-done | bytes 262168
  79.8 3.7 %project.1 = bf16[128,2048]{1,0:T(8,128)(2,1)} custom-call(bf16[8,128,128]{2,1,0:T(8,128)(2,1)S(1)} %copy-done, bf16[8,128,128]{2,1,0:T(8,128)(2,1)S(1)} %collective-permute-done.8.theirs, bf16[4,128,1024]{2,1,0:T(8,128)(2,1)S(1)} %pad_maximum_fusion.rest_0_, bf16[4,128,1024]{2,1,0:T(8,128)(2,1)S(1)} %collective-permute-done.5.rest_1_, ...), custom_call_target="tpu_custom_call" | custom-call | flops 1073741824 | bytes 8388608 | tf_op jit(solution)/shard_map/project/pallas_call | solution.py:547
Async XLA Ops:
  2.4 5.6 %collective-permute-start = (bf16[144,3072]{1,0:T(8,128)(2,1)}, bf16[144,3072]{1,0:T(8,128)(2,1)S(1)}, u32[]{:S(2)}, u32[]{:S(2)}) collective-permute-start(bf16[144,3072]{1,0:T(8,128)(2,1)} %get-tuple-element.31), channel_id=1, source_target_pairs={{0,16},{16,0},{32,48},{48,32},{64,80},{80,64},{96,112},{112,96},{1... | collective-permute-start | bytes 2654216 | tf_op jit(solution)/shard_map/ppermute | solution.py:42
  8.0 7.8 %copy-start.3 = (bf16[144,3072]{1,0:T(8,128)(2,1)}, bf16[144,3072]{1,0:T(8,128)(2,1)S(1)}, u32[]{:S(2)}) copy-start(bf16[144,3072]{1,0:T(8,128)(2,1)S(1)} %collective-permute-done.got) | copy-start | bytes 2654212
  8.9 6.9 %collective-permute-start.1 = (bf16[16,2048]{1,0:T(8,128)(2,1)S(1)}, bf16[16,2048]{1,0:T(8,128)(2,1)S(1)}, u32[]{:S(2)}, u32[]{:S(2)}) collective-permute-start(bf16[16,2048]{1,0:T(8,128)(2,1)S(1)} %slice_select_fusion), channel_id=1, source_target_pairs={{0,32},{16,48},{32,64},{48,80},{64,96},{80,112},{96,128},{112,144}... | collective-permute-start | bytes 196616 | tf_op jit(solution)/shard_map/ppermute | solution.py:589
  10.7 24.4 %copy-start.2 = (bf16[128,1024]{1,0:T(8,128)(2,1)S(1)}, bf16[128,1024]{1,0:T(8,128)(2,1)}, u32[]{:S(2)}) copy-start(bf16[128,1024]{1,0:T(8,128)(2,1)} %get-tuple-element.45) | copy-start | bytes 786436
  10.8 17.1 %collective-permute-start.2 = (bf16[128,1024]{1,0:T(8,128)(2,1)}, bf16[128,1024]{1,0:T(8,128)(2,1)S(1)}, u32[]{:S(2)}, u32[]{:S(2)}) collective-permute-start(bf16[128,1024]{1,0:T(8,128)(2,1)} %get-tuple-element.45), channel_id=1, source_target_pairs={{0,1},{1,2},{2,3},{3,0},{4,5},{5,6},{6,7},{7,4},{8,9},{9,10},{10,1... | collective-permute-start | bytes 786440 | tf_op jit(solution)/shard_map/ppermute | solution.py:570
  12.1 15.7 %collective-permute-start.3 = (bf16[128,1024]{1,0:T(8,128)(2,1)}, bf16[128,1024]{1,0:T(8,128)(2,1)S(1)}, u32[]{:S(2)}, u32[]{:S(2)}) collective-permute-start(bf16[128,1024]{1,0:T(8,128)(2,1)} %get-tuple-element.45), channel_id=1, source_target_pairs={{0,2},{1,3},{2,0},{3,1},{4,6},{5,7},{6,4},{7,5},{8,10},{9,11},{10,... | collective-permute-start | bytes 786440 | tf_op jit(solution)/shard_map/ppermute | solution.py:570
  14.8 13.1 %collective-permute-start.4 = (bf16[128,1024]{1,0:T(8,128)(2,1)}, bf16[128,1024]{1,0:T(8,128)(2,1)S(1)}, u32[]{:S(2)}, u32[]{:S(2)}) collective-permute-start(bf16[128,1024]{1,0:T(8,128)(2,1)} %get-tuple-element.45), channel_id=1, source_target_pairs={{0,3},{1,0},{2,1},{3,2},{4,7},{5,4},{6,5},{7,6},{8,11},{9,8},{10,9... | collective-permute-start | bytes 786440 | tf_op jit(solution)/shard_map/ppermute | solution.py:570
  15.8 0.6 copy-start.4
  27.9 26.1 %all-to-all-start = ((bf16[8,272,128]{2,1,0:T(8,128)(2,1)}), bf16[8,272,128]{2,1,0:T(8,128)(2,1)}, u32[]{:S(2)}, u32[]{:S(2)}) async-start(bf16[8,272,128]{2,1,0:T(8,128)(2,1)} %get-tuple-element.35), calls=%async_computation | async-start | bytes 1114112 | tf_op jit(solution)/shard_map/all_to_all | solution.py:47
  35.3 25.3 %collective-permute-start.5 = (bf16[4,128,1024]{2,1,0:T(8,128)(2,1)S(1)}, bf16[4,128,1024]{2,1,0:T(8,128)(2,1)S(1)}, u32[]{:S(2)}, u32[]{:S(2)}) collective-permute-start(bf16[4,128,1024]{2,1,0:T(8,128)(2,1)S(1)} %pad_maximum_fusion.rest_0_), channel_id=1, source_target_pairs={{0,4},{1,5},{2,6},{3,7},{4,8},{5,9},{6,10},{7,11},{8,12},{9,13},{1... | collective-permute-start | bytes 3145736 | tf_op jit(solution)/shard_map/ppermute | solution.py:570
  36.6 26.2 %collective-permute-start.6 = (bf16[4,128,1024]{2,1,0:T(8,128)(2,1)S(1)}, bf16[4,128,1024]{2,1,0:T(8,128)(2,1)S(1)}, u32[]{:S(2)}, u32[]{:S(2)}) collective-permute-start(bf16[4,128,1024]{2,1,0:T(8,128)(2,1)S(1)} %pad_maximum_fusion.rest_0_), channel_id=1, source_target_pairs={{0,8},{1,9},{2,10},{3,11},{4,12},{5,13},{6,14},{7,15},{8,0},{9,1},... | collective-permute-start | bytes 3145736 | tf_op jit(solution)/shard_map/ppermute | solution.py:570
  39.1 23.7 %collective-permute-start.7 = (bf16[4,128,1024]{2,1,0:T(8,128)(2,1)S(1)}, bf16[4,128,1024]{2,1,0:T(8,128)(2,1)}, u32[]{:S(2)}, u32[]{:S(2)}) collective-permute-start(bf16[4,128,1024]{2,1,0:T(8,128)(2,1)S(1)} %pad_maximum_fusion.rest_0_), channel_id=1, source_target_pairs={{0,12},{1,13},{2,14},{3,15},{4,0},{5,1},{6,2},{7,3},{8,4},{9,5},{1... | collective-permute-start | bytes 3145736 | tf_op jit(solution)/shard_map/ppermute | solution.py:570
  56.6 15.4 %all-to-all-start.1 = ((bf16[8,128,128]{2,1,0:T(8,128)(2,1)}), bf16[8,128,128]{2,1,0:T(8,128)(2,1)S(1)}, u32[]{:S(2)}, u32[]{:S(2)}) async-start(bf16[8,128,128]{2,1,0:T(8,128)(2,1)} %enter.1), calls=%async_computation.1 | async-start | bytes 524288 | tf_op jit(solution)/shard_map/all_to_all | solution.py:47
  60.0 17.2 %collective-permute-start.9 = (bf16[4,128,1024]{2,1,0:T(8,128)(2,1)S(1)}, bf16[4,128,1024]{2,1,0:T(8,128)(2,1)}, u32[]{:S(2)}, u32[]{:S(2)}) collective-permute-start(bf16[4,128,1024]{2,1,0:T(8,128)(2,1)S(1)} %pad_maximum_fusion.rest_0_), channel_id=1, source_target_pairs={{0,16},{16,0},{32,48},{48,32},{64,80},{80,64},{96,112},{112,96},{1... | collective-permute-start | bytes 3145736 | tf_op jit(solution)/shard_map/ppermute | solution.py:42
  72.0 1.3 %copy-start.1 = (bf16[8,128,128]{2,1,0:T(8,128)(2,1)}, bf16[8,128,128]{2,1,0:T(8,128)(2,1)S(1)}, u32[]{:S(2)}) copy-start(bf16[8,128,128]{2,1,0:T(8,128)(2,1)S(1)} %all-to-all-done.1.arrived) | copy-start | bytes 786436
  72.0 6.8 %collective-permute-start.10 = (bf16[4,128,1024]{2,1,0:T(8,128)(2,1)S(1)}, bf16[4,128,1024]{2,1,0:T(8,128)(2,1)S(1)}, u32[]{:S(2)}, u32[]{:S(2)}) collective-permute-start(bf16[4,128,1024]{2,1,0:T(8,128)(2,1)S(1)} %collective-permute-done.5.rest_1_), channel_id=1, source_target_pairs={{0,16},{16,0},{32,48},{48,32},{64,80},{80,64},{96,112},{112,96},{1... | collective-permute-start | bytes 3145736 | tf_op jit(solution)/shard_map/ppermute | solution.py:42
  72.8 6.0 %collective-permute-start.11 = (bf16[4,128,1024]{2,1,0:T(8,128)(2,1)S(1)}, bf16[4,128,1024]{2,1,0:T(8,128)(2,1)S(1)}, u32[]{:S(2)}, u32[]{:S(2)}) collective-permute-start(bf16[4,128,1024]{2,1,0:T(8,128)(2,1)S(1)} %collective-permute-done.6.rest_2_), channel_id=1, source_target_pairs={{0,16},{16,0},{32,48},{48,32},{64,80},{80,64},{96,112},{112,96},{1... | collective-permute-start | bytes 3145736 | tf_op jit(solution)/shard_map/ppermute | solution.py:42
  72.8 6.0 %collective-permute-start.12 = (bf16[4,128,1024]{2,1,0:T(8,128)(2,1)}, bf16[4,128,1024]{2,1,0:T(8,128)(2,1)S(1)}, u32[]{:S(2)}, u32[]{:S(2)}) collective-permute-start(bf16[4,128,1024]{2,1,0:T(8,128)(2,1)} %collective-permute-done.7.rest_3_), channel_id=1, source_target_pairs={{0,16},{16,0},{32,48},{48,32},{64,80},{80,64},{96,112},{112,96},{1... | collective-permute-start | bytes 3145736 | tf_op jit(solution)/shard_map/ppermute | solution.py:42
  77.0 1.8 %collective-permute-start.8 = (bf16[8,128,128]{2,1,0:T(8,128)(2,1)}, bf16[8,128,128]{2,1,0:T(8,128)(2,1)S(1)}, u32[]{:S(2)}, u32[]{:S(2)}) collective-permute-start(bf16[8,128,128]{2,1,0:T(8,128)(2,1)} %get-tuple-element.53), channel_id=1, source_target_pairs={{0,16},{16,0},{32,48},{48,32},{64,80},{80,64},{96,112},{112,96},{1... | collective-permute-start | bytes 786440 | tf_op jit(solution)/shard_map/ppermute | solution.py:42
  78.8 1.0 %copy-start = (bf16[8,128,128]{2,1,0:T(8,128)(2,1)S(1)}, bf16[8,128,128]{2,1,0:T(8,128)(2,1)}, u32[]{:S(2)}) copy-start(bf16[8,128,128]{2,1,0:T(8,128)(2,1)} %get-tuple-element.52.mine) | copy-start | bytes 786436
